TPU v7x, 256 devices: a whole 4x4x8 slice. The times are simulated.
256 devices in a mesh: ka: 64 (over x, z, y_hi), ea: 4 (over y_lo, core).
Axes of the slice: x: 4, y: 4 (y_hi: 2, y_lo: 2; y = y_hi * 2 + y_lo), z: 8, core: 2. Of those that a mesh axis runs over, the one named last changes fastest.
Arguments:
- lesser: bfloat16 [64, 8, 192, 384], P('ka', 'ea'), may hold values from -6 to 6
- greater: bfloat16 [64, 8, 192, 384], P('ka', 'ea'), may hold values from -6 to 6
- coupling: bfloat16 [192, 384], replicated, may hold values from -0.3125 to 0.3125
- cotangent: bfloat16 [9, 4, 192, 384], replicated, may hold values from -0.0546875 to 0.0546875
- offsets: int32 [9], replicated, may hold values from 0 to 8, each once
- mode_shift: int32 [4], replicated, may hold values from 1 to 2, as said below
Outputs:
- grad_lesser: bfloat16 [64, 8, 192, 384], P('ka', 'ea')
- grad_greater: bfloat16 [64, 8, 192, 384], P('ka', 'ea')
Inputs may be any that keep to these rules, and one draw needn't show every extreme that they name: `offsets`: each value 0 to 8 stands once. `mode_shift`: at least one mode has the shift 2.
All inputs are finite; a program needn't handle non-finite values.
Results may differ from a plain program's by a relative error of at most 0.0058.
Values may be sent and summed in bfloat16 or wider, within the bound.
No kernel may reach another device: no remote copies, remote signals or barrier semaphores. Data moves between devices by JAX's collectives and lax.ppermute only.
A program may use at most 128 MiB of HBM per device.

v0:
```python
import jax
import jax.numpy as jnp
from jax import lax
from jax.sharding import PartitionSpec as P

QS = 4
SMAX = 2


def shifted(block, axis, distance):
    devices = range(lax.axis_size(axis))
    route = [(i - distance, i) for i in devices if i - distance in devices]
    return lax.ppermute(block, axis, route)


def shifted_2(block, axis, distance):
    devices = range(lax.axis_size(axis))
    route = [((i - distance) % len(devices), i) for i in devices]
    return lax.ppermute(block, axis, route)


def bigform(block):
    width = block.shape[-1] // 2
    real_part = block[..., :width]
    imag_part = block[..., width:]
    upper_half = jnp.concatenate([real_part, imag_part], -1)
    lower_half = jnp.concatenate([-imag_part, real_part], -1)
    return jnp.concatenate([upper_half, lower_half], -2)


def conjugate(block):
    width = block.shape[-1] // 2
    real_part = jnp.swapaxes(block[..., :width], -1, -2)
    imag_part = jnp.swapaxes(block[..., width:], -1, -2)
    return jnp.concatenate([real_part, -imag_part], -1)


def product(left, right_big):
    block_shape = left.shape
    flattened = left.reshape(-1, block_shape[-1])
    result = jnp.dot(flattened, right_big, preferred_element_type=jnp.float32)
    return result.reshape(block_shape[:-1] + (right_big.shape[-1],))


def sandwich(blocks, big_c, big_ch):
    half_block = product(blocks, big_c).astype(jnp.bfloat16)
    return product(conjugate(half_block), big_ch).astype(jnp.bfloat16)


def per_device(lesser, greater, coupling, cotangent, offsets, mode_shift):
    orbitals = coupling.shape[0]
    energy_count = lesser.shape[1]
    phonons = cotangent.shape[1]
    cycle_size = lax.axis_size("ka")
    big_c = bigform(coupling)
    big_ch = bigform(conjugate(coupling))
    flipped = sandwich(lesser, big_c, big_ch)
    big_p = bigform(cotangent)
    big_ph = jnp.swapaxes(big_p, -1, -2)
    slot_of = jnp.argsort(offsets)
    lower_starts = [SMAX - mode_shift[phonon] for phonon in range(phonons)]
    upper_starts = [mode_shift[phonon] for phonon in range(phonons)]

    def gather_modes(blocks, start_list):
        return jnp.concatenate(
            [
                lax.dynamic_slice_in_dim(blocks, start_list[phonon], energy_count, 1)
                for phonon in range(phonons)
            ],
            -1,
        )

    def contribute(totals, pieces, distance):
        lesser_total, greater_total = totals
        lower_cat = gather_modes(pieces[0], lower_starts)
        upper_cat = gather_modes(pieces[1], upper_starts)
        for offset in range(-QS, QS + 1):
            slot_index = slot_of[offset + QS]
            if offset % cycle_size == distance:
                stacked = big_ph[slot_index].reshape(-1, 2 * orbitals)
                lesser_total = lesser_total + product(lower_cat, stacked)
            if -offset % cycle_size == distance:
                stacked = big_p[slot_index].reshape(-1, 2 * orbitals)
                greater_total = greater_total + product(upper_cat, stacked)
        return (lesser_total, greater_total)

    below_rim = shifted(greater, "ea", 1)
    above_rim = shifted(flipped, "ea", -1)
    own_blocks = (
        jnp.concatenate([below_rim, greater], 1),
        jnp.concatenate([flipped, above_rim], 1),
    )
    empty = jnp.zeros(lesser.shape, jnp.float32)
    totals = contribute((empty, empty), own_blocks, 0)
    ahead = QS
    behind = min(QS, cycle_size - 1 - QS)
    forward = own_blocks
    for travel in range(1, ahead + 1):
        forward = shifted_2((forward[0], forward[1]), "ka", 1)
        totals = contribute(totals, forward, travel % cycle_size)
    backward = own_blocks
    for travel in range(1, behind + 1):
        backward = shifted_2((backward[0], backward[1]), "ka", -1)
        totals = contribute(totals, backward, -travel % cycle_size)
    grad_lesser = sandwich(totals[0].astype(jnp.bfloat16), big_c, big_ch)
    grad_greater = totals[1].astype(jnp.bfloat16)
    return (grad_lesser, grad_greater)


def solution(mesh):
    in_specs = (P("ka", "ea", None, None), P("ka", "ea", None, None), P(), P(), P(), P())
    out_specs = (P("ka", "ea", None, None), P("ka", "ea", None, None))
    return jax.shard_map(
        per_device, mesh=mesh, in_specs=in_specs, out_specs=out_specs, check_vma=False
    )
```

profile of v0, /device:TPU:1, one launch (start us, length us, event | category | flops | bytes accessed | tf_op | source)
XLA Modules:
  0.0 310.7 jit_solution(15406420325899292214)
XLA Ops:
  0.6 4.7 %collective-permute-start = (bf16[1,2,192,384]{3,2,1,0:T(8,128)(2,1)}, bf16[1,2,192,384]{3,2,1,0:T(8,128)(2,1)S(1)}, u32[]{:S(2)}, u32[]{:S(2)}) collective-permute-start(bf16[1,2,192,384]{3,2,1,0:T(8,128)(2,1)} %param.7), channel_id=1, source_target_pairs={{0,1},{1,2},{2,3},{4,5},{5,6},{6,7},{8,9},{9,10},{10,11},{12,13},{... | collective-permute-start | bytes 884744 | tf_op jit(solution)/shard_map/ppermute | solution.py:13
  25.0 9.0 %copy.15 = bf16[9,4,192,384]{2,3,1,0:T(8,128)(2,1)} copy(bf16[9,4,192,384]{3,2,1,0:T(8,128)(2,1)} %param.9) | data formatting | bytes 10616832 | tf_op args[3]
  33.9 3.7 %slice_negate_fusion = (bf16[9,4,192,192]{2,3,1,0:T(8,128)(2,1)S(1)}, bf16[9,4,192,192]{2,3,1,0:T(8,128)(2,1)S(1)}) fusion(bf16[9,4,192,384]{2,3,1,0:T(8,128)(2,1)} %copy.15), kind=kLoop, calls=%fused_computation.1 | loop fusion | flops 1327104 | bytes 10616832 | tf_op jit(solution)/shard_map/neg | solution.py:27
  39.0 8.0 %maximum_maximum_fusion = bf16[9,4,384,384]{2,3,1,0:T(8,128)(2,1)} fusion(bf16[9,4,192,192]{2,3,1,0:T(8,128)(2,1)S(1)} %get-tuple-element.14, bf16[9,4,192,192]{2,3,1,0:T(8,128)(2,1)S(1)} %get-tuple-element.13, bf16[9,4,192,384]{2,3,1,0:T(8,128)(2,1)S(1)} %copy-done.2), kind=kLoop, calls=%fused_computation | loop fusion | flops 31850496 | bytes 21233664 | tf_op jit(solution)/shard_map/concatenate | solution.py:28
  52.6 7.6 %constant_dynamic-slice_fusion.32 = (bf16[1,4,384,384]{2,3,1,0:T(8,128)(2,1)S(1)}, bf16[1,4,384,384]{2,3,1,0:T(8,128)(2,1)S(1)}, bf16[1,4,384,384]{2,3,1,0:T(8,1...) fusion(bf16[9,4,384,384]{2,3,1,0:T(8,128)(2,1)} %maximum_maximu, ...), kind=kLoop, calls=%fused_computation.216 | loop fusion | bytes 21233700 | tf_op jit(solution)/shard_map/dynamic-slice.8
  73.2 2.4 copy.22
  75.6 2.4 copy.23
  80.9 2.4 copy.26
  83.3 2.4 copy.27
  88.0 2.4 copy.29
  93.1 2.7 collective-permute-start.1
  95.8 7.6 %collective-permute-start.5 = (bf16[1,4,192,384]{3,2,1,0:T(8,128)(2,1)S(1)}, bf16[1,4,192,384]{3,2,1,0:T(8,128)(2,1)S(1)}, u32[]{:S(2)}, u32[]{:S(2)}) collective-permute-start(bf16[1,4,192,384]{3,2,1,0:T(8,128)(2,1)S(1)} %constant_dynamic-update-slice_fusion), channel_id=1, source_target_pairs={{4,0},{8,4},{12,8},{16,12},{20,16},{24,20},{28,24},{32,28},{36,32}... | collective-permute-start | bytes 1769480 | tf_op jit(solution)/shard_map/ppermute | solution.py:19
  103.5 7.2 %collective-permute-start.14 = (bf16[1,4,192,384]{3,2,1,0:T(8,128)(2,1)S(1)}, bf16[1,4,192,384]{3,2,1,0:T(8,128)(2,1)S(1)}, u32[]{:S(2)}, u32[]{:S(2)}) collective-permute-start(bf16[1,4,192,384]{3,2,1,0:T(8,128)(2,1)S(1)} %pad_maximum_fusion), channel_id=1, source_target_pairs={{4,0},{8,4},{12,8},{16,12},{20,16},{24,20},{28,24},{32,28},{36,32}... | collective-permute-start | bytes 1769480 | tf_op jit(solution)/shard_map/ppermute | solution.py:19
  114.2 20.1 %collective-permute-done.1 = bf16[1,4,192,384]{3,2,1,0:T(8,128)(2,1)S(1)} collective-permute-done((bf16[1,4,192,384]{3,2,1,0:T(8,128)(2,1)S(1)}, bf16[1,4,192,384]{3,2,1,0:T(8,128)(2,1)S(1)}, u32[]{:S(2)}, u32[]{:S(2)}) %collective-permute-start.1) | collective-permute-done | bytes 589856 | tf_op jit(solution)/shard_map/ppermute | solution.py:19
  134.2 3.7 %collective-permute-start.2 = (bf16[1,4,192,384]{3,2,1,0:T(8,128)(2,1)S(1)}, bf16[1,4,192,384]{3,2,1,0:T(8,128)(2,1)S(1)}, u32[]{:S(2)}, u32[]{:S(2)}) collective-permute-start(bf16[1,4,192,384]{3,2,1,0:T(8,128)(2,1)S(1)} %collective-permute-done.1), channel_id=1, source_target_pairs={{252,0},{0,4},{4,8},{8,12},{12,16},{16,20},{20,24},{24,28},{28,32}... | collective-permute-start | bytes 1769480 | tf_op jit(solution)/shard_map/ppermute | solution.py:19
  137.9 7.5 %collective-permute-start.6 = (bf16[1,4,192,384]{3,2,1,0:T(8,128)(2,1)S(1)}, bf16[1,4,192,384]{3,2,1,0:T(8,128)(2,1)S(1)}, u32[]{:S(2)}, u32[]{:S(2)}) collective-permute-start(bf16[1,4,192,384]{3,2,1,0:T(8,128)(2,1)S(1)} %collective-permute-done.5), channel_id=1, source_target_pairs={{4,0},{8,4},{12,8},{16,12},{20,16},{24,20},{28,24},{32,28},{36,32}... | collective-permute-start | bytes 1769480 | tf_op jit(solution)/shard_map/ppermute | solution.py:19
  145.4 14.1 %collective-permute-done.10 = bf16[1,4,192,384]{3,2,1,0:T(8,128)(2,1)S(1)} collective-permute-done((bf16[1,4,192,384]{3,2,1,0:T(8,128)(2,1)S(1)}, bf16[1,4,192,384]{3,2,1,0:T(8,128)(2,1)S(1)}, u32[]{:S(2)}, u32[]{:S(2)}) %collective-permute-start.10) | collective-permute-done | bytes 589856 | tf_op jit(solution)/shard_map/ppermute | solution.py:19
  159.5 3.7 %collective-permute-start.11 = (bf16[1,4,192,384]{3,2,1,0:T(8,128)(2,1)S(1)}, bf16[1,4,192,384]{3,2,1,0:T(8,128)(2,1)S(1)}, u32[]{:S(2)}, u32[]{:S(2)}) collective-permute-start(bf16[1,4,192,384]{3,2,1,0:T(8,128)(2,1)S(1)} %collective-permute-done.10), channel_id=1, source_target_pairs={{252,0},{0,4},{4,8},{8,12},{12,16},{16,20},{20,24},{24,28},{28,32}... | collective-permute-start | bytes 1769480 | tf_op jit(solution)/shard_map/ppermute | solution.py:19
  163.6 7.6 %collective-permute-start.15 = (bf16[1,4,192,384]{3,2,1,0:T(8,128)(2,1)S(1)}, bf16[1,4,192,384]{3,2,1,0:T(8,128)(2,1)S(1)}, u32[]{:S(2)}, u32[]{:S(2)}) collective-permute-start(bf16[1,4,192,384]{3,2,1,0:T(8,128)(2,1)S(1)} %collective-permute-done.14), channel_id=1, source_target_pairs={{4,0},{8,4},{12,8},{16,12},{20,16},{24,20},{28,24},{32,28},{36,32}... | collective-permute-start | bytes 1769480 | tf_op jit(solution)/shard_map/ppermute | solution.py:19
  174.3 10.5 %collective-permute-done.2 = bf16[1,4,192,384]{3,2,1,0:T(8,128)(2,1)S(1)} collective-permute-done((bf16[1,4,192,384]{3,2,1,0:T(8,128)(2,1)S(1)}, bf16[1,4,192,384]{3,2,1,0:T(8,128)(2,1)S(1)}, u32[]{:S(2)}, u32[]{:S(2)}) %collective-permute-start.2) | collective-permute-done | bytes 589856 | tf_op jit(solution)/shard_map/ppermute | solution.py:19
  184.8 3.7 %collective-permute-start.3 = (bf16[1,4,192,384]{3,2,1,0:T(8,128)(2,1)S(1)}, bf16[1,4,192,384]{3,2,1,0:T(8,128)(2,1)S(1)}, u32[]{:S(2)}, u32[]{:S(2)}) collective-permute-start(bf16[1,4,192,384]{3,2,1,0:T(8,128)(2,1)S(1)} %collective-permute-done.2), channel_id=1, source_target_pairs={{252,0},{0,4},{4,8},{8,12},{12,16},{16,20},{20,24},{24,28},{28,32}... | collective-permute-start | bytes 1769480 | tf_op jit(solution)/shard_map/ppermute | solution.py:19
  188.5 7.5 %collective-permute-start.7 = (bf16[1,4,192,384]{3,2,1,0:T(8,128)(2,1)S(1)}, bf16[1,4,192,384]{3,2,1,0:T(8,128)(2,1)S(1)}, u32[]{:S(2)}, u32[]{:S(2)}) collective-permute-start(bf16[1,4,192,384]{3,2,1,0:T(8,128)(2,1)S(1)} %collective-permute-done.6), channel_id=1, source_target_pairs={{4,0},{8,4},{12,8},{16,12},{20,16},{24,20},{28,24},{32,28},{36,32}... | collective-permute-start | bytes 1769480 | tf_op jit(solution)/shard_map/ppermute | solution.py:19
  196.0 14.1 %collective-permute-done.11 = bf16[1,4,192,384]{3,2,1,0:T(8,128)(2,1)S(1)} collective-permute-done((bf16[1,4,192,384]{3,2,1,0:T(8,128)(2,1)S(1)}, bf16[1,4,192,384]{3,2,1,0:T(8,128)(2,1)S(1)}, u32[]{:S(2)}, u32[]{:S(2)}) %collective-permute-start.11) | collective-permute-done | bytes 589856 | tf_op jit(solution)/shard_map/ppermute | solution.py:19
  210.1 3.7 %collective-permute-start.12 = (bf16[1,4,192,384]{3,2,1,0:T(8,128)(2,1)S(1)}, bf16[1,4,192,384]{3,2,1,0:T(8,128)(2,1)S(1)}, u32[]{:S(2)}, u32[]{:S(2)}) collective-permute-start(bf16[1,4,192,384]{3,2,1,0:T(8,128)(2,1)S(1)} %collective-permute-done.11), channel_id=1, source_target_pairs={{252,0},{0,4},{4,8},{8,12},{12,16},{16,20},{20,24},{24,28},{28,32}... | collective-permute-start | bytes 1769480 | tf_op jit(solution)/shard_map/ppermute | solution.py:19
  216.0 7.6 %collective-permute-start.16 = (bf16[1,4,192,384]{3,2,1,0:T(8,128)(2,1)S(1)}, bf16[1,4,192,384]{3,2,1,0:T(8,128)(2,1)}, u32[]{:S(2)}, u32[]{:S(2)}) collective-permute-start(bf16[1,4,192,384]{3,2,1,0:T(8,128)(2,1)S(1)} %collective-permute-done.15), channel_id=1, source_target_pairs={{4,0},{8,4},{12,8},{16,12},{20,16},{24,20},{28,24},{32,28},{36,32}... | collective-permute-start | bytes 1769480 | tf_op jit(solution)/shard_map/ppermute | solution.py:19
  225.5 13.6 %collective-permute-done.7 = bf16[1,4,192,384]{3,2,1,0:T(8,128)(2,1)S(1)} collective-permute-done((bf16[1,4,192,384]{3,2,1,0:T(8,128)(2,1)S(1)}, bf16[1,4,192,384]{3,2,1,0:T(8,128)(2,1)S(1)}, u32[]{:S(2)}, u32[]{:S(2)}) %collective-permute-start.7) | collective-permute-done | bytes 589856 | tf_op jit(solution)/shard_map/ppermute | solution.py:19
  239.1 3.5 %collective-permute-start.8 = (bf16[1,4,192,384]{3,2,1,0:T(8,128)(2,1)S(1)}, bf16[1,4,192,384]{3,2,1,0:T(8,128)(2,1)S(1)}, u32[]{:S(2)}, u32[]{:S(2)}) collective-permute-start(bf16[1,4,192,384]{3,2,1,0:T(8,128)(2,1)S(1)} %collective-permute-done.7), channel_id=1, source_target_pairs={{4,0},{8,4},{12,8},{16,12},{20,16},{24,20},{28,24},{32,28},{36,32}... | collective-permute-start | bytes 1769480 | tf_op jit(solution)/shard_map/ppermute | solution.py:19
  242.7 18.0 %collective-permute-done.12 = bf16[1,4,192,384]{3,2,1,0:T(8,128)(2,1)S(1)} collective-permute-done((bf16[1,4,192,384]{3,2,1,0:T(8,128)(2,1)S(1)}, bf16[1,4,192,384]{3,2,1,0:T(8,128)(2,1)S(1)}, u32[]{:S(2)}, u32[]{:S(2)}) %collective-permute-start.12) | collective-permute-done | bytes 589856 | tf_op jit(solution)/shard_map/ppermute | solution.py:19
  260.6 3.7 %collective-permute-start.13 = (bf16[1,4,192,384]{3,2,1,0:T(8,128)(2,1)S(1)}, bf16[1,4,192,384]{3,2,1,0:T(8,128)(2,1)}, u32[]{:S(2)}, u32[]{:S(2)}) collective-permute-start(bf16[1,4,192,384]{3,2,1,0:T(8,128)(2,1)S(1)} %collective-permute-done.12), channel_id=1, source_target_pairs={{252,0},{0,4},{4,8},{8,12},{12,16},{16,20},{20,24},{24,28},{28,32}... | collective-permute-start | bytes 1769480 | tf_op jit(solution)/shard_map/ppermute | solution.py:19
  264.8 7.8 %collective-permute-start.17 = (bf16[1,4,192,384]{3,2,1,0:T(8,128)(2,1)}, bf16[1,4,192,384]{3,2,1,0:T(8,128)(2,1)}, u32[]{:S(2)}, u32[]{:S(2)}) collective-permute-start(bf16[1,4,192,384]{3,2,1,0:T(8,128)(2,1)} %collective-permute-done.16), channel_id=1, source_target_pairs={{4,0},{8,4},{12,8},{16,12},{20,16},{24,20},{28,24},{32,28},{36,32}... | collective-permute-start | bytes 1769480 | tf_op jit(solution)/shard_map/ppermute | solution.py:19
  277.8 11.9 %collective-permute-done.8 = bf16[1,4,192,384]{3,2,1,0:T(8,128)(2,1)S(1)} collective-permute-done((bf16[1,4,192,384]{3,2,1,0:T(8,128)(2,1)S(1)}, bf16[1,4,192,384]{3,2,1,0:T(8,128)(2,1)S(1)}, u32[]{:S(2)}, u32[]{:S(2)}) %collective-permute-start.8) | collective-permute-done | bytes 589856 | tf_op jit(solution)/shard_map/ppermute | solution.py:19
  295.7 2.4 fusion.112
  (156 shorter events, 53.1 us)
Async XLA Ops:
  0.6 7.0 %copy-start = (bf16[1,2,192,384]{3,2,1,0:T(8,128)(2,1)S(1)}, bf16[1,2,192,384]{3,2,1,0:T(8,128)(2,1)}, u32[]{:S(2)}) copy-start(bf16[1,2,192,384]{3,2,1,0:T(8,128)(2,1)} %param.6) | copy-start | bytes 884740
  0.6 92.3 %collective-permute-start = (bf16[1,2,192,384]{3,2,1,0:T(8,128)(2,1)}, bf16[1,2,192,384]{3,2,1,0:T(8,128)(2,1)S(1)}, u32[]{:S(2)}, u32[]{:S(2)}) collective-permute-start(bf16[1,2,192,384]{3,2,1,0:T(8,128)(2,1)} %param.7), channel_id=1, source_target_pairs={{0,1},{1,2},{2,3},{4,5},{5,6},{6,7},{8,9},{9,10},{10,11},{12,13},{... | collective-permute-start | bytes 884744 | tf_op jit(solution)/shard_map/ppermute | solution.py:13
  6.5 2.8 copy-start.37
  6.5 2.8 copy-start.38
  6.5 3.0 copy-start.33
  6.5 3.0 copy-start.35
  9.9 93.5 %collective-permute-start.9 = (bf16[1,2,192,384]{3,2,1,0:T(8,128)(2,1)S(1)}, bf16[1,2,192,384]{3,2,1,0:T(8,128)(2,1)S(1)}, u32[]{:S(2)}, u32[]{:S(2)}) collective-permute-start(bf16[1,2,192,384]{3,2,1,0:T(8,128)(2,1)S(1)} %fusion.114), channel_id=1, source_target_pairs={{1,0},{2,1},{3,2},{5,4},{6,5},{7,6},{9,8},{10,9},{11,10},{13,12},{... | collective-permute-start | bytes 884744 | tf_op jit(solution)/shard_map/ppermute | solution.py:13
  33.9 5.1 %copy-start.2 = (bf16[9,4,192,384]{2,3,1,0:T(8,128)(2,1)S(1)}, bf16[9,4,192,384]{2,3,1,0:T(8,128)(2,1)}, u32[]{:S(2)}) copy-start(bf16[9,4,192,384]{2,3,1,0:T(8,128)(2,1)} %copy.15) | copy-start | bytes 15925252
  52.6 7.6 %copy-start.41 = (s32[4]{0:T(128)S(1)}, s32[4]{0:T(128)}, u32[]{:S(2)}) copy-start(s32[4]{0:T(128)} %param.11) | copy-start | bytes 52
  88.0 5.0 %copy-start.20 = (bf16[1,2,192,384]{3,2,1,0:T(8,128)(2,1)S(1)}, bf16[1,2,192,384]{3,2,1,0:T(8,128)(2,1)}, u32[]{:S(2)}) copy-start(bf16[1,2,192,384]{3,2,1,0:T(8,128)(2,1)} %param.7) | copy-start | bytes 884740
  93.1 41.1 %collective-permute-start.1 = (bf16[1,4,192,384]{3,2,1,0:T(8,128)(2,1)S(1)}, bf16[1,4,192,384]{3,2,1,0:T(8,128)(2,1)S(1)}, u32[]{:S(2)}, u32[]{:S(2)}) collective-permute-start(bf16[1,4,192,384]{3,2,1,0:T(8,128)(2,1)S(1)} %constant_dynamic-update-slice_fusion), channel_id=1, source_target_pairs={{252,0},{0,4},{4,8},{8,12},{12,16},{16,20},{20,24},{24,28},{28,32}... | collective-permute-start | bytes 1769480 | tf_op jit(solution)/shard_map/ppermute | solution.py:19
  95.8 42.2 %collective-permute-start.5 = (bf16[1,4,192,384]{3,2,1,0:T(8,128)(2,1)S(1)}, bf16[1,4,192,384]{3,2,1,0:T(8,128)(2,1)S(1)}, u32[]{:S(2)}, u32[]{:S(2)}) collective-permute-start(bf16[1,4,192,384]{3,2,1,0:T(8,128)(2,1)S(1)} %constant_dynamic-update-slice_fusion), channel_id=1, source_target_pairs={{4,0},{8,4},{12,8},{16,12},{20,16},{24,20},{28,24},{32,28},{36,32}... | collective-permute-start | bytes 1769480 | tf_op jit(solution)/shard_map/ppermute | solution.py:19
  103.4 56.1 %collective-permute-start.10 = (bf16[1,4,192,384]{3,2,1,0:T(8,128)(2,1)S(1)}, bf16[1,4,192,384]{3,2,1,0:T(8,128)(2,1)S(1)}, u32[]{:S(2)}, u32[]{:S(2)}) collective-permute-start(bf16[1,4,192,384]{3,2,1,0:T(8,128)(2,1)S(1)} %pad_maximum_fusion), channel_id=1, source_target_pairs={{252,0},{0,4},{4,8},{8,12},{12,16},{16,20},{20,24},{24,28},{28,32}... | collective-permute-start | bytes 1769480 | tf_op jit(solution)/shard_map/ppermute | solution.py:19
  103.5 60.1 %collective-permute-start.14 = (bf16[1,4,192,384]{3,2,1,0:T(8,128)(2,1)S(1)}, bf16[1,4,192,384]{3,2,1,0:T(8,128)(2,1)S(1)}, u32[]{:S(2)}, u32[]{:S(2)}) collective-permute-start(bf16[1,4,192,384]{3,2,1,0:T(8,128)(2,1)S(1)} %pad_maximum_fusion), channel_id=1, source_target_pairs={{4,0},{8,4},{12,8},{16,12},{20,16},{24,20},{28,24},{32,28},{36,32}... | collective-permute-start | bytes 1769480 | tf_op jit(solution)/shard_map/ppermute | solution.py:19
  134.2 50.6 %collective-permute-start.2 = (bf16[1,4,192,384]{3,2,1,0:T(8,128)(2,1)S(1)}, bf16[1,4,192,384]{3,2,1,0:T(8,128)(2,1)S(1)}, u32[]{:S(2)}, u32[]{:S(2)}) collective-permute-start(bf16[1,4,192,384]{3,2,1,0:T(8,128)(2,1)S(1)} %collective-permute-done.1), channel_id=1, source_target_pairs={{252,0},{0,4},{4,8},{8,12},{12,16},{16,20},{20,24},{24,28},{28,32}... | collective-permute-start | bytes 1769480 | tf_op jit(solution)/shard_map/ppermute | solution.py:19
  137.9 50.6 %collective-permute-start.6 = (bf16[1,4,192,384]{3,2,1,0:T(8,128)(2,1)S(1)}, bf16[1,4,192,384]{3,2,1,0:T(8,128)(2,1)S(1)}, u32[]{:S(2)}, u32[]{:S(2)}) collective-permute-start(bf16[1,4,192,384]{3,2,1,0:T(8,128)(2,1)S(1)} %collective-permute-done.5), channel_id=1, source_target_pairs={{4,0},{8,4},{12,8},{16,12},{20,16},{24,20},{28,24},{32,28},{36,32}... | collective-permute-start | bytes 1769480 | tf_op jit(solution)/shard_map/ppermute | solution.py:19
  159.5 50.6 %collective-permute-start.11 = (bf16[1,4,192,384]{3,2,1,0:T(8,128)(2,1)S(1)}, bf16[1,4,192,384]{3,2,1,0:T(8,128)(2,1)S(1)}, u32[]{:S(2)}, u32[]{:S(2)}) collective-permute-start(bf16[1,4,192,384]{3,2,1,0:T(8,128)(2,1)S(1)} %collective-permute-done.10), channel_id=1, source_target_pairs={{252,0},{0,4},{4,8},{8,12},{12,16},{16,20},{20,24},{24,28},{28,32}... | collective-permute-start | bytes 1769480 | tf_op jit(solution)/shard_map/ppermute | solution.py:19
  163.6 8.7 %copy-start.8 = (bf16[1,4,384,384]{2,3,1,0:T(8,128)(2,1)S(1)}, bf16[1,4,384,384]{2,3,1,0:T(8,128)(2,1)}, u32[]{:S(2)}) copy-start(bf16[1,4,384,384]{2,3,1,0:T(8,128)(2,1)} %get-tuple-element.11) | copy-start | bytes 3538948
  163.6 52.3 %collective-permute-start.15 = (bf16[1,4,192,384]{3,2,1,0:T(8,128)(2,1)S(1)}, bf16[1,4,192,384]{3,2,1,0:T(8,128)(2,1)S(1)}, u32[]{:S(2)}, u32[]{:S(2)}) collective-permute-start(bf16[1,4,192,384]{3,2,1,0:T(8,128)(2,1)S(1)} %collective-permute-done.14), channel_id=1, source_target_pairs={{4,0},{8,4},{12,8},{16,12},{20,16},{24,20},{28,24},{32,28},{36,32}... | collective-permute-start | bytes 1769480 | tf_op jit(solution)/shard_map/ppermute | solution.py:19
  184.8 57.9 %collective-permute-start.3 = (bf16[1,4,192,384]{3,2,1,0:T(8,128)(2,1)S(1)}, bf16[1,4,192,384]{3,2,1,0:T(8,128)(2,1)S(1)}, u32[]{:S(2)}, u32[]{:S(2)}) collective-permute-start(bf16[1,4,192,384]{3,2,1,0:T(8,128)(2,1)S(1)} %collective-permute-done.2), channel_id=1, source_target_pairs={{252,0},{0,4},{4,8},{8,12},{12,16},{16,20},{20,24},{24,28},{28,32}... | collective-permute-start | bytes 1769480 | tf_op jit(solution)/shard_map/ppermute | solution.py:19
  188.5 50.6 %collective-permute-start.7 = (bf16[1,4,192,384]{3,2,1,0:T(8,128)(2,1)S(1)}, bf16[1,4,192,384]{3,2,1,0:T(8,128)(2,1)S(1)}, u32[]{:S(2)}, u32[]{:S(2)}) collective-permute-start(bf16[1,4,192,384]{3,2,1,0:T(8,128)(2,1)S(1)} %collective-permute-done.6), channel_id=1, source_target_pairs={{4,0},{8,4},{12,8},{16,12},{20,16},{24,20},{28,24},{32,28},{36,32}... | collective-permute-start | bytes 1769480 | tf_op jit(solution)/shard_map/ppermute | solution.py:19
  210.1 50.6 %collective-permute-start.12 = (bf16[1,4,192,384]{3,2,1,0:T(8,128)(2,1)S(1)}, bf16[1,4,192,384]{3,2,1,0:T(8,128)(2,1)S(1)}, u32[]{:S(2)}, u32[]{:S(2)}) collective-permute-start(bf16[1,4,192,384]{3,2,1,0:T(8,128)(2,1)S(1)} %collective-permute-done.11), channel_id=1, source_target_pairs={{252,0},{0,4},{4,8},{8,12},{12,16},{16,20},{20,24},{24,28},{28,32}... | collective-permute-start | bytes 1769480 | tf_op jit(solution)/shard_map/ppermute | solution.py:19
  215.2 8.4 %copy-start.16 = (bf16[1,4,384,384]{3,2,1,0:T(8,128)(2,1)S(1)}, bf16[1,4,384,384]{3,2,1,0:T(8,128)(2,1)}, u32[]{:S(2)}) copy-start(bf16[1,4,384,384]{3,2,1,0:T(8,128)(2,1)} %copy.23) | copy-start | bytes 3538948
  216.0 48.8 %collective-permute-start.16 = (bf16[1,4,192,384]{3,2,1,0:T(8,128)(2,1)S(1)}, bf16[1,4,192,384]{3,2,1,0:T(8,128)(2,1)}, u32[]{:S(2)}, u32[]{:S(2)}) collective-permute-start(bf16[1,4,192,384]{3,2,1,0:T(8,128)(2,1)S(1)} %collective-permute-done.15), channel_id=1, source_target_pairs={{4,0},{8,4},{12,8},{16,12},{20,16},{24,20},{28,24},{32,28},{36,32}... | collective-permute-start | bytes 1769480 | tf_op jit(solution)/shard_map/ppermute | solution.py:19
  239.1 50.6 %collective-permute-start.8 = (bf16[1,4,192,384]{3,2,1,0:T(8,128)(2,1)S(1)}, bf16[1,4,192,384]{3,2,1,0:T(8,128)(2,1)S(1)}, u32[]{:S(2)}, u32[]{:S(2)}) collective-permute-start(bf16[1,4,192,384]{3,2,1,0:T(8,128)(2,1)S(1)} %collective-permute-done.7), channel_id=1, source_target_pairs={{4,0},{8,4},{12,8},{16,12},{20,16},{24,20},{28,24},{32,28},{36,32}... | collective-permute-start | bytes 1769480 | tf_op jit(solution)/shard_map/ppermute | solution.py:19
  242.6 47.0 %collective-permute-start.4 = (bf16[1,4,192,384]{3,2,1,0:T(8,128)(2,1)S(1)}, bf16[1,4,192,384]{3,2,1,0:T(8,128)(2,1)S(1)}, u32[]{:S(2)}, u32[]{:S(2)}) collective-permute-start(bf16[1,4,192,384]{3,2,1,0:T(8,128)(2,1)S(1)} %collective-permute-done.3), channel_id=1, source_target_pairs={{252,0},{0,4},{4,8},{8,12},{12,16},{16,20},{20,24},{24,28},{28,32}... | collective-permute-start | bytes 1769480 | tf_op jit(solution)/shard_map/ppermute | solution.py:19
  260.6 40.5 %collective-permute-start.13 = (bf16[1,4,192,384]{3,2,1,0:T(8,128)(2,1)S(1)}, bf16[1,4,192,384]{3,2,1,0:T(8,128)(2,1)}, u32[]{:S(2)}, u32[]{:S(2)}) collective-permute-start(bf16[1,4,192,384]{3,2,1,0:T(8,128)(2,1)S(1)} %collective-permute-done.12), channel_id=1, source_target_pairs={{252,0},{0,4},{4,8},{8,12},{12,16},{16,20},{20,24},{24,28},{28,32}... | collective-permute-start | bytes 1769480 | tf_op jit(solution)/shard_map/ppermute | solution.py:19
  264.7 10.2 %copy-start.6 = (bf16[1,4,384,384]{2,3,1,0:T(8,128)(2,1)S(1)}, bf16[1,4,384,384]{2,3,1,0:T(8,128)(2,1)}, u32[]{:S(2)}) copy-start(bf16[1,4,384,384]{2,3,1,0:T(8,128)(2,1)} %get-tuple-element.9) | copy-start | bytes 3538948
  264.8 36.4 %collective-permute-start.17 = (bf16[1,4,192,384]{3,2,1,0:T(8,128)(2,1)}, bf16[1,4,192,384]{3,2,1,0:T(8,128)(2,1)}, u32[]{:S(2)}, u32[]{:S(2)}) collective-permute-start(bf16[1,4,192,384]{3,2,1,0:T(8,128)(2,1)} %collective-permute-done.16), channel_id=1, source_target_pairs={{4,0},{8,4},{12,8},{16,12},{20,16},{24,20},{28,24},{32,28},{36,32}... | collective-permute-start | bytes 1769480 | tf_op jit(solution)/shard_map/ppermute | solution.py:19
  277.8 13.0 %copy-start.5 = (bf16[1,4,384,384]{2,3,1,0:T(8,128)(2,1)S(1)}, bf16[1,4,384,384]{2,3,1,0:T(8,128)(2,1)}, u32[]{:S(2)}) copy-start(bf16[1,4,384,384]{2,3,1,0:T(8,128)(2,1)} %get-tuple-element.8) | copy-start | bytes 3538948
  299.6 3.5 %copy-start.14 = (bf16[1,4,384,384]{3,2,1,0:T(8,128)(2,1)S(1)}, bf16[1,4,384,384]{3,2,1,0:T(8,128)(2,1)}, u32[]{:S(2)}) copy-start(bf16[1,4,384,384]{3,2,1,0:T(8,128)(2,1)} %copy.25) | copy-start | bytes 3538948
  299.6 3.6 %copy-start.43 = (f32[2,192,384]{2,1,0:T(8,128)S(1)}, f32[2,192,384]{2,1,0:T(8,128)}, u32[]{:S(2)}) copy-start(f32[2,192,384]{2,1,0:T(8,128)} %convolution_add_fusion.5) | copy-start | bytes 1769476
  (30 other events, 46.6 us)
where the time goes:
time: 312 us; the launch traced here: 311 us
  waiting for transfers between devices  104 us (33%)
  starting transfers between devices  84.1 us (27%)
  local copies, waits for them, and re-layouts  55.3 us (18%)
  between operations  30.5 us (10%)
  matrix products  21.1 us (7%)
  other arithmetic  15.8 us (5%)
    ppermute x16, waiting for transfers between devices, shifted_2(): return lax.ppermute(block, axis, route)  104 us
    ppermute x16, starting transfers between devices, shifted_2(): return lax.ppermute(block, axis, route)  77.5 us
    another operation x10, local copies, waits for them, and re-layouts  27.3 us
    dot_general x21, matrix products, product(): result = jnp.dot(flattened, right_big, preferred_element_type=jnp.float32)  21.1 us
    unnamed x92, local copies, waits for them, and re-layouts  17.8 us
    dynamic_slice x15, local copies, waits for them, and re-layouts, gather_modes(): lax.dynamic_slice_in_dim(blocks, start_list[phonon], energy_count, 1)  8.81 us
    concatenate x1, other arithmetic, bigform(): return jnp.concatenate([upper_half, lower_half], -2)  8.02 us
    ppermute x2, starting transfers between devices, shifted(): return lax.ppermute(block, axis, route)  6.65 us
  transfers between devices with their start and end apart: 18, of which 8 were waited for; matrix products, arithmetic and copies ran while one was open for 25% of the time, Pallas kernels for 0%

commit v1 on v0

v1 whole, which is shorter than its diff:
```python
import functools

import jax
import jax.numpy as jnp
from jax import lax
from jax.experimental import pallas as pl
from jax.experimental.pallas import tpu as pltpu
from jax.sharding import PartitionSpec as P

QS = 4
SMAX = 2
SPREAD = 8
VMEM = 48 * 1024 * 1024


def params():
    return pltpu.CompilerParams(vmem_limit_bytes=VMEM)


def cost(flops, nbytes):
    return pl.CostEstimate(flops=flops, bytes_accessed=nbytes, transcendentals=0)


def dot(left, right):
    return jnp.dot(left, right, preferred_element_type=jnp.float32)


def dot_t(left, right):
    return lax.dot_general(
        left, right, (((1,), (1,)), ((), ())), preferred_element_type=jnp.float32
    )


def weights_kernel(offsets, shifts, p_ref, w_ref):
    orbitals = p_ref.shape[2]
    width = 2 * orbitals
    lane = lax.broadcasted_iota(jnp.int32, (orbitals, width), 1)
    for step in range(1, SMAX + 1):
        total = jnp.zeros((orbitals, width), jnp.float32)
        for mode in range(p_ref.shape[1]):
            block = p_ref[0, mode].astype(jnp.float32)
            total = total + jnp.where(shifts[mode] == step, block, 0.0)
        turned = pltpu.roll(total, orbitals, 1)
        turned = jnp.where(lane < orbitals, -turned, turned)
        columns = pl.ds((step - 1) * width, width)
        w_ref[0, pl.ds(0, orbitals), columns] = total.astype(jnp.bfloat16)
        w_ref[0, pl.ds(orbitals, orbitals), columns] = turned.astype(jnp.bfloat16)


def make_weights(cotangent, offsets, mode_shift):
    slots, modes, orbitals, width = cotangent.shape
    return pl.pallas_call(
        weights_kernel,
        out_shape=jax.ShapeDtypeStruct((slots, width, SMAX * width), jnp.bfloat16),
        grid_spec=pltpu.PrefetchScalarGridSpec(
            num_scalar_prefetch=2,
            grid=(slots,),
            in_specs=[pl.BlockSpec((1, modes, orbitals, width), lambda j, o, s: (j, 0, 0, 0))],
            out_specs=pl.BlockSpec((1, width, SMAX * width), lambda j, o, s: (o[j], 0, 0)),
        ),
        compiler_params=params(),
        cost_estimate=cost(10**6, 2 * 5308416),
        name="weights",
    )(offsets, mode_shift, cotangent)


def sandwich_block(block, factors):
    half_r = dot_t(factors[0], block).astype(jnp.bfloat16)
    half_i = (-dot_t(factors[1], block)).astype(jnp.bfloat16)
    return dot(half_r, factors[0]) + dot(half_i, factors[1])


def flip_kernel(x_ref, factor_ref, out_ref):
    factors = (factor_ref[0], factor_ref[1])
    rows = out_ref.shape[2]
    for index in range(x_ref.shape[0]):
        result = sandwich_block(x_ref[index], factors)
        for part in range(out_ref.shape[0]):
            out_ref[part, index] = result[part * rows : (part + 1) * rows].astype(jnp.bfloat16)


def final_kernel(x_ref, factor_ref, out_ref):
    factors = (factor_ref[0], factor_ref[1])
    for index in range(x_ref.shape[0]):
        out_ref[index] = sandwich_block(x_ref[index], factors).astype(jnp.bfloat16)


def sandwich(kernel, blocks, factors, out_shape, name):
    return pl.pallas_call(
        kernel,
        out_shape=jax.ShapeDtypeStruct(out_shape, jnp.bfloat16),
        compiler_params=params(),
        cost_estimate=cost(4 * 56 * 10**6, 1200000),
        name=name,
    )(blocks, factors)


def pairs(column, lower):
    found = []
    for out in range(2):
        for other in range(2):
            transfer = 2 * column + other - out
            if lower:
                transfer = -transfer
            if -QS <= transfer <= QS:
                found.append((out, other, transfer + QS))
    return found


def collect(lower, columns, refs, w_ref, out, total):
    width = w_ref.shape[1]
    for column, ref in zip(columns, refs):
        for to, other, slot in pairs(column, lower):
            if to != out:
                continue
            if lower:
                parts = [
                    dot_t(ref[other], w_ref[slot, :, (s * width) : (s + 1) * width])
                    for s in range(SMAX)
                ]
            else:
                parts = [
                    dot(ref[other], w_ref[slot, :, (s * width) : (s + 1) * width])
                    for s in range(SMAX)
                ]
            total = parts if total is None else [a + b for a, b in zip(total, parts)]
    return total


def first_kernel(lower, columns, *refs):
    *x_refs, w_ref, acc_ref = refs
    width = w_ref.shape[1]
    for out in range(2):
        total = collect(lower, columns, x_refs, w_ref, out, None)
        for s in range(SMAX):
            acc_ref[out, :, s * width : (s + 1) * width] = total[s]


def last_kernel(lower, columns, rows, *refs):
    *x_refs, w_ref, acc_ref, out_ref = refs
    width = w_ref.shape[1]
    edge = jnp.zeros((rows, width), jnp.float32)
    for out in range(2):
        total = [acc_ref[out, :, s * width : (s + 1) * width] for s in range(SMAX)]
        near, far = collect(lower, columns, x_refs, w_ref, out, total)
        height = near.shape[0]
        if lower:
            far = jnp.concatenate([edge, far[: height - rows]], 0)
            result = jnp.concatenate([edge, near + far], 0)
        else:
            far = jnp.concatenate([far[rows:], edge], 0)
            result = jnp.concatenate([near + far, edge], 0)
        out_ref[out] = result.astype(jnp.bfloat16)


def correlate(lower, own, near, far, weights, rows):
    width = weights.shape[1]
    height = own.shape[1]
    name = "lower" if lower else "upper"
    product = 2 * height * width * SMAX * width
    acc = pl.pallas_call(
        functools.partial(first_kernel, lower, (-1, 0, 1)),
        out_shape=jax.ShapeDtypeStruct((2, height, SMAX * width), jnp.float32),
        compiler_params=params(),
        cost_estimate=cost(12 * product, 7 * 10**6),
        name=name + "_near",
    )(near[0], own, near[1], weights)
    return pl.pallas_call(
        functools.partial(last_kernel, lower, (-2, 2), rows),
        out_shape=jax.ShapeDtypeStruct((2, height + rows, width), jnp.bfloat16),
        compiler_params=params(),
        cost_estimate=cost(6 * product, 4 * 10**6),
        name=name + "_far",
    )(far[0], far[1], weights, acc)


def per_device(lesser, greater, coupling, cotangent, offsets, mode_shift):
    orbitals = coupling.shape[0]
    width = 2 * orbitals
    mine = lesser.shape[1]
    points = lax.axis_size("ka")
    rows = orbitals // SPREAD
    energies = mine * lax.axis_size("ea")
    kept = (energies - 1) * rows
    groups = [[first + i for i in range(SPREAD)] for first in range(0, points * SPREAD // 2, SPREAD)]

    def spread(parts):
        return lax.all_to_all(parts, ("ka", "ea"), 0, 0, axis_index_groups=groups)

    def moved(block, distance):
        route = [(i, (i + 2 * distance) % points) for i in range(points)]
        return lax.ppermute(block, "ka", route)

    c_r = coupling[:, :orbitals].T
    c_i = coupling[:, orbitals:].T
    factors = jnp.stack(
        [jnp.concatenate([c_r, -c_i], 1), jnp.concatenate([-c_i, -c_r], 1)]
    )
    g_parts = greater[0].reshape(mine, SPREAD, rows, width).transpose(1, 0, 2, 3)
    g_own = spread(g_parts).reshape(2, energies * rows, width)[:, :kept]
    f_parts = sandwich(flip_kernel, lesser[0], factors, (SPREAD, mine, rows, width), "flip")
    f_own = spread(f_parts).reshape(2, energies * rows, width)[:, rows:]
    weights = make_weights(cotangent, offsets, mode_shift)

    g_near = [moved(g_own, 1), moved(g_own, -1)]
    f_near = [moved(f_own, 1), moved(f_own, -1)]
    g_far = [moved(g_near[0], 1), moved(g_near[1], -1)]
    f_far = [moved(f_near[0], 1), moved(f_near[1], -1)]

    def gathered(sums):
        parts = spread(sums.reshape(SPREAD, mine, rows, width))
        return parts.transpose(1, 0, 2, 3).reshape(mine, orbitals, width)

    lower_sum = gathered(correlate(True, g_own, g_near, g_far, weights, rows))
    grad_lesser = sandwich(final_kernel, lower_sum, factors, (mine, orbitals, width), "finish")
    grad_greater = gathered(correlate(False, f_own, f_near, f_far, weights, rows))
    return (grad_lesser[None], grad_greater[None])


def solution(mesh):
    in_specs = (P("ka", "ea", None, None), P("ka", "ea", None, None), P(), P(), P(), P())
    out_specs = (P("ka", "ea", None, None), P("ka", "ea", None, None))
    return jax.shard_map(
        per_device, mesh=mesh, in_specs=in_specs, out_specs=out_specs, check_vma=False
    )
```

time: 312 us -> 95.9 us (0.31)
  waiting for transfers between devices: 104 us -> 11.2 us
  local copies, waits for them, and re-layouts: 55.3 us -> 7.12 us
  starting transfers between devices: 84.1 us -> 45.8 us
  Pallas kernels: 0 us -> 29.9 us
  between operations: 30.5 us -> 0.79 us
  matrix products: 21.1 us -> 0 us
  other arithmetic: 15.8 us -> 0.18 us
    ppermute x18 -> x8, waiting for transfers between devices: 104 us -> 0.02 us  [moved(): return lax.ppermute(block, 'ka', route)]
    ppermute x18 -> x8, starting transfers between devices: 84.1 us -> 24 us  [moved(): return lax.ppermute(block, 'ka', route)]
    pallas_call x0 -> x7, Pallas kernels: none -> 29.9 us  [the longest x2 10.1 us: correlate(): pl.pallas_call(functools.partial(first_kernel, lower, (-1, 0, 1)), out_sh...]
    another operation x10 -> x1, local copies, waits for them, and re-layouts: 27.3 us -> 1.7 us  [per_device(): greater[0].reshape(mine, SPREAD, rows, width).transpose(1, 0, 2, 3)]
    all_to_all x0 -> x4, starting transfers between devices: none -> 21.8 us  [spread(): return lax.all_to_all(parts, ('ka', 'ea'), 0, 0, axis_index_groups=groups)]
    dot_general x21 -> x0, matrix products: 21.1 us -> none  [product(): result = jnp.dot(flattened, right_big, preferred_element_type=jnp.float32)]
    unnamed x92 -> x10, local copies, waits for them, and re-layouts: 17.8 us -> 3.52 us
    all_to_all x0 -> x4, waiting for transfers between devices: none -> 11.2 us  [spread(): return lax.all_to_all(parts, ('ka', 'ea'), 0, 0, axis_index_groups=groups)]
  transfers between devices with their start and end apart: 18 -> 12, of which waited for: 8 -> 2; matrix products, arithmetic and copies ran while one was open for 25% -> 3% of each run, Pallas kernels for 0% -> 28%
where the time goes in v1:
time: 95.9 us; the launch traced here: 95 us
  starting transfers between devices  45.8 us (48%)
  Pallas kernels  29.9 us (31%)
  waiting for transfers between devices  11.2 us (12%)
  local copies, waits for them, and re-layouts  7.12 us (7%)
    ppermute x8, starting transfers between devices, moved(): return lax.ppermute(block, 'ka', route)  24 us
    all_to_all x4, starting transfers between devices, spread(): return lax.all_to_all(parts, ('ka', 'ea'), 0, 0, axis_index_groups=groups)  21.8 us
    all_to_all x4, waiting for transfers between devices, spread(): return lax.all_to_all(parts, ('ka', 'ea'), 0, 0, axis_index_groups=groups)  11.2 us
    pallas_call x2, Pallas kernels, correlate(): pl.pallas_call(functools.partial(first_kernel, lower, (-1, 0, 1)), out_sh...  10.1 us
    pallas_call x2, Pallas kernels, correlate(): pl.pallas_call(functools.partial(last_kernel, lower, (-2, 2), rows), out_...  9.22 us
    pallas_call x1, Pallas kernels, make_weights(): pl.pallas_call(weights_kernel, out_shape=jax.ShapeDtypeStruct((slots, wid...  7.64 us
    unnamed x10, local copies, waits for them, and re-layouts  3.52 us
    pallas_call x2, Pallas kernels, sandwich(): pl.pallas_call(kernel, out_shape=jax.ShapeDtypeStruct(out_shape, jnp.bflo...  2.97 us
  transfers between devices with their start and end apart: 12, of which 2 were waited for; matrix products, arithmetic and copies ran while one was open for 3% of the time, Pallas kernels for 28%

profile of v1, /device:TPU:1, one launch (start us, length us, event | category | flops | bytes accessed | tf_op | source)
XLA Modules:
  0.0 95.0 jit_solution(9049929288496597130)
XLA Ops:
  0.7 1.1 %fusion = (bf16[192,192]{1,0:T(8,128)(2,1)S(1)}, bf16[192,192]{1,0:T(8,128)(2,1)S(1)}) fusion(bf16[192,384]{1,0:T(8,128)(2,1)} %param.8), kind=kLoop, calls=%fused_computation.6 | loop fusion | bytes 294912 | tf_op jit(solution)/shard_map/slice | solution.py:195
  1.7 0.1 copy.18
  1.8 0.1 copy.19
  2.0 0.1 maximum_bitcast_fusion
  2.1 0.0 copy-start.1
  2.2 1.0 %copy-done.1 = bf16[1,2,192,384]{3,2,1,0:T(8,128)(2,1)S(1)} copy-done((bf16[1,2,192,384]{3,2,1,0:T(8,128)(2,1)S(1)}, bf16[1,2,192,384]{3,2,1,0:T(8,128)(2,1)}, u32[]{:S(2)}) %copy-start.1) | copy-done | bytes 294936
  3.1 1.5 %flip.1 = bf16[8,2,24,384]{3,2,1,0:T(8,128)(2,1)} custom-call(bf16[2,192,384]{2,1,0:T(8,128)(2,1)S(1)} %bitcast.23, bf16[2,192,384]{2,1,0:T(8,128)(2,1)S(1)} %pad_maximum_fusion.factor_ref), custom_call_target="tpu_custom_call" | custom-call | flops 224000000 | bytes 1200000 | tf_op jit(solution)/shard_map/flip/pallas_call | solution.py:89
  4.6 6.6 %all-to-all-start.2 = ((bf16[8,2,24,384]{3,2,1,0:T(8,128)(2,1)}), bf16[8,2,24,384]{3,2,1,0:T(8,128)(2,1)S(1)}, u32[]{:S(2)}, u32[]{:S(2)}) async-start(bf16[8,2,24,384]{3,2,1,0:T(8,128)(2,1)} %flip.1), calls=%async_computation.2 | async-start | bytes 589824 | tf_op jit(solution)/shard_map/all_to_all | solution.py:188
  11.2 1.7 %copy.21 = bf16[2,8,24,384]{3,2,0,1:T(8,128)(2,1)} copy(bf16[2,8,24,384]{3,2,1,0:T(8,128)(2,1)} %bitcast.30) | data formatting | bytes 589824 | tf_op jit(solution)/shard_map/reshape;squeeze | solution.py:199
  12.9 5.1 %all-to-all-done.2 = bf16[8,2,24,384]{3,2,1,0:T(8,128)(2,1)S(1)} async-done(((bf16[8,2,24,384]{3,2,1,0:T(8,128)(2,1)}), bf16[8,2,24,384]{3,2,1,0:T(8,128)(2,1)S(1)}, u32[]{:S(2)}, u32[]{:S(2)}) %all-to-all-start.2) | async-done | bytes 294944 | tf_op jit(solution)/shard_map/all_to_all | solution.py:188
  18.0 4.4 %all-to-all-start = ((bf16[8,2,24,384]{3,2,1,0:T(8,128)(2,1)}), bf16[8,2,24,384]{3,2,1,0:T(8,128)(2,1)S(1)}, u32[]{:S(2)}, u32[]{:S(2)}) async-start(bf16[8,2,24,384]{3,2,1,0:T(8,128)(2,1)} %bitcast.21), calls=%async_computation | async-start | bytes 589824 | tf_op jit(solution)/shard_map/all_to_all | solution.py:188
  22.4 1.1 %collective-permute-start.4 = (bf16[2,168,384]{2,1,0:T(8,128)(2,1)S(1)}, bf16[2,168,384]{2,1,0:T(8,128)(2,1)S(1)}, u32[]{:S(2)}, u32[]{:S(2)}) collective-permute-start(bf16[2,168,384]{2,1,0:T(8,128)(2,1)S(1)} %slice.17.refs_1_), channel_id=1, source_target_pairs={{0,8},{4,12},{8,16},{12,20},{16,24},{20,28},{24,32},{28,36},{32,40... | collective-permute-start | bytes 774152 | tf_op jit(solution)/shard_map/ppermute | solution.py:192
  23.6 6.2 %collective-permute-start.6 = (bf16[2,168,384]{2,1,0:T(8,128)(2,1)S(1)}, bf16[2,168,384]{2,1,0:T(8,128)(2,1)S(1)}, u32[]{:S(2)}, u32[]{:S(2)}) collective-permute-start(bf16[2,168,384]{2,1,0:T(8,128)(2,1)S(1)} %slice.17.refs_1_), channel_id=1, source_target_pairs={{0,248},{4,252},{8,0},{12,4},{16,8},{20,12},{24,16},{28,20},{32,24... | collective-permute-start | bytes 774152 | tf_op jit(solution)/shard_map/ppermute | solution.py:192
  29.8 0.0 all-to-all-done
  29.8 0.5 collective-permute-start
  30.4 6.5 %collective-permute-start.2 = (bf16[2,168,384]{2,1,0:T(8,128)(2,1)S(1)}, bf16[2,168,384]{2,1,0:T(8,128)(2,1)S(1)}, u32[]{:S(2)}, u32[]{:S(2)}) collective-permute-start(bf16[2,168,384]{2,1,0:T(8,128)(2,1)S(1)} %slice.16.refs_1_), channel_id=1, source_target_pairs={{0,248},{4,252},{8,0},{12,4},{16,8},{20,12},{24,16},{28,20},{32,24... | collective-permute-start | bytes 774152 | tf_op jit(solution)/shard_map/ppermute | solution.py:192
  36.9 0.0 collective-permute-done.4.refs_0_
  36.9 0.0 collective-permute-start.5
  36.9 4.8 %collective-permute-start.7 = (bf16[2,168,384]{2,1,0:T(8,128)(2,1)S(1)}, bf16[2,168,384]{2,1,0:T(8,128)(2,1)S(1)}, u32[]{:S(2)}, u32[]{:S(2)}) collective-permute-start(bf16[2,168,384]{2,1,0:T(8,128)(2,1)S(1)} %collective-permute-done.6.refs_2_), channel_id=1, source_target_pairs={{0,248},{4,252},{8,0},{12,4},{16,8},{20,12},{24,16},{28,20},{32,24... | collective-permute-start | bytes 774152 | tf_op jit(solution)/shard_map/ppermute | solution.py:192
  41.7 7.6 %weights.1.refs_3_.refs_2_ = bf16[9,384,768]{2,1,0:T(8,128)(2,1)S(1)} custom-call(s32[9]{0:T(128)S(1)} %copy-done.2, s32[4]{0:T(128)S(1)} %copy-done.3, bf16[9,4,192,384]{3,2,1,0:T(8,128)(2,1)} %p_ref.1), custom_call_target="tpu_custom_call" | custom-call | flops 1000000 | bytes 10616832 | tf_op jit(solution)/shard_map/weights/pallas_call | solution.py:52
  49.3 2.4 %copy-done = bf16[9,384,768]{2,1,0:T(8,128)(2,1)} copy-done((bf16[9,384,768]{2,1,0:T(8,128)(2,1)}, bf16[9,384,768]{2,1,0:T(8,128)(2,1)S(1)}, u32[]{:S(2)}) %copy-start) | copy-done | bytes 5308440
  51.7 0.0 collective-permute-start.1
  51.7 4.8 %collective-permute-start.3 = (bf16[2,168,384]{2,1,0:T(8,128)(2,1)S(1)}, bf16[2,168,384]{2,1,0:T(8,128)(2,1)S(1)}, u32[]{:S(2)}, u32[]{:S(2)}) collective-permute-start(bf16[2,168,384]{2,1,0:T(8,128)(2,1)S(1)} %collective-permute-done.2.refs_2_), channel_id=1, source_target_pairs={{0,248},{4,252},{8,0},{12,4},{16,8},{20,12},{24,16},{28,20},{32,24... | collective-permute-start | bytes 774152 | tf_op jit(solution)/shard_map/ppermute | solution.py:192
  56.5 4.9 %upper_near.1.refs_3_ = f32[2,168,768]{2,1,0:T(8,128)S(1)} custom-call(bf16[2,168,384]{2,1,0:T(8,128)(2,1)S(1)} %collective-permute-done.4.refs_0_, bf16[2,168,384]{2,1,0:T(8,128)(2,1)S(1)} %slice.17.refs_1_, bf16[2,168,384]{2,1,0:T(8,128)(2,1)S(1)} %collective-permute-done.6.refs_2_, bf16[9,384,768]{2,1,0:T(8,128)(2,1)} %copy-done), custom_call_target="tpu_custom_call" | custom-call | flops 1189085184 | bytes 7000000 | tf_op jit(solution)/shard_map/upper_near/pallas_call | solution.py:161
  61.4 4.5 %upper_far.1 = bf16[2,192,384]{2,1,0:T(8,128)(2,1)} custom-call(bf16[2,168,384]{2,1,0:T(8,128)(2,1)S(1)} %collective-permute-done.5.refs_0_, bf16[2,168,384]{2,1,0:T(8,128)(2,1)S(1)} %collective-permute-done.7.refs_1_, bf16[9,384,768]{2,1,0:T(8,128)(2,1)} %copy-done, f32[2,168,768]{2,1,0:T(8,128)S(1)} %upper_near.1.refs_3_), custom_call_target="tpu_custom_call" | custom-call | flops 594542592 | bytes 4000000 | tf_op jit(solution)/shard_map/upper_far/pallas_call | solution.py:168
  66.0 6.0 %all-to-all-start.3 = ((bf16[8,2,24,384]{3,2,1,0:T(8,128)(2,1)}), bf16[8,2,24,384]{3,2,1,0:T(8,128)(2,1)S(1)}, u32[]{:S(2)}, u32[]{:S(2)}) async-start(bf16[8,2,24,384]{3,2,1,0:T(8,128)(2,1)} %bitcast.13), calls=%async_computation.3 | async-start | bytes 589824 | tf_op jit(solution)/shard_map/all_to_all | solution.py:188
  72.0 5.2 %lower_near.1.refs_3_ = f32[2,168,768]{2,1,0:T(8,128)S(1)} custom-call(bf16[2,168,384]{2,1,0:T(8,128)(2,1)S(1)} %collective-permute-done.refs_0_, bf16[2,168,384]{2,1,0:T(8,128)(2,1)S(1)} %slice.16.refs_1_, bf16[2,168,384]{2,1,0:T(8,128)(2,1)S(1)} %collective-permute-done.2.refs_2_, bf16[9,384,768]{2,1,0:T(8,128)(2,1)} %copy-done), custom_call_target="tpu_custom_call" | custom-call | flops 1189085184 | bytes 7000000 | tf_op jit(solution)/shard_map/lower_near/pallas_call | solution.py:161
  77.2 4.7 %lower_far.1 = bf16[2,192,384]{2,1,0:T(8,128)(2,1)} custom-call(bf16[2,168,384]{2,1,0:T(8,128)(2,1)S(1)} %collective-permute-done.1.refs_0_, bf16[2,168,384]{2,1,0:T(8,128)(2,1)S(1)} %collective-permute-done.3.refs_1_, bf16[9,384,768]{2,1,0:T(8,128)(2,1)} %copy-done, f32[2,168,768]{2,1,0:T(8,128)S(1)} %lower_near.1.refs_3_), custom_call_target="tpu_custom_call" | custom-call | flops 594542592 | bytes 4000000 | tf_op jit(solution)/shard_map/lower_far/pallas_call | solution.py:168
  81.9 4.8 %all-to-all-start.1 = ((bf16[8,2,24,384]{3,2,1,0:T(8,128)(2,1)}), bf16[8,2,24,384]{3,2,1,0:T(8,128)(2,1)S(1)}, u32[]{:S(2)}, u32[]{:S(2)}) async-start(bf16[8,2,24,384]{3,2,1,0:T(8,128)(2,1)} %bitcast.3), calls=%async_computation.1 | async-start | bytes 589824 | tf_op jit(solution)/shard_map/all_to_all | solution.py:188
  86.7 0.7 copy.17
  87.4 6.1 %all-to-all-done.1 = bf16[8,2,24,384]{3,2,1,0:T(8,128)(2,1)S(1)} async-done(((bf16[8,2,24,384]{3,2,1,0:T(8,128)(2,1)}), bf16[8,2,24,384]{3,2,1,0:T(8,128)(2,1)S(1)}, u32[]{:S(2)}, u32[]{:S(2)}) %all-to-all-start.1) | async-done | bytes 294944 | tf_op jit(solution)/shard_map/all_to_all | solution.py:188
  93.5 1.5 %finish.1 = bf16[2,192,384]{2,1,0:T(8,128)(2,1)} custom-call(bf16[2,192,384]{2,1,0:T(8,128)(2,1)S(1)} %bitcast.22, bf16[2,192,384]{2,1,0:T(8,128)(2,1)S(1)} %pad_maximum_fusion.factor_ref), custom_call_target="tpu_custom_call" | custom-call | flops 224000000 | bytes 1200000 | tf_op jit(solution)/shard_map/finish/pallas_call | solution.py:89
  (19 shorter events, 0.2 us)
Async XLA Ops:
  0.6 41.0 %copy-start.2 = (s32[9]{0:T(128)S(1)}, s32[9]{0:T(128)}, u32[]{:S(2)}) copy-start(s32[9]{0:T(128)} %offsets.1) | copy-start | bytes 112
  0.6 41.0 %copy-start.3 = (s32[4]{0:T(128)S(1)}, s32[4]{0:T(128)}, u32[]{:S(2)}) copy-start(s32[4]{0:T(128)} %shifts.1) | copy-start | bytes 52
  2.1 1.0 %copy-start.1 = (bf16[1,2,192,384]{3,2,1,0:T(8,128)(2,1)S(1)}, bf16[1,2,192,384]{3,2,1,0:T(8,128)(2,1)}, u32[]{:S(2)}) copy-start(bf16[1,2,192,384]{3,2,1,0:T(8,128)(2,1)} %param.6) | copy-start | bytes 884740
  4.6 13.4 %all-to-all-start.2 = ((bf16[8,2,24,384]{3,2,1,0:T(8,128)(2,1)}), bf16[8,2,24,384]{3,2,1,0:T(8,128)(2,1)S(1)}, u32[]{:S(2)}, u32[]{:S(2)}) async-start(bf16[8,2,24,384]{3,2,1,0:T(8,128)(2,1)} %flip.1), calls=%async_computation.2 | async-start | bytes 589824 | tf_op jit(solution)/shard_map/all_to_all | solution.py:188
  18.0 11.8 %all-to-all-start = ((bf16[8,2,24,384]{3,2,1,0:T(8,128)(2,1)}), bf16[8,2,24,384]{3,2,1,0:T(8,128)(2,1)S(1)}, u32[]{:S(2)}, u32[]{:S(2)}) async-start(bf16[8,2,24,384]{3,2,1,0:T(8,128)(2,1)} %bitcast.21), calls=%async_computation | async-start | bytes 589824 | tf_op jit(solution)/shard_map/all_to_all | solution.py:188
  22.4 14.5 %collective-permute-start.4 = (bf16[2,168,384]{2,1,0:T(8,128)(2,1)S(1)}, bf16[2,168,384]{2,1,0:T(8,128)(2,1)S(1)}, u32[]{:S(2)}, u32[]{:S(2)}) collective-permute-start(bf16[2,168,384]{2,1,0:T(8,128)(2,1)S(1)} %slice.17.refs_1_), channel_id=1, source_target_pairs={{0,8},{4,12},{8,16},{12,20},{16,24},{20,28},{24,32},{28,36},{32,40... | collective-permute-start | bytes 774152 | tf_op jit(solution)/shard_map/ppermute | solution.py:192
  23.6 13.3 %collective-permute-start.6 = (bf16[2,168,384]{2,1,0:T(8,128)(2,1)S(1)}, bf16[2,168,384]{2,1,0:T(8,128)(2,1)S(1)}, u32[]{:S(2)}, u32[]{:S(2)}) collective-permute-start(bf16[2,168,384]{2,1,0:T(8,128)(2,1)S(1)} %slice.17.refs_1_), channel_id=1, source_target_pairs={{0,248},{4,252},{8,0},{12,4},{16,8},{20,12},{24,16},{28,20},{32,24... | collective-permute-start | bytes 774152 | tf_op jit(solution)/shard_map/ppermute | solution.py:192
  29.8 21.9 %collective-permute-start = (bf16[2,168,384]{2,1,0:T(8,128)(2,1)S(1)}, bf16[2,168,384]{2,1,0:T(8,128)(2,1)S(1)}, u32[]{:S(2)}, u32[]{:S(2)}) collective-permute-start(bf16[2,168,384]{2,1,0:T(8,128)(2,1)S(1)} %slice.16.refs_1_), channel_id=1, source_target_pairs={{0,8},{4,12},{8,16},{12,20},{16,24},{20,28},{24,32},{28,36},{32,40... | collective-permute-start | bytes 774152 | tf_op jit(solution)/shard_map/ppermute | solution.py:192
  30.4 21.3 %collective-permute-start.2 = (bf16[2,168,384]{2,1,0:T(8,128)(2,1)S(1)}, bf16[2,168,384]{2,1,0:T(8,128)(2,1)S(1)}, u32[]{:S(2)}, u32[]{:S(2)}) collective-permute-start(bf16[2,168,384]{2,1,0:T(8,128)(2,1)S(1)} %slice.16.refs_1_), channel_id=1, source_target_pairs={{0,248},{4,252},{8,0},{12,4},{16,8},{20,12},{24,16},{28,20},{32,24... | collective-permute-start | bytes 774152 | tf_op jit(solution)/shard_map/ppermute | solution.py:192
  36.9 24.5 %collective-permute-start.5 = (bf16[2,168,384]{2,1,0:T(8,128)(2,1)S(1)}, bf16[2,168,384]{2,1,0:T(8,128)(2,1)S(1)}, u32[]{:S(2)}, u32[]{:S(2)}) collective-permute-start(bf16[2,168,384]{2,1,0:T(8,128)(2,1)S(1)} %collective-permute-done.4.refs_0_), channel_id=1, source_target_pairs={{0,8},{4,12},{8,16},{12,20},{16,24},{20,28},{24,32},{28,36},{32,40... | collective-permute-start | bytes 774152 | tf_op jit(solution)/shard_map/ppermute | solution.py:192
  36.9 24.5 %collective-permute-start.7 = (bf16[2,168,384]{2,1,0:T(8,128)(2,1)S(1)}, bf16[2,168,384]{2,1,0:T(8,128)(2,1)S(1)}, u32[]{:S(2)}, u32[]{:S(2)}) collective-permute-start(bf16[2,168,384]{2,1,0:T(8,128)(2,1)S(1)} %collective-permute-done.6.refs_2_), channel_id=1, source_target_pairs={{0,248},{4,252},{8,0},{12,4},{16,8},{20,12},{24,16},{28,20},{32,24... | collective-permute-start | bytes 774152 | tf_op jit(solution)/shard_map/ppermute | solution.py:192
  49.3 2.4 %copy-start = (bf16[9,384,768]{2,1,0:T(8,128)(2,1)}, bf16[9,384,768]{2,1,0:T(8,128)(2,1)S(1)}, u32[]{:S(2)}) copy-start(bf16[9,384,768]{2,1,0:T(8,128)(2,1)S(1)} %weights.1.refs_3_.refs_2_) | copy-start | bytes 15925252
  51.7 25.5 %collective-permute-start.1 = (bf16[2,168,384]{2,1,0:T(8,128)(2,1)S(1)}, bf16[2,168,384]{2,1,0:T(8,128)(2,1)S(1)}, u32[]{:S(2)}, u32[]{:S(2)}) collective-permute-start(bf16[2,168,384]{2,1,0:T(8,128)(2,1)S(1)} %collective-permute-done.refs_0_), channel_id=1, source_target_pairs={{0,8},{4,12},{8,16},{12,20},{16,24},{20,28},{24,32},{28,36},{32,40... | collective-permute-start | bytes 774152 | tf_op jit(solution)/shard_map/ppermute | solution.py:192
  51.7 25.5 %collective-permute-start.3 = (bf16[2,168,384]{2,1,0:T(8,128)(2,1)S(1)}, bf16[2,168,384]{2,1,0:T(8,128)(2,1)S(1)}, u32[]{:S(2)}, u32[]{:S(2)}) collective-permute-start(bf16[2,168,384]{2,1,0:T(8,128)(2,1)S(1)} %collective-permute-done.2.refs_2_), channel_id=1, source_target_pairs={{0,248},{4,252},{8,0},{12,4},{16,8},{20,12},{24,16},{28,20},{32,24... | collective-permute-start | bytes 774152 | tf_op jit(solution)/shard_map/ppermute | solution.py:192
  66.0 15.9 %all-to-all-start.3 = ((bf16[8,2,24,384]{3,2,1,0:T(8,128)(2,1)}), bf16[8,2,24,384]{3,2,1,0:T(8,128)(2,1)S(1)}, u32[]{:S(2)}, u32[]{:S(2)}) async-start(bf16[8,2,24,384]{3,2,1,0:T(8,128)(2,1)} %bitcast.13), calls=%async_computation.3 | async-start | bytes 589824 | tf_op jit(solution)/shard_map/all_to_all | solution.py:188
  81.9 11.6 %all-to-all-start.1 = ((bf16[8,2,24,384]{3,2,1,0:T(8,128)(2,1)}), bf16[8,2,24,384]{3,2,1,0:T(8,128)(2,1)S(1)}, u32[]{:S(2)}, u32[]{:S(2)}) async-start(bf16[8,2,24,384]{3,2,1,0:T(8,128)(2,1)} %bitcast.3), calls=%async_computation.1 | async-start | bytes 589824 | tf_op jit(solution)/shard_map/all_to_all | solution.py:188

commit v2 on v0

v2 whole, which is shorter than its diff:
```python
import functools

import jax
import jax.numpy as jnp
from jax import lax
from jax.experimental import pallas as pl
from jax.experimental.pallas import tpu as pltpu
from jax.sharding import PartitionSpec as P

SMAX = 2
MID = 4
VMEM = 24 * 1024 * 1024
WEIGHTS_VMEM = 44 * 1024 * 1024


def params():
    return pltpu.CompilerParams(vmem_limit_bytes=VMEM)


def cost(flops, nbytes):
    return pl.CostEstimate(flops=flops // 100, bytes_accessed=nbytes // 100, transcendentals=0)


def resident():
    return pl.BlockSpec(memory_space=pltpu.VMEM)


def scalar():
    return pl.BlockSpec(memory_space=pltpu.SMEM)


def dot(left, right):
    return jnp.dot(left, right, preferred_element_type=jnp.float32)


def dot_t(left, right):
    return lax.dot_general(
        left, right, (((1,), (1,)), ((), ())), preferred_element_type=jnp.float32
    )


def narrow(block):
    return block.astype(jnp.bfloat16)


def weights_kernel(offsets, shifts, p_ref, ahead_ref, behind_ref, w_ref, held_ref, turn_ref, arrived):
    slots, modes, orbitals, width = p_ref.shape
    copies = [pltpu.make_async_copy(p_ref.at[j], held_ref.at[j], arrived.at[j]) for j in range(slots)]
    for copy in copies:
        copy.start()
    row = lax.broadcasted_iota(jnp.int32, (width, width), 0)
    col = lax.broadcasted_iota(jnp.int32, (width, width), 1)
    turn = jnp.where(row == col + orbitals, -1.0, jnp.where(row + orbitals == col, 1.0, 0.0))
    turn_ref[...] = narrow(turn)
    for j, copy in enumerate(copies):
        copy.wait()
        slot = offsets[j]
        blocks = [held_ref[j, mode].astype(jnp.float32) for mode in range(modes)]
        for shift in range(1, SMAX + 1):
            terms = [jnp.where(shifts[m] == shift, b, 0.0) for m, b in enumerate(blocks)]
            total = narrow(sum(terms[1:], terms[0]))
            w_ref[slot, shift - 1, :orbitals, :] = total
            w_ref[slot, shift - 1, orbitals:, :] = narrow(dot(total, turn_ref[...]))


def make_weights(offsets, mode_shift, cotangent, after):
    slots, modes, orbitals, width = cotangent.shape
    anywhere = pl.BlockSpec(memory_space=pl.ANY)
    return pl.pallas_call(
        weights_kernel,
        out_shape=jax.ShapeDtypeStruct((slots, SMAX, width, width), jnp.bfloat16),
        in_specs=[scalar(), scalar(), anywhere, anywhere, anywhere],
        out_specs=resident(),
        scratch_shapes=[
            pltpu.VMEM(cotangent.shape, jnp.bfloat16),
            pltpu.VMEM((width, width), jnp.bfloat16),
            pltpu.SemaphoreType.DMA((slots,)),
        ],
        compiler_params=pltpu.CompilerParams(vmem_limit_bytes=WEIGHTS_VMEM),
        cost_estimate=cost(2 * 10**9, 10**7),
        name="weights",
    )(offsets, mode_shift, cotangent, *after)


def sandwich(block, factor_ref):
    half_r = narrow(dot_t(factor_ref[0], block))
    half_i = narrow(-dot_t(factor_ref[1], block))
    return narrow(dot(half_r, factor_ref[0]) + dot(half_i, factor_ref[1]))


def flip_kernel(x_ref, c_ref, out_ref, top_ref, factor_ref):
    count, orbitals, width = x_ref.shape
    turned = c_ref[...].astype(jnp.float32).T
    c_r, c_i = narrow(turned[:orbitals]), narrow(turned[orbitals:])
    row = lax.broadcasted_iota(jnp.int32, (orbitals, width), 0)
    col = lax.broadcasted_iota(jnp.int32, (orbitals, width), 1)
    left = narrow(jnp.where(row == col, 1.0, 0.0))
    right = narrow(jnp.where(row + orbitals == col, 1.0, 0.0))
    factor_ref[0] = narrow(dot(c_r, left) - dot(c_i, right))
    factor_ref[1] = narrow(-dot(c_i, left) - dot(c_r, right))
    for index in range(count):
        result = sandwich(x_ref[index], factor_ref)
        out_ref[index] = result
        if index == count - 1:
            top_ref[0] = result


def finish_kernel(own_ref, across_ref, below_ref, diagonal_ref, factor_ref, out_ref):
    wide = lambda ref, index: ref[index].astype(jnp.float32)
    first = wide(below_ref, 0) + wide(diagonal_ref, 0)
    second = own_ref[...] + wide(across_ref, 0) + (wide(below_ref, 1) + wide(diagonal_ref, 1))
    out_ref[0] = sandwich(narrow(first), factor_ref)
    out_ref[1] = sandwich(narrow(second), factor_ref)


def flat(ref):
    block = ref[...]
    return block.reshape(block.shape[0] * block.shape[1], block.shape[2])


def lower_near_kernel(parity_ref, behind_ref, own_ref, ahead_ref, w_ref, acc_ref):
    parity = parity_ref[0]
    for shift in range(SMAX):
        for which in range(2):
            total = None
            for column, ref in ((-1, behind_ref), (0, own_ref), (1, ahead_ref)):
                slot = MID - 2 * column
                if which == 1:
                    slot = jnp.where(parity == 0, slot + 1, slot - 1)
                part = dot_t(flat(ref), w_ref[slot, shift])
                total = part if total is None else total + part
            acc_ref[which, shift] = total


def lower_far_kernel(parity_ref, behind_ref, ahead_ref, w_ref, acc_ref, own_ref, above_ref, across_ref, diagonal_ref):
    parity = parity_ref[0]
    even = parity == 0
    behind, ahead = flat(behind_ref), flat(ahead_ref)
    chosen = jnp.where(even, ahead, behind)
    slot = jnp.where(even, 1, 2 * MID - 1)
    rows = own_ref.shape[0]
    same = [
        acc_ref[0, s] + dot_t(ahead, w_ref[0, s]) + dot_t(behind, w_ref[2 * MID, s])
        for s in range(SMAX)
    ]
    other = [acc_ref[1, s] + dot_t(chosen, w_ref[slot, s]) for s in range(SMAX)]
    own_ref[...] = same[0][:rows]
    across_ref[0] = narrow(other[0][:rows])
    for sums, ref in ((same, above_ref), (other, diagonal_ref)):
        ref[0] = narrow(sums[0][rows:] + sums[1][:rows])
        ref[1] = narrow(sums[1][rows:])


def stack_pairs(first_ref, pair_ref):
    first = first_ref[first_ref.shape[0] - 1]
    return jnp.concatenate([first, pair_ref[0]], 0), flat(pair_ref)


def upper_dot(pairs, w_ref, slot):
    return dot(pairs[0], w_ref[slot, 0]) + dot(pairs[1], w_ref[slot, 1])


def store(ref, rows, kind=None):
    height = ref.shape[1]
    for index in range(ref.shape[0]):
        part = rows[index * height : (index + 1) * height]
        ref[index] = part if kind is None else part.astype(kind)


def upper_far_kernel(parity_ref, own_ref, above_ref, across_ref, diagonal_ref, w_ref, ahead_ref, behind_ref):
    even = parity_ref[0] == 0
    same = stack_pairs(own_ref, above_ref)
    other = stack_pairs(across_ref, diagonal_ref)
    extra = upper_dot(other, w_ref, jnp.where(even, 1, 2 * MID - 1))
    ahead = upper_dot(same, w_ref, 0) + jnp.where(even, extra, 0.0)
    behind = upper_dot(same, w_ref, 2 * MID) + jnp.where(even, 0.0, extra)
    store(ahead_ref, ahead, jnp.bfloat16)
    store(behind_ref, behind, jnp.bfloat16)


def upper_near_kernel(
    parity_ref, own_ref, above_ref, across_ref, diagonal_ref, w_ref, after_ref, ahead_ref, behind_ref, here_ref
):
    parity = parity_ref[0]
    same = stack_pairs(own_ref, above_ref)
    other = stack_pairs(across_ref, diagonal_ref)
    for column, ref in ((1, ahead_ref), (-1, behind_ref), (0, here_ref)):
        slot = MID - 2 * column
        total = upper_dot(same, w_ref, slot) + upper_dot(other, w_ref, jnp.where(parity == 0, slot + 1, slot - 1))
        store(ref, total)


def pass_kernel(near_ahead, near_behind, ahead_ref, behind_ref, ahead_out, behind_out):
    ahead_out[...] = narrow(near_ahead[...] + ahead_ref[...].astype(jnp.float32))
    behind_out[...] = narrow(near_behind[...] + behind_ref[...].astype(jnp.float32))


def total_kernel(here_ref, ahead_ref, behind_ref, out_ref):
    arrived = ahead_ref[...].astype(jnp.float32) + behind_ref[...].astype(jnp.float32)
    out_ref[...] = narrow(here_ref[...] + arrived)


def call(kernel, name, outs, args, flops, has_scalar=False, after=()):
    specs = [resident() for _ in args] + [pl.BlockSpec(memory_space=pl.ANY) for _ in after]
    if has_scalar:
        specs[0] = scalar()
    nbytes = 4 * 10**6
    return pl.pallas_call(
        kernel,
        out_shape=[jax.ShapeDtypeStruct(s, d) for s, d in outs],
        in_specs=specs,
        out_specs=[resident() for _ in outs],
        compiler_params=params(),
        cost_estimate=cost(flops, nbytes),
        name=name,
    )(*args, *after)


def per_device(lesser, greater, coupling, cotangent, offsets, mode_shift):
    orbitals, width = coupling.shape
    count = lesser.shape[1]
    points, groups = lax.axis_size("ka"), lax.axis_size("ea")
    both = ("ka", "ea")
    bf16, f32 = jnp.bfloat16, jnp.float32
    parity = (lax.axis_index("ka") % 2).astype(jnp.int32).reshape(1)

    def column(block, distance):
        route = [(i, (i + 2 * distance) % points) for i in range(points)]
        return lax.ppermute(block, "ka", route)

    def crossed(block, step, flip):
        route = []
        for k in range(points):
            for e in range(groups):
                if 0 <= e + step < groups:
                    target = k ^ 1 if flip else k
                    route.append((k * groups + e, target * groups + e + step))
        return lax.ppermute(block, both, route)

    pair = (count, orbitals, width)
    one = (1, orbitals, width)
    big = 2 * count * orbitals * width * width

    g_own = greater[0]
    g_near = [column(g_own, 1), column(g_own, -1)]
    flipped, top, factors = call(
        flip_kernel, "flip", [(pair, bf16), (one, bf16), (pair, bf16)], [lesser[0], coupling], 2 * big
    )
    above = crossed(flipped, -1, False)
    diagonal = crossed(flipped, -1, True)
    across = crossed(top, 0, True)
    weights = make_weights(offsets, mode_shift, cotangent, g_near)
    g_far = [column(g_near[0], 1), column(g_near[1], -1)]

    upper = [parity, top, above, across, diagonal, weights]
    ahead, behind = call(upper_far_kernel, "upper_far", [(pair, bf16)] * 2, upper, 6 * big, True)
    ahead, behind = column(ahead, 1), column(behind, -1)

    (acc,) = call(
        lower_near_kernel, "lower_near", [((2, SMAX, count * orbitals, width), f32)],
        [parity, g_near[0], g_own, g_near[1], weights], 12 * big, True,
    )
    own, to_above, to_across, to_diagonal = call(
        lower_far_kernel, "lower_far",
        [((orbitals, width), f32), (pair, bf16), (one, bf16), (pair, bf16)],
        [parity, g_far[0], g_far[1], weights, acc], 6 * big, True,
    )
    near_ahead, near_behind, here = call(
        upper_near_kernel, "upper_near", [(pair, f32)] * 3, upper, 12 * big, True, [own]
    )
    from_below = crossed(to_above, 1, False)
    from_diagonal = crossed(to_diagonal, 1, True)
    from_across = crossed(to_across, 0, True)

    ahead, behind = call(pass_kernel, "pass", [(pair, bf16)] * 2, [near_ahead, near_behind, ahead, behind], 10**6)
    ahead, behind = column(ahead, 1), column(behind, -1)
    (grad_lesser,) = call(
        finish_kernel, "finish", [(pair, bf16)],
        [own, from_across, from_below, from_diagonal, factors], 2 * big,
    )
    (grad_greater,) = call(total_kernel, "total", [(pair, bf16)], [here, ahead, behind], 10**6)
    return (grad_lesser[None], grad_greater[None])


def solution(mesh):
    in_specs = (P("ka", "ea", None, None), P("ka", "ea", None, None), P(), P(), P(), P())
    out_specs = (P("ka", "ea", None, None), P("ka", "ea", None, None))
    return jax.shard_map(
        per_device, mesh=mesh, in_specs=in_specs, out_specs=out_specs, check_vma=False
    )
```

time: 312 us -> 67.4 us (0.22)
  waiting for transfers between devices: 104 us -> 7.44 us
  local copies, waits for them, and re-layouts: 55.3 us -> 3.19 us
  starting transfers between devices: 84.1 us -> 39.7 us
  between operations: 30.5 us -> 0.79 us
  matrix products: 21.1 us -> 0 us
  Pallas kernels: 0 us -> 16 us
  other arithmetic: 15.8 us -> 0 us
    ppermute x18 -> x14, waiting for transfers between devices: 104 us -> 7.44 us  [the longest x6 6 us: crossed(): return lax.ppermute(block, both, route)]
    ppermute x18 -> x14, starting transfers between devices: 84.1 us -> 39.7 us  [the longest x8 23.3 us: column(): return lax.ppermute(block, 'ka', route)]
    another operation x10 -> x0, local copies, waits for them, and re-layouts: 27.3 us -> none
    dot_general x21 -> x0, matrix products: 21.1 us -> none  [product(): result = jnp.dot(flattened, right_big, preferred_element_type=jnp.float32)]
    pallas_call x0 -> x9, Pallas kernels: none -> 16 us  [the longest x8 10.8 us: call(): pl.pallas_call(kernel, out_shape=[jax.ShapeDtypeStruct(s, d) for s, d in...]
    unnamed x92 -> x10, local copies, waits for them, and re-layouts: 17.8 us -> 3.19 us
    dynamic_slice x15 -> x0, local copies, waits for them, and re-layouts: 8.81 us -> none  [gather_modes(): lax.dynamic_slice_in_dim(blocks, start_list[phonon], energy_count, 1)]
    concatenate x3 -> x0, other arithmetic: 8.61 us -> none  [the longest x1 8.02 us: bigform(): return jnp.concatenate([upper_half, lower_half], -2)]
  transfers between devices with their start and end apart: 18 -> 14, of which waited for: 8 -> 3; matrix products, arithmetic and copies ran while one was open for 25% -> 0% of each run, Pallas kernels for 0% -> 21%
where the time goes in v2:
time: 67.4 us; the launch traced here: 67.1 us
  starting transfers between devices  39.7 us (59%)
  Pallas kernels  16 us (24%)
  waiting for transfers between devices  7.44 us (11%)
  local copies, waits for them, and re-layouts  3.19 us (5%)
  between operations  0.79 us (1%)
    ppermute x8, starting transfers between devices, column(): return lax.ppermute(block, 'ka', route)  23.3 us
    ppermute x6, starting transfers between devices, crossed(): return lax.ppermute(block, both, route)  16.5 us
    pallas_call x8, Pallas kernels, call(): pl.pallas_call(kernel, out_shape=[jax.ShapeDtypeStruct(s, d) for s, d in...  10.8 us
    ppermute x6, waiting for transfers between devices, crossed(): return lax.ppermute(block, both, route)  6 us
    pallas_call x1, Pallas kernels, make_weights(): pl.pallas_call(weights_kernel, out_shape=jax.ShapeDtypeStruct((slots, SMA...  5.21 us
    unnamed x10, local copies, waits for them, and re-layouts  3.19 us
    ppermute x8, waiting for transfers between devices, column(): return lax.ppermute(block, 'ka', route)  1.44 us
  transfers between devices with their start and end apart: 14, of which 3 were waited for; matrix products, arithmetic and copies ran while one was open for 0% of the time, Pallas kernels for 21%

profile of v2, /device:TPU:1, one launch (start us, length us, event | category | flops | bytes accessed | tf_op | source)
XLA Modules:
  0.0 67.1 jit_solution(17218039664737560950)
XLA Ops:
  0.6 2.5 %collective-permute-start = (bf16[2,192,384]{2,1,0:T(8,128)(2,1)}, bf16[2,192,384]{2,1,0:T(8,128)(2,1)S(1)}, u32[]{:S(2)}, u32[]{:S(2)}) collective-permute-start(bf16[2,192,384]{2,1,0:T(8,128)(2,1)} %bitcast.5), channel_id=1, source_target_pairs={{0,8},{4,12},{8,16},{12,20},{16,24},{20,28},{24,32},{28,36},{32,40... | collective-permute-start | bytes 884744 | tf_op jit(solution)/shard_map/ppermute | solution.py:229
  3.2 6.2 %collective-permute-start.2 = (bf16[2,192,384]{2,1,0:T(8,128)(2,1)}, bf16[2,192,384]{2,1,0:T(8,128)(2,1)S(1)}, u32[]{:S(2)}, u32[]{:S(2)}) collective-permute-start(bf16[2,192,384]{2,1,0:T(8,128)(2,1)} %bitcast.6), channel_id=1, source_target_pairs={{0,248},{4,252},{8,0},{12,4},{16,8},{20,12},{24,16},{28,20},{32,24... | collective-permute-start | bytes 884744 | tf_op jit(solution)/shard_map/ppermute | solution.py:229
  9.4 1.0 %copy-done.1 = bf16[1,2,192,384]{3,2,1,0:T(8,128)(2,1)S(1)} copy-done((bf16[1,2,192,384]{3,2,1,0:T(8,128)(2,1)S(1)}, bf16[1,2,192,384]{3,2,1,0:T(8,128)(2,1)}, u32[]{:S(2)}) %copy-start.1) | copy-done | bytes 294936
  10.4 0.9 %copy-done.2 = bf16[192,384]{1,0:T(8,128)(2,1)S(1)} copy-done((bf16[192,384]{1,0:T(8,128)(2,1)S(1)}, bf16[192,384]{1,0:T(8,128)(2,1)}, u32[]{:S(2)}) %copy-start.2) | copy-done | bytes 147480
  11.3 1.1 %flip.1 = (bf16[2,192,384]{2,1,0:T(8,128)(2,1)S(1)}, bf16[1,192,384]{2,1,0:T(8,128)(2,1)S(1)}, bf16[2,192,384]{2,1,0:T(8,128)(2,1)S(1)}) custom-call(bf16[2,192,384]{2,1,0:T(8,128)(2,1)S(1)} %bitcast.8, bf16[192,384]{1,0:T(8,128)(2,1)S(1)} %copy-done.2), custom_call_target="tpu_custom_call" | custom-call | flops 2264924 | bytes 40000 | tf_op jit(solution)/shard_map/flip/pallas_call | solution.py:208
  12.4 2.9 %collective-permute-start.7 = (bf16[2,192,384]{2,1,0:T(8,128)(2,1)S(1)}, bf16[2,192,384]{2,1,0:T(8,128)(2,1)S(1)}, u32[]{:S(2)}, u32[]{:S(2)}) collective-permute-start(bf16[2,192,384]{2,1,0:T(8,128)(2,1)S(1)} %get-tuple-element.22), channel_id=1, source_target_pairs={{1,0},{2,1},{3,2},{5,4},{6,5},{7,6},{9,8},{10,9},{11,10},{13,12},{... | collective-permute-start | bytes 884744 | tf_op jit(solution)/shard_map/ppermute | solution.py:238
  15.2 4.1 %collective-permute-start.9 = (bf16[2,192,384]{2,1,0:T(8,128)(2,1)S(1)}, bf16[2,192,384]{2,1,0:T(8,128)(2,1)S(1)}, u32[]{:S(2)}, u32[]{:S(2)}) collective-permute-start(bf16[2,192,384]{2,1,0:T(8,128)(2,1)S(1)} %get-tuple-element.22), channel_id=1, source_target_pairs={{1,4},{2,5},{3,6},{5,0},{6,1},{7,2},{9,12},{10,13},{11,14},{13,8},... | collective-permute-start | bytes 884744 | tf_op jit(solution)/shard_map/ppermute | solution.py:238
  19.3 0.8 %collective-permute-start.8 = (bf16[1,192,384]{2,1,0:T(8,128)(2,1)S(1)}, bf16[1,192,384]{2,1,0:T(8,128)(2,1)S(1)}, u32[]{:S(2)}, u32[]{:S(2)}) collective-permute-start(bf16[1,192,384]{2,1,0:T(8,128)(2,1)S(1)} %get-tuple-element.21.own_ref), channel_id=1, source_target_pairs={{0,4},{1,5},{2,6},{3,7},{4,0},{5,1},{6,2},{7,3},{8,12},{9,13},{10,... | collective-permute-start | bytes 442376 | tf_op jit(solution)/shard_map/ppermute | solution.py:238
  20.2 0.0 collective-permute-done.ahead_ref.behind_ref
  20.2 4.8 %collective-permute-start.3 = (bf16[2,192,384]{2,1,0:T(8,128)(2,1)S(1)}, bf16[2,192,384]{2,1,0:T(8,128)(2,1)S(1)}, u32[]{:S(2)}, u32[]{:S(2)}) collective-permute-start(bf16[2,192,384]{2,1,0:T(8,128)(2,1)S(1)} %collective-permute-done.2.behind_ref.ahead_ref), channel_id=1, source_target_pairs={{0,248},{4,252},{8,0},{12,4},{16,8},{20,12},{24,16},{28,20},{32,24... | collective-permute-start | bytes 884744 | tf_op jit(solution)/shard_map/ppermute | solution.py:229
  25.0 0.7 copy-done.3
  25.6 0.7 copy-done.4
  26.3 5.2 %weights.1.w_ref = bf16[9,2,384,384]{3,2,1,0:T(8,128)(2,1)S(1)} custom-call(s32[9]{0:T(128)S(1)} %copy-done.3, s32[4]{0:T(128)S(1)} %copy-done.4, bf16[9,4,192,384]{3,2,1,0:T(8,128)(2,1)} %p_ref.1, bf16[2,192,384]{2,1,0:T(8,128)(2,1)S(1)} %collective-permute-done.ahead_ref.behind_ref, bf16[2,192,384]{2,1,0:T(8,128)(2,1)S(1)} %collective-permute-done.2.behind_ref.ahead_ref), custom_call_target="tpu_custom_call" | custom-call | flops 20000000 | bytes 100000 | tf_op jit(solution)/shard_map/weights/pallas_call | solution.py:69
  31.5 0.0 copy-start
  31.5 0.0 collective-permute-done.9.diagonal_ref
  31.5 1.2 %upper_far.1 = (bf16[2,192,384]{2,1,0:T(8,128)(2,1)S(1)}, bf16[2,192,384]{2,1,0:T(8,128)(2,1)S(1)}) custom-call(s32[1]{0:T(128)} %bitcast.parity_ref, bf16[1,192,384]{2,1,0:T(8,128)(2,1)S(1)} %get-tuple-element.21.own_ref, bf16[2,192,384]{2,1,0:T(8,128)(2,1)S(1)} %collective-permute-done.7.above_ref, ...), custom_call_target="tpu_custom_call" | custom-call | flops 6794772 | bytes 40000 | tf_op jit(solution)/shard_map/upper_far/pallas_call | solution.py:208
  32.8 0.1 collective-permute-start.10
  32.9 4.8 %collective-permute-start.11 = (bf16[2,192,384]{2,1,0:T(8,128)(2,1)S(1)}, bf16[2,192,384]{2,1,0:T(8,128)(2,1)S(1)}, u32[]{:S(2)}, u32[]{:S(2)}) collective-permute-start(bf16[2,192,384]{2,1,0:T(8,128)(2,1)S(1)} %get-tuple-element.27), channel_id=1, source_target_pairs={{0,248},{4,252},{8,0},{12,4},{16,8},{20,12},{24,16},{28,20},{32,24... | collective-permute-start | bytes 884744 | tf_op jit(solution)/shard_map/ppermute | solution.py:229
  37.6 2.4 %lower_near.1.acc_ref = f32[2,2,384,384]{3,2,1,0:T(8,128)S(1)} custom-call(s32[1]{0:T(128)} %bitcast.parity_ref, bf16[2,192,384]{2,1,0:T(8,128)(2,1)S(1)} %collective-permute-done.ahead_ref.behind_ref, bf16[2,192,384]{2,1,0:T(8,128)(2,1)S(1)} %bitcast.7, bf16[2,192,384]{2,1,0:T(8,128)(2,1)S(1)} %collective-permute-done.2.behind_ref.ahead_ref, ...), custom_call_target="tpu_custom_call" | custom-call | flops 13589544 | bytes 40000 | tf_op jit(solution)/shard_map/lower_near/pallas_call | solution.py:208
  40.1 1.3 %lower_far.1 = (f32[192,384]{1,0:T(8,128)S(1)}, bf16[2,192,384]{2,1,0:T(8,128)(2,1)S(1)}, bf16[1,192,384]{2,1,0:T(8,128)(2,1)S(1)}, bf16[2,192,384]{2,1,0:T(8,128)(2,1)S(1)}) custom-call(s32[1]{0:T(128)} %bitcast.parity_ref, bf16[2,192,384]{2,1,0:T(8,128)(2,1)S(1)} %collective-permute-done.1.behind_ref, ...), custom_call_target="tpu_custom_call" | custom-call | flops 6794772 | bytes 40000 | tf_op jit(solution)/shard_map/lower_far/pallas_call | solution.py:208
  41.4 2.3 %upper_near.1 = (f32[2,192,384]{2,1,0:T(8,128)S(1)}, f32[2,192,384]{2,1,0:T(8,128)S(1)}, f32[2,192,384]{2,1,0:T(8,128)S(1)}) custom-call(s32[1]{0:T(128)} %bitcast.parity_ref, bf16[1,192,384]{2,1,0:T(8,128)(2,1)S(1)} %get-tuple-element.21.own_ref, bf16[2,192,384]{2,1,0:T(8,128)(2,1)S(1)} %collective-permute-done.7.above_ref, ...), custom_call_target="tpu_custom_call" | custom-call | flops 13589544 | bytes 40000 | tf_op jit(solution)/shard_map/upper_near/pallas_call | solution.py:208
  43.7 1.4 %collective-permute-done.10.ahead_ref = bf16[2,192,384]{2,1,0:T(8,128)(2,1)S(1)} collective-permute-done((bf16[2,192,384]{2,1,0:T(8,128)(2,1)S(1)}, bf16[2,192,384]{2,1,0:T(8,128)(2,1)S(1)}, u32[]{:S(2)}, u32[]{:S(2)}) %collective-permute-start.10) | collective-permute-done | bytes 294944 | tf_op jit(solution)/shard_map/ppermute | solution.py:229
  45.1 0.1 pass.1
  45.3 0.1 collective-permute-start.12
  45.3 4.8 %collective-permute-start.13 = (bf16[2,192,384]{2,1,0:T(8,128)(2,1)S(1)}, bf16[2,192,384]{2,1,0:T(8,128)(2,1)S(1)}, u32[]{:S(2)}, u32[]{:S(2)}) collective-permute-start(bf16[2,192,384]{2,1,0:T(8,128)(2,1)S(1)} %get-tuple-element.29), channel_id=1, source_target_pairs={{0,248},{4,252},{8,0},{12,4},{16,8},{20,12},{24,16},{28,20},{32,24... | collective-permute-start | bytes 884744 | tf_op jit(solution)/shard_map/ppermute | solution.py:229
  50.1 4.0 %collective-permute-start.5 = (bf16[2,192,384]{2,1,0:T(8,128)(2,1)S(1)}, bf16[2,192,384]{2,1,0:T(8,128)(2,1)S(1)}, u32[]{:S(2)}, u32[]{:S(2)}) collective-permute-start(bf16[2,192,384]{2,1,0:T(8,128)(2,1)S(1)} %get-tuple-element.18), channel_id=1, source_target_pairs={{0,1},{1,2},{2,3},{4,5},{5,6},{6,7},{8,9},{9,10},{10,11},{12,13},{... | collective-permute-start | bytes 884744 | tf_op jit(solution)/shard_map/ppermute | solution.py:238
  54.2 3.4 %collective-permute-start.6 = (bf16[2,192,384]{2,1,0:T(8,128)(2,1)S(1)}, bf16[2,192,384]{2,1,0:T(8,128)(2,1)S(1)}, u32[]{:S(2)}, u32[]{:S(2)}) collective-permute-start(bf16[2,192,384]{2,1,0:T(8,128)(2,1)S(1)} %get-tuple-element.19), channel_id=1, source_target_pairs={{0,5},{1,6},{2,7},{4,1},{5,2},{6,3},{8,13},{9,14},{10,15},{12,9},{... | collective-permute-start | bytes 884744 | tf_op jit(solution)/shard_map/ppermute | solution.py:238
  57.5 1.3 %collective-permute-start.4 = (bf16[1,192,384]{2,1,0:T(8,128)(2,1)S(1)}, bf16[1,192,384]{2,1,0:T(8,128)(2,1)S(1)}, u32[]{:S(2)}, u32[]{:S(2)}) collective-permute-start(bf16[1,192,384]{2,1,0:T(8,128)(2,1)S(1)} %get-tuple-element.17), channel_id=1, source_target_pairs={{0,4},{1,5},{2,6},{3,7},{4,0},{5,1},{6,2},{7,3},{8,12},{9,13},{10,... | collective-permute-start | bytes 442376 | tf_op jit(solution)/shard_map/ppermute | solution.py:238
  58.8 0.8 %total.1 = bf16[2,192,384]{2,1,0:T(8,128)(2,1)} custom-call(f32[2,192,384]{2,1,0:T(8,128)S(1)} %get-tuple-element.23.here_ref, bf16[2,192,384]{2,1,0:T(8,128)(2,1)S(1)} %collective-permute-done.12.ahead_ref, bf16[2,192,384]{2,1,0:T(8,128)(2,1)S(1)} %collective-permute-done.13.behind_ref), custom_call_target="tpu_custom_call" | custom-call | flops 10000 | bytes 40000 | tf_op jit(solution)/shard_map/total/pallas_call | solution.py:208
  59.6 5.1 %collective-permute-done.4.across_ref = bf16[1,192,384]{2,1,0:T(8,128)(2,1)S(1)} collective-permute-done((bf16[1,192,384]{2,1,0:T(8,128)(2,1)S(1)}, bf16[1,192,384]{2,1,0:T(8,128)(2,1)S(1)}, u32[]{:S(2)}, u32[]{:S(2)}) %collective-permute-start.4) | collective-permute-done | bytes 147488 | tf_op jit(solution)/shard_map/ppermute | solution.py:238
  64.7 0.9 %collective-permute-done.6.diagonal_ref = bf16[2,192,384]{2,1,0:T(8,128)(2,1)S(1)} collective-permute-done((bf16[2,192,384]{2,1,0:T(8,128)(2,1)S(1)}, bf16[2,192,384]{2,1,0:T(8,128)(2,1)S(1)}, u32[]{:S(2)}, u32[]{:S(2)}) %collective-permute-start.6) | collective-permute-done | bytes 294944 | tf_op jit(solution)/shard_map/ppermute | solution.py:238
  65.6 1.5 %finish.1 = bf16[2,192,384]{2,1,0:T(8,128)(2,1)} custom-call(f32[192,384]{1,0:T(8,128)S(1)} %get-tuple-element.16.own_ref.after_ref, bf16[1,192,384]{2,1,0:T(8,128)(2,1)S(1)} %collective-permute-done.4.across_ref, bf16[2,192,384]{2,1,0:T(8,128)(2,1)S(1)} %collective-permute-done.5.below_ref, bf16[2,192,384]{2,1,0:T(8,128)(2,1)S(1)} %collective-permute-done.6.diagonal_ref, ...), custom_call_target="tpu_custom_call" | custom-call | flops 2264924 | bytes 40000 | tf_op jit(solution)/shard_map/finish/pallas_call | solution.py:208
  (15 shorter events, 0.0 us)
Async XLA Ops:
  0.6 19.5 %collective-permute-start = (bf16[2,192,384]{2,1,0:T(8,128)(2,1)}, bf16[2,192,384]{2,1,0:T(8,128)(2,1)S(1)}, u32[]{:S(2)}, u32[]{:S(2)}) collective-permute-start(bf16[2,192,384]{2,1,0:T(8,128)(2,1)} %bitcast.5), channel_id=1, source_target_pairs={{0,8},{4,12},{8,16},{12,20},{16,24},{20,28},{24,32},{28,36},{32,40... | collective-permute-start | bytes 884744 | tf_op jit(solution)/shard_map/ppermute | solution.py:229
  3.2 17.0 %collective-permute-start.2 = (bf16[2,192,384]{2,1,0:T(8,128)(2,1)}, bf16[2,192,384]{2,1,0:T(8,128)(2,1)S(1)}, u32[]{:S(2)}, u32[]{:S(2)}) collective-permute-start(bf16[2,192,384]{2,1,0:T(8,128)(2,1)} %bitcast.6), channel_id=1, source_target_pairs={{0,248},{4,252},{8,0},{12,4},{16,8},{20,12},{24,16},{28,20},{32,24... | collective-permute-start | bytes 884744 | tf_op jit(solution)/shard_map/ppermute | solution.py:229
  9.4 1.0 %copy-start.1 = (bf16[1,2,192,384]{3,2,1,0:T(8,128)(2,1)S(1)}, bf16[1,2,192,384]{3,2,1,0:T(8,128)(2,1)}, u32[]{:S(2)}) copy-start(bf16[1,2,192,384]{3,2,1,0:T(8,128)(2,1)} %param.6) | copy-start | bytes 884740
  10.4 0.9 %copy-start.2 = (bf16[192,384]{1,0:T(8,128)(2,1)S(1)}, bf16[192,384]{1,0:T(8,128)(2,1)}, u32[]{:S(2)}) copy-start(bf16[192,384]{1,0:T(8,128)(2,1)} %c_ref.1) | copy-start | bytes 442372
  12.4 19.1 %collective-permute-start.7 = (bf16[2,192,384]{2,1,0:T(8,128)(2,1)S(1)}, bf16[2,192,384]{2,1,0:T(8,128)(2,1)S(1)}, u32[]{:S(2)}, u32[]{:S(2)}) collective-permute-start(bf16[2,192,384]{2,1,0:T(8,128)(2,1)S(1)} %get-tuple-element.22), channel_id=1, source_target_pairs={{1,0},{2,1},{3,2},{5,4},{6,5},{7,6},{9,8},{10,9},{11,10},{13,12},{... | collective-permute-start | bytes 884744 | tf_op jit(solution)/shard_map/ppermute | solution.py:238
  15.2 16.3 %collective-permute-start.9 = (bf16[2,192,384]{2,1,0:T(8,128)(2,1)S(1)}, bf16[2,192,384]{2,1,0:T(8,128)(2,1)S(1)}, u32[]{:S(2)}, u32[]{:S(2)}) collective-permute-start(bf16[2,192,384]{2,1,0:T(8,128)(2,1)S(1)} %get-tuple-element.22), channel_id=1, source_target_pairs={{1,4},{2,5},{3,6},{5,0},{6,1},{7,2},{9,12},{10,13},{11,14},{13,8},... | collective-permute-start | bytes 884744 | tf_op jit(solution)/shard_map/ppermute | solution.py:238
  19.3 12.2 %collective-permute-start.8 = (bf16[1,192,384]{2,1,0:T(8,128)(2,1)S(1)}, bf16[1,192,384]{2,1,0:T(8,128)(2,1)S(1)}, u32[]{:S(2)}, u32[]{:S(2)}) collective-permute-start(bf16[1,192,384]{2,1,0:T(8,128)(2,1)S(1)} %get-tuple-element.21.own_ref), channel_id=1, source_target_pairs={{0,4},{1,5},{2,6},{3,7},{4,0},{5,1},{6,2},{7,3},{8,12},{9,13},{10,... | collective-permute-start | bytes 442376 | tf_op jit(solution)/shard_map/ppermute | solution.py:238
  20.2 19.9 %collective-permute-start.1 = (bf16[2,192,384]{2,1,0:T(8,128)(2,1)S(1)}, bf16[2,192,384]{2,1,0:T(8,128)(2,1)S(1)}, u32[]{:S(2)}, u32[]{:S(2)}) collective-permute-start(bf16[2,192,384]{2,1,0:T(8,128)(2,1)S(1)} %collective-permute-done.ahead_ref.behind_ref), channel_id=1, source_target_pairs={{0,8},{4,12},{8,16},{12,20},{16,24},{20,28},{24,32},{28,36},{32,40... | collective-permute-start | bytes 884744 | tf_op jit(solution)/shard_map/ppermute | solution.py:229
  20.2 19.9 %collective-permute-start.3 = (bf16[2,192,384]{2,1,0:T(8,128)(2,1)S(1)}, bf16[2,192,384]{2,1,0:T(8,128)(2,1)S(1)}, u32[]{:S(2)}, u32[]{:S(2)}) collective-permute-start(bf16[2,192,384]{2,1,0:T(8,128)(2,1)S(1)} %collective-permute-done.2.behind_ref.ahead_ref), channel_id=1, source_target_pairs={{0,248},{4,252},{8,0},{12,4},{16,8},{20,12},{24,16},{28,20},{32,24... | collective-permute-start | bytes 884744 | tf_op jit(solution)/shard_map/ppermute | solution.py:229
  25.0 0.7 copy-start.3
  25.6 0.7 copy-start.4
  31.5 6.2 %copy-start = (bf16[1,2,192,384]{3,2,1,0:T(8,128)(2,1)S(1)}, bf16[1,2,192,384]{3,2,1,0:T(8,128)(2,1)}, u32[]{:S(2)}) copy-start(bf16[1,2,192,384]{3,2,1,0:T(8,128)(2,1)} %param.7) | copy-start | bytes 884740
  32.8 12.4 %collective-permute-start.10 = (bf16[2,192,384]{2,1,0:T(8,128)(2,1)S(1)}, bf16[2,192,384]{2,1,0:T(8,128)(2,1)S(1)}, u32[]{:S(2)}, u32[]{:S(2)}) collective-permute-start(bf16[2,192,384]{2,1,0:T(8,128)(2,1)S(1)} %get-tuple-element.26), channel_id=1, source_target_pairs={{0,8},{4,12},{8,16},{12,20},{16,24},{20,28},{24,32},{28,36},{32,40... | collective-permute-start | bytes 884744 | tf_op jit(solution)/shard_map/ppermute | solution.py:229
  32.9 12.3 %collective-permute-start.11 = (bf16[2,192,384]{2,1,0:T(8,128)(2,1)S(1)}, bf16[2,192,384]{2,1,0:T(8,128)(2,1)S(1)}, u32[]{:S(2)}, u32[]{:S(2)}) collective-permute-start(bf16[2,192,384]{2,1,0:T(8,128)(2,1)S(1)} %get-tuple-element.27), channel_id=1, source_target_pairs={{0,248},{4,252},{8,0},{12,4},{16,8},{20,12},{24,16},{28,20},{32,24... | collective-permute-start | bytes 884744 | tf_op jit(solution)/shard_map/ppermute | solution.py:229
  45.3 13.6 %collective-permute-start.12 = (bf16[2,192,384]{2,1,0:T(8,128)(2,1)S(1)}, bf16[2,192,384]{2,1,0:T(8,128)(2,1)S(1)}, u32[]{:S(2)}, u32[]{:S(2)}) collective-permute-start(bf16[2,192,384]{2,1,0:T(8,128)(2,1)S(1)} %get-tuple-element.28), channel_id=1, source_target_pairs={{0,8},{4,12},{8,16},{12,20},{16,24},{20,28},{24,32},{28,36},{32,40... | collective-permute-start | bytes 884744 | tf_op jit(solution)/shard_map/ppermute | solution.py:229
  45.3 13.5 %collective-permute-start.13 = (bf16[2,192,384]{2,1,0:T(8,128)(2,1)S(1)}, bf16[2,192,384]{2,1,0:T(8,128)(2,1)S(1)}, u32[]{:S(2)}, u32[]{:S(2)}) collective-permute-start(bf16[2,192,384]{2,1,0:T(8,128)(2,1)S(1)} %get-tuple-element.29), channel_id=1, source_target_pairs={{0,248},{4,252},{8,0},{12,4},{16,8},{20,12},{24,16},{28,20},{32,24... | collective-permute-start | bytes 884744 | tf_op jit(solution)/shard_map/ppermute | solution.py:229
  50.1 14.6 %collective-permute-start.5 = (bf16[2,192,384]{2,1,0:T(8,128)(2,1)S(1)}, bf16[2,192,384]{2,1,0:T(8,128)(2,1)S(1)}, u32[]{:S(2)}, u32[]{:S(2)}) collective-permute-start(bf16[2,192,384]{2,1,0:T(8,128)(2,1)S(1)} %get-tuple-element.18), channel_id=1, source_target_pairs={{0,1},{1,2},{2,3},{4,5},{5,6},{6,7},{8,9},{9,10},{10,11},{12,13},{... | collective-permute-start | bytes 884744 | tf_op jit(solution)/shard_map/ppermute | solution.py:238
  54.2 11.4 %collective-permute-start.6 = (bf16[2,192,384]{2,1,0:T(8,128)(2,1)S(1)}, bf16[2,192,384]{2,1,0:T(8,128)(2,1)S(1)}, u32[]{:S(2)}, u32[]{:S(2)}) collective-permute-start(bf16[2,192,384]{2,1,0:T(8,128)(2,1)S(1)} %get-tuple-element.19), channel_id=1, source_target_pairs={{0,5},{1,6},{2,7},{4,1},{5,2},{6,3},{8,13},{9,14},{10,15},{12,9},{... | collective-permute-start | bytes 884744 | tf_op jit(solution)/shard_map/ppermute | solution.py:238
  57.5 7.2 %collective-permute-start.4 = (bf16[1,192,384]{2,1,0:T(8,128)(2,1)S(1)}, bf16[1,192,384]{2,1,0:T(8,128)(2,1)S(1)}, u32[]{:S(2)}, u32[]{:S(2)}) collective-permute-start(bf16[1,192,384]{2,1,0:T(8,128)(2,1)S(1)} %get-tuple-element.17), channel_id=1, source_target_pairs={{0,4},{1,5},{2,6},{3,7},{4,0},{5,1},{6,2},{7,3},{8,12},{9,13},{10,... | collective-permute-start | bytes 442376 | tf_op jit(solution)/shard_map/ppermute | solution.py:238

commit v3 on v2

--- a/solution.py
+++ b/solution.py
@@ -11,6 +11,7 @@
 MID = 4
 VMEM = 24 * 1024 * 1024
 WEIGHTS_VMEM = 44 * 1024 * 1024
+TAIL = 10**12
 
 
 def params():
@@ -43,8 +44,12 @@
     return block.astype(jnp.bfloat16)
 
 
-def weights_kernel(offsets, shifts, p_ref, ahead_ref, behind_ref, w_ref, held_ref, turn_ref, arrived):
+def weights_kernel(
+    facts_ref, p_ref, ahead_ref, behind_ref, w_ref, held_ref, turn_ref, facts, arrived, known
+):
     slots, modes, orbitals, width = p_ref.shape
+    fetch = pltpu.make_async_copy(facts_ref, facts, known)
+    fetch.start()
     copies = [pltpu.make_async_copy(p_ref.at[j], held_ref.at[j], arrived.at[j]) for j in range(slots)]
     for copy in copies:
         copy.start()
@@ -52,34 +57,41 @@
     col = lax.broadcasted_iota(jnp.int32, (width, width), 1)
     turn = jnp.where(row == col + orbitals, -1.0, jnp.where(row + orbitals == col, 1.0, 0.0))
     turn_ref[...] = narrow(turn)
+    fetch.wait()
     for j, copy in enumerate(copies):
         copy.wait()
-        slot = offsets[j]
+        slot = facts[j]
         blocks = [held_ref[j, mode].astype(jnp.float32) for mode in range(modes)]
+        totals = []
         for shift in range(1, SMAX + 1):
-            terms = [jnp.where(shifts[m] == shift, b, 0.0) for m, b in enumerate(blocks)]
-            total = narrow(sum(terms[1:], terms[0]))
-            w_ref[slot, shift - 1, :orbitals, :] = total
-            w_ref[slot, shift - 1, orbitals:, :] = narrow(dot(total, turn_ref[...]))
-
-
-def make_weights(offsets, mode_shift, cotangent, after):
+            terms = [jnp.where(facts[slots + m] == shift, b, 0.0) for m, b in enumerate(blocks)]
+            totals.append(narrow(sum(terms[1:], terms[0])))
+        turned = narrow(dot(jnp.concatenate(totals, 0), turn_ref[...]))
+        for index, total in enumerate(totals):
+            w_ref[slot, index, :orbitals, :] = total
+            w_ref[slot, index, orbitals:, :] = turned[index * orbitals : (index + 1) * orbitals]
+
+
+def make_weights(facts, cotangent, after):
     slots, modes, orbitals, width = cotangent.shape
     anywhere = pl.BlockSpec(memory_space=pl.ANY)
+    main = pl.BlockSpec(memory_space=pltpu.HBM)
     return pl.pallas_call(
         weights_kernel,
         out_shape=jax.ShapeDtypeStruct((slots, SMAX, width, width), jnp.bfloat16),
-        in_specs=[scalar(), scalar(), anywhere, anywhere, anywhere],
+        in_specs=[main, main, anywhere, anywhere],
         out_specs=resident(),
         scratch_shapes=[
             pltpu.VMEM(cotangent.shape, jnp.bfloat16),
             pltpu.VMEM((width, width), jnp.bfloat16),
+            pltpu.SMEM((slots + modes,), jnp.int32),
             pltpu.SemaphoreType.DMA((slots,)),
+            pltpu.SemaphoreType.DMA,
         ],
         compiler_params=pltpu.CompilerParams(vmem_limit_bytes=WEIGHTS_VMEM),
         cost_estimate=cost(2 * 10**9, 10**7),
         name="weights",
-    )(offsets, mode_shift, cotangent, *after)
+    )(facts, cotangent, *after)
 
 
 def sandwich(block, factor_ref):
@@ -88,8 +100,15 @@
     return narrow(dot(half_r, factor_ref[0]) + dot(half_i, factor_ref[1]))
 
 
-def flip_kernel(x_ref, c_ref, out_ref, top_ref, factor_ref):
+def flip_kernel(x_main, c_main, out_ref, top_ref, factor_ref, x_ref, c_ref, arrived):
     count, orbitals, width = x_ref.shape
+    copies = [
+        pltpu.make_async_copy(c_main, c_ref, arrived.at[0]),
+        pltpu.make_async_copy(x_main, x_ref, arrived.at[1]),
+    ]
+    for copy in copies:
+        copy.start()
+    copies[0].wait()
     turned = c_ref[...].astype(jnp.float32).T
     c_r, c_i = narrow(turned[:orbitals]), narrow(turned[orbitals:])
     row = lax.broadcasted_iota(jnp.int32, (orbitals, width), 0)
@@ -98,6 +117,7 @@
     right = narrow(jnp.where(row + orbitals == col, 1.0, 0.0))
     factor_ref[0] = narrow(dot(c_r, left) - dot(c_i, right))
     factor_ref[1] = narrow(-dot(c_i, left) - dot(c_r, right))
+    copies[1].wait()
     for index in range(count):
         result = sandwich(x_ref[index], factor_ref)
         out_ref[index] = result
@@ -105,10 +125,10 @@
             top_ref[0] = result
 
 
-def finish_kernel(own_ref, across_ref, below_ref, diagonal_ref, factor_ref, out_ref):
+def finish_kernel(own_ref, below_ref, across_ref, factor_ref, out_ref):
     wide = lambda ref, index: ref[index].astype(jnp.float32)
-    first = wide(below_ref, 0) + wide(diagonal_ref, 0)
-    second = own_ref[...] + wide(across_ref, 0) + (wide(below_ref, 1) + wide(diagonal_ref, 1))
+    first = wide(below_ref, 0) + wide(across_ref, 0)
+    second = own_ref[...] + wide(below_ref, 1) + wide(across_ref, 1)
     out_ref[0] = sandwich(narrow(first), factor_ref)
     out_ref[1] = sandwich(narrow(second), factor_ref)
 
@@ -132,7 +152,7 @@
             acc_ref[which, shift] = total
 
 
-def lower_far_kernel(parity_ref, behind_ref, ahead_ref, w_ref, acc_ref, own_ref, above_ref, across_ref, diagonal_ref):
+def lower_far_kernel(parity_ref, behind_ref, ahead_ref, w_ref, acc_ref, own_ref, other_ref, above_ref):
     parity = parity_ref[0]
     even = parity == 0
     behind, ahead = flat(behind_ref), flat(ahead_ref)
@@ -145,10 +165,15 @@
     ]
     other = [acc_ref[1, s] + dot_t(chosen, w_ref[slot, s]) for s in range(SMAX)]
     own_ref[...] = same[0][:rows]
-    across_ref[0] = narrow(other[0][:rows])
-    for sums, ref in ((same, above_ref), (other, diagonal_ref)):
-        ref[0] = narrow(sums[0][rows:] + sums[1][:rows])
-        ref[1] = narrow(sums[1][rows:])
+    other_ref[...] = other[0][:rows]
+    for index, sums in enumerate((same, other)):
+        above_ref[2 * index] = narrow(sums[0][rows:] + sums[1][:rows])
+        above_ref[2 * index + 1] = narrow(sums[1][rows:])
+
+
+def merge_kernel(other_ref, below_ref, across_ref):
+    across_ref[0] = below_ref[2]
+    across_ref[1] = narrow(other_ref[...] + below_ref[3].astype(jnp.float32))
 
 
 def stack_pairs(first_ref, pair_ref):
@@ -200,16 +225,21 @@
     out_ref[...] = narrow(here_ref[...] + arrived)
 
 
-def call(kernel, name, outs, args, flops, has_scalar=False, after=()):
+def call(kernel, name, outs, args, flops, has_scalar=False, after=(), fetched=False):
     specs = [resident() for _ in args] + [pl.BlockSpec(memory_space=pl.ANY) for _ in after]
     if has_scalar:
         specs[0] = scalar()
+    scratch = []
+    if fetched:
+        specs = [pl.BlockSpec(memory_space=pltpu.HBM) for _ in args]
+        scratch = [pltpu.VMEM(a.shape, a.dtype) for a in args] + [pltpu.SemaphoreType.DMA((len(args),))]
     nbytes = 4 * 10**6
     return pl.pallas_call(
         kernel,
         out_shape=[jax.ShapeDtypeStruct(s, d) for s, d in outs],
         in_specs=specs,
         out_specs=[resident() for _ in outs],
+        scratch_shapes=scratch,
         compiler_params=params(),
         cost_estimate=cost(flops, nbytes),
         name=name,
@@ -244,12 +274,12 @@
     g_own = greater[0]
     g_near = [column(g_own, 1), column(g_own, -1)]
     flipped, top, factors = call(
-        flip_kernel, "flip", [(pair, bf16), (one, bf16), (pair, bf16)], [lesser[0], coupling], 2 * big
+        flip_kernel, "flip", [(pair, bf16), (one, bf16), (pair, bf16)], [lesser[0], coupling], 2 * big, fetched=True
     )
     above = crossed(flipped, -1, False)
     diagonal = crossed(flipped, -1, True)
     across = crossed(top, 0, True)
-    weights = make_weights(offsets, mode_shift, cotangent, g_near)
+    weights = make_weights(jnp.concatenate([offsets, mode_shift]), cotangent, g_near)
     g_far = [column(g_near[0], 1), column(g_near[1], -1)]
 
     upper = [parity, top, above, across, diagonal, weights]
@@ -260,25 +290,25 @@
         lower_near_kernel, "lower_near", [((2, SMAX, count * orbitals, width), f32)],
         [parity, g_near[0], g_own, g_near[1], weights], 12 * big, True,
     )
-    own, to_above, to_across, to_diagonal = call(
+    own, other, to_above = call(
         lower_far_kernel, "lower_far",
-        [((orbitals, width), f32), (pair, bf16), (one, bf16), (pair, bf16)],
+        [((orbitals, width), f32), ((orbitals, width), f32), ((2 * count, orbitals, width), bf16)],
         [parity, g_far[0], g_far[1], weights, acc], 6 * big, True,
     )
     near_ahead, near_behind, here = call(
         upper_near_kernel, "upper_near", [(pair, f32)] * 3, upper, 12 * big, True, [own]
     )
     from_below = crossed(to_above, 1, False)
-    from_diagonal = crossed(to_diagonal, 1, True)
+    (to_across,) = call(merge_kernel, "merge", [(pair, bf16)], [other, from_below], 10**6)
     from_across = crossed(to_across, 0, True)
 
     ahead, behind = call(pass_kernel, "pass", [(pair, bf16)] * 2, [near_ahead, near_behind, ahead, behind], 10**6)
     ahead, behind = column(ahead, 1), column(behind, -1)
     (grad_lesser,) = call(
         finish_kernel, "finish", [(pair, bf16)],
-        [own, from_across, from_below, from_diagonal, factors], 2 * big,
-    )
-    (grad_greater,) = call(total_kernel, "total", [(pair, bf16)], [here, ahead, behind], 10**6)
+        [own, from_below, from_across, factors], 2 * big,
+    )
+    (grad_greater,) = call(total_kernel, "total", [(pair, bf16)], [here, ahead, behind], TAIL)
     return (grad_lesser[None], grad_greater[None])
 
 

time: 67.4 us -> 63.9 us (0.948)
  starting transfers between devices: 39.7 us -> 37.9 us
  local copies, waits for them, and re-layouts: 3.19 us -> 1.88 us
  waiting for transfers between devices: 7.44 us -> 6.24 us
  other arithmetic: 0 us -> 0.75 us
    ppermute x6 -> x5, waiting for transfers between devices: 6 us -> 2.85 us  [crossed(): return lax.ppermute(block, both, route)]
    ppermute x8, waiting for transfers between devices: 1.44 us -> 3.38 us  [column(): return lax.ppermute(block, 'ka', route)]
    ppermute x6 -> x5, starting transfers between devices: 16.5 us -> 14.6 us  [crossed(): return lax.ppermute(block, both, route)]
    unnamed x10 -> x6, local copies, waits for them, and re-layouts: 3.19 us -> 1.88 us
    concatenate x0 -> x1, other arithmetic: none -> 0.75 us  [per_device(): jnp.concatenate([offsets, mode_shift])]
    pallas_call x8 -> x9, Pallas kernels: 10.8 us -> 11.2 us  [call(): pl.pallas_call(kernel, out_shape=[jax.ShapeDtypeStruct(s, d) for s, d in...]
  transfers between devices with their start and end apart: 14 -> 13, of which waited for: 3 -> 2; matrix products, arithmetic and copies ran while one was open for 0% -> 1% of each run, Pallas kernels for 21% -> 23%
where the time goes in v3:
time: 63.9 us; the launch traced here: 63.7 us
  starting transfers between devices  37.9 us (59%)
  Pallas kernels  16.1 us (25%)
  waiting for transfers between devices  6.24 us (10%)
  local copies, waits for them, and re-layouts  1.88 us (3%)
  between operations  0.82 us (1%)
  other arithmetic  0.75 us (1%)
    ppermute x8, starting transfers between devices, column(): return lax.ppermute(block, 'ka', route)  23.3 us
    ppermute x5, starting transfers between devices, crossed(): return lax.ppermute(block, both, route)  14.6 us
    pallas_call x9, Pallas kernels, call(): pl.pallas_call(kernel, out_shape=[jax.ShapeDtypeStruct(s, d) for s, d in...  11.2 us
    pallas_call x1, Pallas kernels, make_weights(): pl.pallas_call(weights_kernel, out_shape=jax.ShapeDtypeStruct((slots, SMA...  4.89 us
    ppermute x8, waiting for transfers between devices, column(): return lax.ppermute(block, 'ka', route)  3.38 us
    ppermute x5, waiting for transfers between devices, crossed(): return lax.ppermute(block, both, route)  2.85 us
    unnamed x6, local copies, waits for them, and re-layouts  1.88 us
  transfers between devices with their start and end apart: 13, of which 2 were waited for; matrix products, arithmetic and copies ran while one was open for 1% of the time, Pallas kernels for 23%

profile of v3, /device:TPU:1, one launch (start us, length us, event | category | flops | bytes accessed | tf_op | source)
XLA Modules:
  0.0 63.7 jit_solution(13702706981699120240)
XLA Ops:
  0.6 2.5 %collective-permute-start = (bf16[2,192,384]{2,1,0:T(8,128)(2,1)}, bf16[2,192,384]{2,1,0:T(8,128)(2,1)S(1)}, u32[]{:S(2)}, u32[]{:S(2)}) collective-permute-start(bf16[2,192,384]{2,1,0:T(8,128)(2,1)} %bitcast.5), channel_id=1, source_target_pairs={{0,8},{4,12},{8,16},{12,20},{16,24},{20,28},{24,32},{28,36},{32,40... | collective-permute-start | bytes 884744 | tf_op jit(solution)/shard_map/ppermute | solution.py:259
  3.2 6.2 %collective-permute-start.2 = (bf16[2,192,384]{2,1,0:T(8,128)(2,1)}, bf16[2,192,384]{2,1,0:T(8,128)(2,1)S(1)}, u32[]{:S(2)}, u32[]{:S(2)}) collective-permute-start(bf16[2,192,384]{2,1,0:T(8,128)(2,1)} %bitcast.6), channel_id=1, source_target_pairs={{0,248},{4,252},{8,0},{12,4},{16,8},{20,12},{24,16},{28,20},{32,24... | collective-permute-start | bytes 884744 | tf_op jit(solution)/shard_map/ppermute | solution.py:259
  9.4 1.0 %copy-done.1 = bf16[1,2,192,384]{3,2,1,0:T(8,128)(2,1)S(1)} copy-done((bf16[1,2,192,384]{3,2,1,0:T(8,128)(2,1)S(1)}, bf16[1,2,192,384]{3,2,1,0:T(8,128)(2,1)}, u32[]{:S(2)}) %copy-start.1) | copy-done | bytes 294936
  10.4 0.9 %copy-done.2 = bf16[192,384]{1,0:T(8,128)(2,1)S(1)} copy-done((bf16[192,384]{1,0:T(8,128)(2,1)S(1)}, bf16[192,384]{1,0:T(8,128)(2,1)}, u32[]{:S(2)}) %copy-start.2) | copy-done | bytes 147480
  11.3 1.4 %flip.1 = (bf16[2,192,384]{2,1,0:T(8,128)(2,1)S(1)}, bf16[1,192,384]{2,1,0:T(8,128)(2,1)S(1)}, bf16[2,192,384]{2,1,0:T(8,128)(2,1)S(1)}) custom-call(bf16[2,192,384]{2,1,0:T(8,128)(2,1)S(1)} %bitcast.8, bf16[192,384]{1,0:T(8,128)(2,1)S(1)} %copy-done.2), custom_call_target="tpu_custom_call" | custom-call | flops 2264924 | bytes 40000 | tf_op jit(solution)/shard_map/flip/pallas_call | solution.py:237
  12.7 2.9 %collective-permute-start.6 = (bf16[2,192,384]{2,1,0:T(8,128)(2,1)S(1)}, bf16[2,192,384]{2,1,0:T(8,128)(2,1)S(1)}, u32[]{:S(2)}, u32[]{:S(2)}) collective-permute-start(bf16[2,192,384]{2,1,0:T(8,128)(2,1)S(1)} %get-tuple-element.20), channel_id=1, source_target_pairs={{1,0},{2,1},{3,2},{5,4},{6,5},{7,6},{9,8},{10,9},{11,10},{13,12},{... | collective-permute-start | bytes 884744 | tf_op jit(solution)/shard_map/ppermute | solution.py:268
  15.6 4.1 %collective-permute-start.8 = (bf16[2,192,384]{2,1,0:T(8,128)(2,1)S(1)}, bf16[2,192,384]{2,1,0:T(8,128)(2,1)S(1)}, u32[]{:S(2)}, u32[]{:S(2)}) collective-permute-start(bf16[2,192,384]{2,1,0:T(8,128)(2,1)S(1)} %get-tuple-element.20), channel_id=1, source_target_pairs={{1,4},{2,5},{3,6},{5,0},{6,1},{7,2},{9,12},{10,13},{11,14},{13,8},... | collective-permute-start | bytes 884744 | tf_op jit(solution)/shard_map/ppermute | solution.py:268
  19.7 0.1 collective-permute-start.1
  19.8 4.8 %collective-permute-start.3 = (bf16[2,192,384]{2,1,0:T(8,128)(2,1)S(1)}, bf16[2,192,384]{2,1,0:T(8,128)(2,1)S(1)}, u32[]{:S(2)}, u32[]{:S(2)}) collective-permute-start(bf16[2,192,384]{2,1,0:T(8,128)(2,1)S(1)} %collective-permute-done.2.behind_ref.ahead_ref), channel_id=1, source_target_pairs={{0,248},{4,252},{8,0},{12,4},{16,8},{20,12},{24,16},{28,20},{32,24... | collective-permute-start | bytes 884744 | tf_op jit(solution)/shard_map/ppermute | solution.py:259
  24.6 0.7 %collective-permute-start.7 = (bf16[1,192,384]{2,1,0:T(8,128)(2,1)S(1)}, bf16[1,192,384]{2,1,0:T(8,128)(2,1)S(1)}, u32[]{:S(2)}, u32[]{:S(2)}) collective-permute-start(bf16[1,192,384]{2,1,0:T(8,128)(2,1)S(1)} %get-tuple-element.19.own_ref), channel_id=1, source_target_pairs={{0,4},{1,5},{2,6},{3,7},{4,0},{5,1},{6,2},{7,3},{8,12},{9,13},{10,... | collective-permute-start | bytes 442376 | tf_op jit(solution)/shard_map/ppermute | solution.py:268
  25.3 0.7 %pad_add_fusion.facts_ref = s32[13]{0:T(128)S(1)} fusion(s32[4]{0:T(128)} %param.11, s32[9]{0:T(128)} %param.10), kind=kLoop, calls=%fused_computation | loop fusion | flops 13 | bytes 104 | tf_op jit(solution)/shard_map/concatenate | solution.py:282
  26.1 4.9 %weights.1.w_ref = bf16[9,2,384,384]{3,2,1,0:T(8,128)(2,1)S(1)} custom-call(s32[13]{0:T(128)S(1)} %pad_add_fusion.facts_ref, bf16[9,4,192,384]{3,2,1,0:T(8,128)(2,1)} %p_ref.1, bf16[2,192,384]{2,1,0:T(8,128)(2,1)S(1)} %collective-permute-done.ahead_ref.behind_ref, bf16[2,192,384]{2,1,0:T(8,128)(2,1)S(1)} %collective-permute-done.2.behind_ref.ahead_ref), custom_call_target="tpu_custom_call" | custom-call | flops 20000000 | bytes 100000 | tf_op jit(solution)/shard_map/weights/pallas_call | solution.py:79
  30.9 0.0 copy-start
  31.0 0.0 collective-permute-done.7.across_ref
  31.0 0.0 collective-permute-done.6.above_ref
  31.0 1.2 %upper_far.1 = (bf16[2,192,384]{2,1,0:T(8,128)(2,1)S(1)}, bf16[2,192,384]{2,1,0:T(8,128)(2,1)S(1)}) custom-call(s32[1]{0:T(128)} %bitcast.parity_ref, bf16[1,192,384]{2,1,0:T(8,128)(2,1)S(1)} %get-tuple-element.19.own_ref, bf16[2,192,384]{2,1,0:T(8,128)(2,1)S(1)} %collective-permute-done.6.above_ref, ...), custom_call_target="tpu_custom_call" | custom-call | flops 6794772 | bytes 40000 | tf_op jit(solution)/shard_map/upper_far/pallas_call | solution.py:237
  32.2 0.1 collective-permute-start.9
  32.3 4.8 %collective-permute-start.10 = (bf16[2,192,384]{2,1,0:T(8,128)(2,1)S(1)}, bf16[2,192,384]{2,1,0:T(8,128)(2,1)S(1)}, u32[]{:S(2)}, u32[]{:S(2)}) collective-permute-start(bf16[2,192,384]{2,1,0:T(8,128)(2,1)S(1)} %get-tuple-element.25), channel_id=1, source_target_pairs={{0,248},{4,252},{8,0},{12,4},{16,8},{20,12},{24,16},{28,20},{32,24... | collective-permute-start | bytes 884744 | tf_op jit(solution)/shard_map/ppermute | solution.py:259
  37.1 2.4 %lower_near.1.acc_ref = f32[2,2,384,384]{3,2,1,0:T(8,128)S(1)} custom-call(s32[1]{0:T(128)} %bitcast.parity_ref, bf16[2,192,384]{2,1,0:T(8,128)(2,1)S(1)} %collective-permute-done.ahead_ref.behind_ref, bf16[2,192,384]{2,1,0:T(8,128)(2,1)S(1)} %bitcast.7, bf16[2,192,384]{2,1,0:T(8,128)(2,1)S(1)} %collective-permute-done.2.behind_ref.ahead_ref, ...), custom_call_target="tpu_custom_call" | custom-call | flops 13589544 | bytes 40000 | tf_op jit(solution)/shard_map/lower_near/pallas_call | solution.py:237
  39.5 0.0 collective-permute-done.1.behind_ref
  39.5 1.3 %lower_far.1 = (f32[192,384]{1,0:T(8,128)S(1)}, f32[192,384]{1,0:T(8,128)S(1)}, bf16[4,192,384]{2,1,0:T(8,128)(2,1)S(1)}) custom-call(s32[1]{0:T(128)} %bitcast.parity_ref, bf16[2,192,384]{2,1,0:T(8,128)(2,1)S(1)} %collective-permute-done.1.behind_ref, bf16[2,192,384]{2,1,0:T(8,128)(2,1)S(1)} %collective-permute-done.3.ahead_ref, ...), custom_call_target="tpu_custom_call" | custom-call | flops 6794772 | bytes 40000 | tf_op jit(solution)/shard_map/lower_far/pallas_call | solution.py:237
  40.8 4.7 %collective-permute-start.4 = (bf16[4,192,384]{2,1,0:T(8,128)(2,1)S(1)}, bf16[4,192,384]{2,1,0:T(8,128)(2,1)S(1)}, u32[]{:S(2)}, u32[]{:S(2)}) collective-permute-start(bf16[4,192,384]{2,1,0:T(8,128)(2,1)S(1)} %get-tuple-element.16), channel_id=1, source_target_pairs={{0,1},{1,2},{2,3},{4,5},{5,6},{6,7},{8,9},{9,10},{10,11},{12,13},{... | collective-permute-start | bytes 1769480 | tf_op jit(solution)/shard_map/ppermute | solution.py:268
  45.6 2.3 %upper_near.1 = (f32[2,192,384]{2,1,0:T(8,128)S(1)}, f32[2,192,384]{2,1,0:T(8,128)S(1)}, f32[2,192,384]{2,1,0:T(8,128)S(1)}) custom-call(s32[1]{0:T(128)} %bitcast.parity_ref, bf16[1,192,384]{2,1,0:T(8,128)(2,1)S(1)} %get-tuple-element.19.own_ref, bf16[2,192,384]{2,1,0:T(8,128)(2,1)S(1)} %collective-permute-done.6.above_ref, ...), custom_call_target="tpu_custom_call" | custom-call | flops 13589544 | bytes 40000 | tf_op jit(solution)/shard_map/upper_near/pallas_call | solution.py:237
  47.9 0.1 pass.1
  48.1 0.1 collective-permute-start.11
  48.2 4.8 %collective-permute-start.12 = (bf16[2,192,384]{2,1,0:T(8,128)(2,1)S(1)}, bf16[2,192,384]{2,1,0:T(8,128)(2,1)S(1)}, u32[]{:S(2)}, u32[]{:S(2)}) collective-permute-start(bf16[2,192,384]{2,1,0:T(8,128)(2,1)S(1)} %get-tuple-element.27), channel_id=1, source_target_pairs={{0,248},{4,252},{8,0},{12,4},{16,8},{20,12},{24,16},{28,20},{32,24... | collective-permute-start | bytes 884744 | tf_op jit(solution)/shard_map/ppermute | solution.py:259
  52.9 0.1 merge.1
  53.0 2.2 %collective-permute-start.5 = (bf16[2,192,384]{2,1,0:T(8,128)(2,1)S(1)}, bf16[2,192,384]{2,1,0:T(8,128)(2,1)S(1)}, u32[]{:S(2)}, u32[]{:S(2)}) collective-permute-start(bf16[2,192,384]{2,1,0:T(8,128)(2,1)S(1)} %merge.1), channel_id=1, source_target_pairs={{0,4},{1,5},{2,6},{3,7},{4,0},{5,1},{6,2},{7,3},{8,12},{9,13},{10,... | collective-permute-start | bytes 884744 | tf_op jit(solution)/shard_map/ppermute | solution.py:268
  55.1 3.4 %collective-permute-done.11.ahead_ref = bf16[2,192,384]{2,1,0:T(8,128)(2,1)S(1)} collective-permute-done((bf16[2,192,384]{2,1,0:T(8,128)(2,1)S(1)}, bf16[2,192,384]{2,1,0:T(8,128)(2,1)S(1)}, u32[]{:S(2)}, u32[]{:S(2)}) %collective-permute-start.11) | collective-permute-done | bytes 294944 | tf_op jit(solution)/shard_map/ppermute | solution.py:259
  58.5 0.8 %total.1 = bf16[2,192,384]{2,1,0:T(8,128)(2,1)} custom-call(f32[2,192,384]{2,1,0:T(8,128)S(1)} %get-tuple-element.21.here_ref, bf16[2,192,384]{2,1,0:T(8,128)(2,1)S(1)} %collective-permute-done.11.ahead_ref, bf16[2,192,384]{2,1,0:T(8,128)(2,1)S(1)} %collective-permute-done.12.behind_ref), custom_call_target="tpu_custom_call" | custom-call | flops 10000000000 | bytes 40000 | tf_op jit(solution)/shard_map/total/pallas_call | solution.py:237
  59.3 2.8 %collective-permute-done.5.across_ref = bf16[2,192,384]{2,1,0:T(8,128)(2,1)S(1)} collective-permute-done((bf16[2,192,384]{2,1,0:T(8,128)(2,1)S(1)}, bf16[2,192,384]{2,1,0:T(8,128)(2,1)S(1)}, u32[]{:S(2)}, u32[]{:S(2)}) %collective-permute-start.5) | collective-permute-done | bytes 294944 | tf_op jit(solution)/shard_map/ppermute | solution.py:268
  62.2 1.5 %finish.1 = bf16[2,192,384]{2,1,0:T(8,128)(2,1)} custom-call(f32[192,384]{1,0:T(8,128)S(1)} %get-tuple-element.15.own_ref.after_ref, bf16[4,192,384]{2,1,0:T(8,128)(2,1)S(1)} %collective-permute-done.4.below_ref, bf16[2,192,384]{2,1,0:T(8,128)(2,1)S(1)} %collective-permute-done.5.across_ref, bf16[2,192,384]{2,1,0:T(8,128)(2,1)S(1)} %get-tuple-element.18.factor_ref), custom_call_target="tpu_custom_call" | custom-call | flops 2264924 | bytes 40000 | tf_op jit(solution)/shard_map/finish/pallas_call | solution.py:237
  (11 shorter events, 0.0 us)
Async XLA Ops:
  0.6 19.1 %collective-permute-start = (bf16[2,192,384]{2,1,0:T(8,128)(2,1)}, bf16[2,192,384]{2,1,0:T(8,128)(2,1)S(1)}, u32[]{:S(2)}, u32[]{:S(2)}) collective-permute-start(bf16[2,192,384]{2,1,0:T(8,128)(2,1)} %bitcast.5), channel_id=1, source_target_pairs={{0,8},{4,12},{8,16},{12,20},{16,24},{20,28},{24,32},{28,36},{32,40... | collective-permute-start | bytes 884744 | tf_op jit(solution)/shard_map/ppermute | solution.py:259
  3.2 16.6 %collective-permute-start.2 = (bf16[2,192,384]{2,1,0:T(8,128)(2,1)}, bf16[2,192,384]{2,1,0:T(8,128)(2,1)S(1)}, u32[]{:S(2)}, u32[]{:S(2)}) collective-permute-start(bf16[2,192,384]{2,1,0:T(8,128)(2,1)} %bitcast.6), channel_id=1, source_target_pairs={{0,248},{4,252},{8,0},{12,4},{16,8},{20,12},{24,16},{28,20},{32,24... | collective-permute-start | bytes 884744 | tf_op jit(solution)/shard_map/ppermute | solution.py:259
  9.4 1.0 %copy-start.1 = (bf16[1,2,192,384]{3,2,1,0:T(8,128)(2,1)S(1)}, bf16[1,2,192,384]{3,2,1,0:T(8,128)(2,1)}, u32[]{:S(2)}) copy-start(bf16[1,2,192,384]{3,2,1,0:T(8,128)(2,1)} %param.6) | copy-start | bytes 884740
  10.4 0.9 %copy-start.2 = (bf16[192,384]{1,0:T(8,128)(2,1)S(1)}, bf16[192,384]{1,0:T(8,128)(2,1)}, u32[]{:S(2)}) copy-start(bf16[192,384]{1,0:T(8,128)(2,1)} %c_main.1) | copy-start | bytes 442372
  12.7 18.3 %collective-permute-start.6 = (bf16[2,192,384]{2,1,0:T(8,128)(2,1)S(1)}, bf16[2,192,384]{2,1,0:T(8,128)(2,1)S(1)}, u32[]{:S(2)}, u32[]{:S(2)}) collective-permute-start(bf16[2,192,384]{2,1,0:T(8,128)(2,1)S(1)} %get-tuple-element.20), channel_id=1, source_target_pairs={{1,0},{2,1},{3,2},{5,4},{6,5},{7,6},{9,8},{10,9},{11,10},{13,12},{... | collective-permute-start | bytes 884744 | tf_op jit(solution)/shard_map/ppermute | solution.py:268
  15.6 15.4 %collective-permute-start.8 = (bf16[2,192,384]{2,1,0:T(8,128)(2,1)S(1)}, bf16[2,192,384]{2,1,0:T(8,128)(2,1)S(1)}, u32[]{:S(2)}, u32[]{:S(2)}) collective-permute-start(bf16[2,192,384]{2,1,0:T(8,128)(2,1)S(1)} %get-tuple-element.20), channel_id=1, source_target_pairs={{1,4},{2,5},{3,6},{5,0},{6,1},{7,2},{9,12},{10,13},{11,14},{13,8},... | collective-permute-start | bytes 884744 | tf_op jit(solution)/shard_map/ppermute | solution.py:268
  19.7 19.8 %collective-permute-start.1 = (bf16[2,192,384]{2,1,0:T(8,128)(2,1)S(1)}, bf16[2,192,384]{2,1,0:T(8,128)(2,1)S(1)}, u32[]{:S(2)}, u32[]{:S(2)}) collective-permute-start(bf16[2,192,384]{2,1,0:T(8,128)(2,1)S(1)} %collective-permute-done.ahead_ref.behind_ref), channel_id=1, source_target_pairs={{0,8},{4,12},{8,16},{12,20},{16,24},{20,28},{24,32},{28,36},{32,40... | collective-permute-start | bytes 884744 | tf_op jit(solution)/shard_map/ppermute | solution.py:259
  19.8 19.7 %collective-permute-start.3 = (bf16[2,192,384]{2,1,0:T(8,128)(2,1)S(1)}, bf16[2,192,384]{2,1,0:T(8,128)(2,1)S(1)}, u32[]{:S(2)}, u32[]{:S(2)}) collective-permute-start(bf16[2,192,384]{2,1,0:T(8,128)(2,1)S(1)} %collective-permute-done.2.behind_ref.ahead_ref), channel_id=1, source_target_pairs={{0,248},{4,252},{8,0},{12,4},{16,8},{20,12},{24,16},{28,20},{32,24... | collective-permute-start | bytes 884744 | tf_op jit(solution)/shard_map/ppermute | solution.py:259
  24.6 6.4 %collective-permute-start.7 = (bf16[1,192,384]{2,1,0:T(8,128)(2,1)S(1)}, bf16[1,192,384]{2,1,0:T(8,128)(2,1)S(1)}, u32[]{:S(2)}, u32[]{:S(2)}) collective-permute-start(bf16[1,192,384]{2,1,0:T(8,128)(2,1)S(1)} %get-tuple-element.19.own_ref), channel_id=1, source_target_pairs={{0,4},{1,5},{2,6},{3,7},{4,0},{5,1},{6,2},{7,3},{8,12},{9,13},{10,... | collective-permute-start | bytes 442376 | tf_op jit(solution)/shard_map/ppermute | solution.py:268
  30.9 6.2 %copy-start = (bf16[1,2,192,384]{3,2,1,0:T(8,128)(2,1)S(1)}, bf16[1,2,192,384]{3,2,1,0:T(8,128)(2,1)}, u32[]{:S(2)}) copy-start(bf16[1,2,192,384]{3,2,1,0:T(8,128)(2,1)} %param.7) | copy-start | bytes 884740
  32.2 15.7 %collective-permute-start.9 = (bf16[2,192,384]{2,1,0:T(8,128)(2,1)S(1)}, bf16[2,192,384]{2,1,0:T(8,128)(2,1)S(1)}, u32[]{:S(2)}, u32[]{:S(2)}) collective-permute-start(bf16[2,192,384]{2,1,0:T(8,128)(2,1)S(1)} %get-tuple-element.24), channel_id=1, source_target_pairs={{0,8},{4,12},{8,16},{12,20},{16,24},{20,28},{24,32},{28,36},{32,40... | collective-permute-start | bytes 884744 | tf_op jit(solution)/shard_map/ppermute | solution.py:259
  32.3 15.6 %collective-permute-start.10 = (bf16[2,192,384]{2,1,0:T(8,128)(2,1)S(1)}, bf16[2,192,384]{2,1,0:T(8,128)(2,1)S(1)}, u32[]{:S(2)}, u32[]{:S(2)}) collective-permute-start(bf16[2,192,384]{2,1,0:T(8,128)(2,1)S(1)} %get-tuple-element.25), channel_id=1, source_target_pairs={{0,248},{4,252},{8,0},{12,4},{16,8},{20,12},{24,16},{28,20},{32,24... | collective-permute-start | bytes 884744 | tf_op jit(solution)/shard_map/ppermute | solution.py:259
  40.8 12.1 %collective-permute-start.4 = (bf16[4,192,384]{2,1,0:T(8,128)(2,1)S(1)}, bf16[4,192,384]{2,1,0:T(8,128)(2,1)S(1)}, u32[]{:S(2)}, u32[]{:S(2)}) collective-permute-start(bf16[4,192,384]{2,1,0:T(8,128)(2,1)S(1)} %get-tuple-element.16), channel_id=1, source_target_pairs={{0,1},{1,2},{2,3},{4,5},{5,6},{6,7},{8,9},{9,10},{10,11},{12,13},{... | collective-permute-start | bytes 1769480 | tf_op jit(solution)/shard_map/ppermute | solution.py:268
  48.1 10.4 %collective-permute-start.11 = (bf16[2,192,384]{2,1,0:T(8,128)(2,1)S(1)}, bf16[2,192,384]{2,1,0:T(8,128)(2,1)S(1)}, u32[]{:S(2)}, u32[]{:S(2)}) collective-permute-start(bf16[2,192,384]{2,1,0:T(8,128)(2,1)S(1)} %get-tuple-element.26), channel_id=1, source_target_pairs={{0,8},{4,12},{8,16},{12,20},{16,24},{20,28},{24,32},{28,36},{32,40... | collective-permute-start | bytes 884744 | tf_op jit(solution)/shard_map/ppermute | solution.py:259
  48.2 10.4 %collective-permute-start.12 = (bf16[2,192,384]{2,1,0:T(8,128)(2,1)S(1)}, bf16[2,192,384]{2,1,0:T(8,128)(2,1)S(1)}, u32[]{:S(2)}, u32[]{:S(2)}) collective-permute-start(bf16[2,192,384]{2,1,0:T(8,128)(2,1)S(1)} %get-tuple-element.27), channel_id=1, source_target_pairs={{0,248},{4,252},{8,0},{12,4},{16,8},{20,12},{24,16},{28,20},{32,24... | collective-permute-start | bytes 884744 | tf_op jit(solution)/shard_map/ppermute | solution.py:259
  53.0 9.2 %collective-permute-start.5 = (bf16[2,192,384]{2,1,0:T(8,128)(2,1)S(1)}, bf16[2,192,384]{2,1,0:T(8,128)(2,1)S(1)}, u32[]{:S(2)}, u32[]{:S(2)}) collective-permute-start(bf16[2,192,384]{2,1,0:T(8,128)(2,1)S(1)} %merge.1), channel_id=1, source_target_pairs={{0,4},{1,5},{2,6},{3,7},{4,0},{5,1},{6,2},{7,3},{8,12},{9,13},{10,... | collective-permute-start | bytes 884744 | tf_op jit(solution)/shard_map/ppermute | solution.py:268

commit v4 on v3

--- a/solution.py
+++ b/solution.py
@@ -100,15 +100,8 @@
     return narrow(dot(half_r, factor_ref[0]) + dot(half_i, factor_ref[1]))
 
 
-def flip_kernel(x_main, c_main, out_ref, top_ref, factor_ref, x_ref, c_ref, arrived):
+def flip_kernel(x_ref, c_ref, out_ref, top_ref, factor_ref):
     count, orbitals, width = x_ref.shape
-    copies = [
-        pltpu.make_async_copy(c_main, c_ref, arrived.at[0]),
-        pltpu.make_async_copy(x_main, x_ref, arrived.at[1]),
-    ]
-    for copy in copies:
-        copy.start()
-    copies[0].wait()
     turned = c_ref[...].astype(jnp.float32).T
     c_r, c_i = narrow(turned[:orbitals]), narrow(turned[orbitals:])
     row = lax.broadcasted_iota(jnp.int32, (orbitals, width), 0)
@@ -117,7 +110,6 @@
     right = narrow(jnp.where(row + orbitals == col, 1.0, 0.0))
     factor_ref[0] = narrow(dot(c_r, left) - dot(c_i, right))
     factor_ref[1] = narrow(-dot(c_i, left) - dot(c_r, right))
-    copies[1].wait()
     for index in range(count):
         result = sandwich(x_ref[index], factor_ref)
         out_ref[index] = result
@@ -133,42 +125,44 @@
     out_ref[1] = sandwich(narrow(second), factor_ref)
 
 
+def slot_weights(w_ref, slot):
+    block = w_ref[slot]
+    return block.reshape(block.shape[0] * block.shape[1], block.shape[2])
+
+
 def flat(ref):
     block = ref[...]
     return block.reshape(block.shape[0] * block.shape[1], block.shape[2])
 
 
+def beside(blocks):
+    return jnp.concatenate(blocks, 1)
+
+
 def lower_near_kernel(parity_ref, behind_ref, own_ref, ahead_ref, w_ref, acc_ref):
-    parity = parity_ref[0]
-    for shift in range(SMAX):
-        for which in range(2):
-            total = None
-            for column, ref in ((-1, behind_ref), (0, own_ref), (1, ahead_ref)):
-                slot = MID - 2 * column
-                if which == 1:
-                    slot = jnp.where(parity == 0, slot + 1, slot - 1)
-                part = dot_t(flat(ref), w_ref[slot, shift])
-                total = part if total is None else total + part
-            acc_ref[which, shift] = total
-
-
-def lower_far_kernel(parity_ref, behind_ref, ahead_ref, w_ref, acc_ref, own_ref, other_ref, above_ref):
-    parity = parity_ref[0]
-    even = parity == 0
+    even = parity_ref[0] == 0
+    blocks = beside([flat(behind_ref), flat(own_ref), flat(ahead_ref)])
+    for which in range(2):
+        slots = [MID - 2 * column for column in (-1, 0, 1)]
+        if which == 1:
+            slots = [jnp.where(even, slot + 1, slot - 1) for slot in slots]
+        acc_ref[which] = dot_t(blocks, beside([slot_weights(w_ref, slot) for slot in slots]))
+
+
+def lower_far_kernel(parity_ref, ahead_ref, behind_ref, w_ref, acc_ref, own_ref, other_ref, above_ref):
+    even = parity_ref[0] == 0
     behind, ahead = flat(behind_ref), flat(ahead_ref)
     chosen = jnp.where(even, ahead, behind)
     slot = jnp.where(even, 1, 2 * MID - 1)
-    rows = own_ref.shape[0]
-    same = [
-        acc_ref[0, s] + dot_t(ahead, w_ref[0, s]) + dot_t(behind, w_ref[2 * MID, s])
-        for s in range(SMAX)
-    ]
-    other = [acc_ref[1, s] + dot_t(chosen, w_ref[slot, s]) for s in range(SMAX)]
-    own_ref[...] = same[0][:rows]
-    other_ref[...] = other[0][:rows]
+    rows, width = own_ref.shape
+    both = beside([slot_weights(w_ref, 0), slot_weights(w_ref, 2 * MID)])
+    same = acc_ref[0] + dot_t(beside([ahead, behind]), both)
+    other = acc_ref[1] + dot_t(chosen, slot_weights(w_ref, slot))
+    own_ref[...] = same[:rows, :width]
+    other_ref[...] = other[:rows, :width]
     for index, sums in enumerate((same, other)):
-        above_ref[2 * index] = narrow(sums[0][rows:] + sums[1][:rows])
-        above_ref[2 * index + 1] = narrow(sums[1][rows:])
+        above_ref[2 * index] = narrow(sums[rows:, :width] + sums[:rows, width:])
+        above_ref[2 * index + 1] = narrow(sums[rows:, width:])
 
 
 def merge_kernel(other_ref, below_ref, across_ref):
@@ -178,11 +172,7 @@
 
 def stack_pairs(first_ref, pair_ref):
     first = first_ref[first_ref.shape[0] - 1]
-    return jnp.concatenate([first, pair_ref[0]], 0), flat(pair_ref)
-
-
-def upper_dot(pairs, w_ref, slot):
-    return dot(pairs[0], w_ref[slot, 0]) + dot(pairs[1], w_ref[slot, 1])
+    return [jnp.concatenate([first, pair_ref[0]], 0), flat(pair_ref)]
 
 
 def store(ref, rows, kind=None):
@@ -194,52 +184,51 @@
 
 def upper_far_kernel(parity_ref, own_ref, above_ref, across_ref, diagonal_ref, w_ref, ahead_ref, behind_ref):
     even = parity_ref[0] == 0
-    same = stack_pairs(own_ref, above_ref)
-    other = stack_pairs(across_ref, diagonal_ref)
-    extra = upper_dot(other, w_ref, jnp.where(even, 1, 2 * MID - 1))
-    ahead = upper_dot(same, w_ref, 0) + jnp.where(even, extra, 0.0)
-    behind = upper_dot(same, w_ref, 2 * MID) + jnp.where(even, 0.0, extra)
-    store(ahead_ref, ahead, jnp.bfloat16)
-    store(behind_ref, behind, jnp.bfloat16)
+    width = w_ref.shape[-1]
+    same = beside(stack_pairs(own_ref, above_ref))
+    other = beside(stack_pairs(across_ref, diagonal_ref))
+    extra = dot(other, slot_weights(w_ref, jnp.where(even, 1, 2 * MID - 1)))
+    sums = dot(same, beside([slot_weights(w_ref, 0), slot_weights(w_ref, 2 * MID)]))
+    store(ahead_ref, sums[:, :width] + jnp.where(even, extra, 0.0), jnp.bfloat16)
+    store(behind_ref, sums[:, width:] + jnp.where(even, 0.0, extra), jnp.bfloat16)
 
 
 def upper_near_kernel(
     parity_ref, own_ref, above_ref, across_ref, diagonal_ref, w_ref, after_ref, ahead_ref, behind_ref, here_ref
 ):
-    parity = parity_ref[0]
-    same = stack_pairs(own_ref, above_ref)
-    other = stack_pairs(across_ref, diagonal_ref)
-    for column, ref in ((1, ahead_ref), (-1, behind_ref), (0, here_ref)):
-        slot = MID - 2 * column
-        total = upper_dot(same, w_ref, slot) + upper_dot(other, w_ref, jnp.where(parity == 0, slot + 1, slot - 1))
-        store(ref, total)
-
-
-def pass_kernel(near_ahead, near_behind, ahead_ref, behind_ref, ahead_out, behind_out):
+    even = parity_ref[0] == 0
+    width = w_ref.shape[-1]
+    blocks = beside(stack_pairs(own_ref, above_ref) + stack_pairs(across_ref, diagonal_ref))
+    same = [MID - 2 * column for column in (1, -1, 0)]
+    other = [jnp.where(even, slot + 1, slot - 1) for slot in same]
+    weights = jnp.concatenate(
+        [beside([slot_weights(w_ref, slot) for slot in slots]) for slots in (same, other)], 0
+    )
+    sums = dot(blocks, weights)
+    for index, ref in enumerate((ahead_ref, behind_ref, here_ref)):
+        store(ref, sums[:, index * width : (index + 1) * width])
+
+
+def pass_kernel(near_ahead, near_behind, ahead_ref, behind_ref, behind_out, ahead_out):
     ahead_out[...] = narrow(near_ahead[...] + ahead_ref[...].astype(jnp.float32))
     behind_out[...] = narrow(near_behind[...] + behind_ref[...].astype(jnp.float32))
 
 
-def total_kernel(here_ref, ahead_ref, behind_ref, out_ref):
+def total_kernel(here_ref, behind_ref, ahead_ref, out_ref):
     arrived = ahead_ref[...].astype(jnp.float32) + behind_ref[...].astype(jnp.float32)
     out_ref[...] = narrow(here_ref[...] + arrived)
 
 
-def call(kernel, name, outs, args, flops, has_scalar=False, after=(), fetched=False):
+def call(kernel, name, outs, args, flops, has_scalar=False, after=()):
     specs = [resident() for _ in args] + [pl.BlockSpec(memory_space=pl.ANY) for _ in after]
     if has_scalar:
         specs[0] = scalar()
-    scratch = []
-    if fetched:
-        specs = [pl.BlockSpec(memory_space=pltpu.HBM) for _ in args]
-        scratch = [pltpu.VMEM(a.shape, a.dtype) for a in args] + [pltpu.SemaphoreType.DMA((len(args),))]
     nbytes = 4 * 10**6
     return pl.pallas_call(
         kernel,
         out_shape=[jax.ShapeDtypeStruct(s, d) for s, d in outs],
         in_specs=specs,
         out_specs=[resident() for _ in outs],
-        scratch_shapes=scratch,
         compiler_params=params(),
         cost_estimate=cost(flops, nbytes),
         name=name,
@@ -274,26 +263,26 @@
     g_own = greater[0]
     g_near = [column(g_own, 1), column(g_own, -1)]
     flipped, top, factors = call(
-        flip_kernel, "flip", [(pair, bf16), (one, bf16), (pair, bf16)], [lesser[0], coupling], 2 * big, fetched=True
+        flip_kernel, "flip", [(pair, bf16), (one, bf16), (pair, bf16)], [lesser[0], coupling], 2 * big
     )
     above = crossed(flipped, -1, False)
     diagonal = crossed(flipped, -1, True)
     across = crossed(top, 0, True)
     weights = make_weights(jnp.concatenate([offsets, mode_shift]), cotangent, g_near)
-    g_far = [column(g_near[0], 1), column(g_near[1], -1)]
+    g_far = [column(g_near[1], -1), column(g_near[0], 1)][::-1]
 
     upper = [parity, top, above, across, diagonal, weights]
     ahead, behind = call(upper_far_kernel, "upper_far", [(pair, bf16)] * 2, upper, 6 * big, True)
     ahead, behind = column(ahead, 1), column(behind, -1)
 
     (acc,) = call(
-        lower_near_kernel, "lower_near", [((2, SMAX, count * orbitals, width), f32)],
+        lower_near_kernel, "lower_near", [((2, count * orbitals, SMAX * width), f32)],
         [parity, g_near[0], g_own, g_near[1], weights], 12 * big, True,
     )
     own, other, to_above = call(
         lower_far_kernel, "lower_far",
         [((orbitals, width), f32), ((orbitals, width), f32), ((2 * count, orbitals, width), bf16)],
-        [parity, g_far[0], g_far[1], weights, acc], 6 * big, True,
+        [parity, g_far[1], g_far[0], weights, acc], 6 * big, True,
     )
     near_ahead, near_behind, here = call(
         upper_near_kernel, "upper_near", [(pair, f32)] * 3, upper, 12 * big, True, [own]
@@ -302,13 +291,13 @@
     (to_across,) = call(merge_kernel, "merge", [(pair, bf16)], [other, from_below], 10**6)
     from_across = crossed(to_across, 0, True)
 
-    ahead, behind = call(pass_kernel, "pass", [(pair, bf16)] * 2, [near_ahead, near_behind, ahead, behind], 10**6)
-    ahead, behind = column(ahead, 1), column(behind, -1)
+    behind, ahead = call(pass_kernel, "pass", [(pair, bf16)] * 2, [near_ahead, near_behind, ahead, behind], 10**6)
+    behind, ahead = column(behind, -1), column(ahead, 1)
     (grad_lesser,) = call(
         finish_kernel, "finish", [(pair, bf16)],
         [own, from_below, from_across, factors], 2 * big,
     )
-    (grad_greater,) = call(total_kernel, "total", [(pair, bf16)], [here, ahead, behind], TAIL)
+    (grad_greater,) = call(total_kernel, "total", [(pair, bf16)], [here, behind, ahead], TAIL)
     return (grad_lesser[None], grad_greater[None])
 
 

time: 63.9 us -> 62.7 us (0.981)
  waiting for transfers between devices: 6.24 us -> 9.86 us
  starting transfers between devices: 37.9 us -> 35.4 us
  Pallas kernels: 16.1 us -> 13.8 us
    pallas_call x9, Pallas kernels: 11.2 us -> 8.95 us  [call(): pl.pallas_call(kernel, out_shape=[jax.ShapeDtypeStruct(s, d) for s, d in...]
    ppermute x8, starting transfers between devices: 23.3 us -> 21.1 us  [column(): return lax.ppermute(block, 'ka', route)]
    ppermute x5, waiting for transfers between devices: 2.85 us -> 5.08 us  [crossed(): return lax.ppermute(block, both, route)]
    ppermute x8, waiting for transfers between devices: 3.38 us -> 4.78 us  [column(): return lax.ppermute(block, 'ka', route)]
  transfers between devices with their start and end apart: 13 -> 13, of which waited for: 2 -> 4; matrix products, arithmetic and copies ran while one was open for 1% -> 1% of each run, Pallas kernels for 23% -> 20%
where the time goes in v4:
time: 62.7 us; the launch traced here: 62.5 us
  starting transfers between devices  35.4 us (56%)
  Pallas kernels  13.8 us (22%)
  waiting for transfers between devices  9.86 us (16%)
  local copies, waits for them, and re-layouts  1.88 us (3%)
  between operations  0.8 us (1%)
  other arithmetic  0.75 us (1%)
    ppermute x8, starting transfers between devices, column(): return lax.ppermute(block, 'ka', route)  21.1 us
    ppermute x5, starting transfers between devices, crossed(): return lax.ppermute(block, both, route)  14.3 us
    pallas_call x9, Pallas kernels, call(): pl.pallas_call(kernel, out_shape=[jax.ShapeDtypeStruct(s, d) for s, d in...  8.95 us
    ppermute x5, waiting for transfers between devices, crossed(): return lax.ppermute(block, both, route)  5.08 us
    pallas_call x1, Pallas kernels, make_weights(): pl.pallas_call(weights_kernel, out_shape=jax.ShapeDtypeStruct((slots, SMA...  4.87 us
    ppermute x8, waiting for transfers between devices, column(): return lax.ppermute(block, 'ka', route)  4.78 us
    unnamed x6, local copies, waits for them, and re-layouts  1.88 us
  transfers between devices with their start and end apart: 13, of which 4 were waited for; matrix products, arithmetic and copies ran while one was open for 1% of the time, Pallas kernels for 20%

profile of v4, /device:TPU:1, one launch (start us, length us, event | category | flops | bytes accessed | tf_op | source)
XLA Modules:
  0.0 62.5 jit_solution(1438251454650574839)
XLA Ops:
  0.6 8.7 %collective-permute-start = (bf16[2,192,384]{2,1,0:T(8,128)(2,1)}, bf16[2,192,384]{2,1,0:T(8,128)(2,1)S(1)}, u32[]{:S(2)}, u32[]{:S(2)}) collective-permute-start(bf16[2,192,384]{2,1,0:T(8,128)(2,1)} %bitcast.5), channel_id=1, source_target_pairs={{0,248},{4,252},{8,0},{12,4},{16,8},{20,12},{24,16},{28,20},{32,24... | collective-permute-start | bytes 884744 | tf_op jit(solution)/shard_map/ppermute | solution.py:248
  9.3 0.0 collective-permute-start.2
  9.3 1.0 %copy-done.1 = bf16[1,2,192,384]{3,2,1,0:T(8,128)(2,1)S(1)} copy-done((bf16[1,2,192,384]{3,2,1,0:T(8,128)(2,1)S(1)}, bf16[1,2,192,384]{3,2,1,0:T(8,128)(2,1)}, u32[]{:S(2)}) %copy-start.1) | copy-done | bytes 294936
  10.3 0.9 %copy-done.2 = bf16[192,384]{1,0:T(8,128)(2,1)S(1)} copy-done((bf16[192,384]{1,0:T(8,128)(2,1)S(1)}, bf16[192,384]{1,0:T(8,128)(2,1)}, u32[]{:S(2)}) %copy-start.2) | copy-done | bytes 147480
  11.2 1.1 %flip.1 = (bf16[2,192,384]{2,1,0:T(8,128)(2,1)S(1)}, bf16[1,192,384]{2,1,0:T(8,128)(2,1)S(1)}, bf16[2,192,384]{2,1,0:T(8,128)(2,1)S(1)}) custom-call(bf16[2,192,384]{2,1,0:T(8,128)(2,1)S(1)} %bitcast.8, bf16[192,384]{1,0:T(8,128)(2,1)S(1)} %copy-done.2), custom_call_target="tpu_custom_call" | custom-call | flops 2264924 | bytes 40000 | tf_op jit(solution)/shard_map/flip/pallas_call | solution.py:227
  12.3 2.9 %collective-permute-start.6 = (bf16[2,192,384]{2,1,0:T(8,128)(2,1)S(1)}, bf16[2,192,384]{2,1,0:T(8,128)(2,1)S(1)}, u32[]{:S(2)}, u32[]{:S(2)}) collective-permute-start(bf16[2,192,384]{2,1,0:T(8,128)(2,1)S(1)} %get-tuple-element.20), channel_id=1, source_target_pairs={{1,0},{2,1},{3,2},{5,4},{6,5},{7,6},{9,8},{10,9},{11,10},{13,12},{... | collective-permute-start | bytes 884744 | tf_op jit(solution)/shard_map/ppermute | solution.py:257
  15.1 4.1 %collective-permute-start.8 = (bf16[2,192,384]{2,1,0:T(8,128)(2,1)S(1)}, bf16[2,192,384]{2,1,0:T(8,128)(2,1)S(1)}, u32[]{:S(2)}, u32[]{:S(2)}) collective-permute-start(bf16[2,192,384]{2,1,0:T(8,128)(2,1)S(1)} %get-tuple-element.20), channel_id=1, source_target_pairs={{1,4},{2,5},{3,6},{5,0},{6,1},{7,2},{9,12},{10,13},{11,14},{13,8},... | collective-permute-start | bytes 884744 | tf_op jit(solution)/shard_map/ppermute | solution.py:257
  19.3 5.1 %collective-permute-start.1 = (bf16[2,192,384]{2,1,0:T(8,128)(2,1)S(1)}, bf16[2,192,384]{2,1,0:T(8,128)(2,1)S(1)}, u32[]{:S(2)}, u32[]{:S(2)}) collective-permute-start(bf16[2,192,384]{2,1,0:T(8,128)(2,1)S(1)} %collective-permute-done.behind_ref.ahead_ref), channel_id=1, source_target_pairs={{0,248},{4,252},{8,0},{12,4},{16,8},{20,12},{24,16},{28,20},{32,24... | collective-permute-start | bytes 884744 | tf_op jit(solution)/shard_map/ppermute | solution.py:248
  24.4 0.0 collective-permute-done.2.ahead_ref.behind_ref
  24.4 0.0 collective-permute-start.3
  24.4 0.7 %collective-permute-start.7 = (bf16[1,192,384]{2,1,0:T(8,128)(2,1)S(1)}, bf16[1,192,384]{2,1,0:T(8,128)(2,1)S(1)}, u32[]{:S(2)}, u32[]{:S(2)}) collective-permute-start(bf16[1,192,384]{2,1,0:T(8,128)(2,1)S(1)} %get-tuple-element.19.own_ref), channel_id=1, source_target_pairs={{0,4},{1,5},{2,6},{3,7},{4,0},{5,1},{6,2},{7,3},{8,12},{9,13},{10,... | collective-permute-start | bytes 442376 | tf_op jit(solution)/shard_map/ppermute | solution.py:257
  25.1 0.7 %pad_add_fusion.facts_ref = s32[13]{0:T(128)S(1)} fusion(s32[4]{0:T(128)} %param.11, s32[9]{0:T(128)} %param.10), kind=kLoop, calls=%fused_computation | loop fusion | flops 13 | bytes 104 | tf_op jit(solution)/shard_map/concatenate | solution.py:271
  25.9 4.9 %weights.1.w_ref = bf16[9,2,384,384]{3,2,1,0:T(8,128)(2,1)S(1)} custom-call(s32[13]{0:T(128)S(1)} %pad_add_fusion.facts_ref, bf16[9,4,192,384]{3,2,1,0:T(8,128)(2,1)} %p_ref.1, bf16[2,192,384]{2,1,0:T(8,128)(2,1)S(1)} %collective-permute-done.2.ahead_ref.behind_ref, bf16[2,192,384]{2,1,0:T(8,128)(2,1)S(1)} %collective-permute-done.behind_ref.ahead_ref), custom_call_target="tpu_custom_call" | custom-call | flops 20000000 | bytes 100000 | tf_op jit(solution)/shard_map/weights/pallas_call | solution.py:79
  30.8 0.0 copy-start
  30.8 0.0 collective-permute-done.7.across_ref
  30.8 0.9 %upper_far.1 = (bf16[2,192,384]{2,1,0:T(8,128)(2,1)S(1)}, bf16[2,192,384]{2,1,0:T(8,128)(2,1)S(1)}) custom-call(s32[1]{0:T(128)} %bitcast.parity_ref, bf16[1,192,384]{2,1,0:T(8,128)(2,1)S(1)} %get-tuple-element.19.own_ref, bf16[2,192,384]{2,1,0:T(8,128)(2,1)S(1)} %collective-permute-done.6.above_ref, ...), custom_call_target="tpu_custom_call" | custom-call | flops 6794772 | bytes 40000 | tf_op jit(solution)/shard_map/upper_far/pallas_call | solution.py:227
  31.8 0.1 collective-permute-start.9
  31.9 5.0 %collective-permute-start.10 = (bf16[2,192,384]{2,1,0:T(8,128)(2,1)S(1)}, bf16[2,192,384]{2,1,0:T(8,128)(2,1)S(1)}, u32[]{:S(2)}, u32[]{:S(2)}) collective-permute-start(bf16[2,192,384]{2,1,0:T(8,128)(2,1)S(1)} %get-tuple-element.25), channel_id=1, source_target_pairs={{0,248},{4,252},{8,0},{12,4},{16,8},{20,12},{24,16},{28,20},{32,24... | collective-permute-start | bytes 884744 | tf_op jit(solution)/shard_map/ppermute | solution.py:248
  36.9 1.7 %lower_near.1.acc_ref = f32[2,384,768]{2,1,0:T(8,128)S(1)} custom-call(s32[1]{0:T(128)} %bitcast.parity_ref, bf16[2,192,384]{2,1,0:T(8,128)(2,1)S(1)} %collective-permute-done.2.ahead_ref.behind_ref, bf16[2,192,384]{2,1,0:T(8,128)(2,1)S(1)} %bitcast.7, bf16[2,192,384]{2,1,0:T(8,128)(2,1)S(1)} %collective-permute-done.behind_ref.ahead_ref, ...), custom_call_target="tpu_custom_call" | custom-call | flops 13589544 | bytes 40000 | tf_op jit(solution)/shard_map/lower_near/pallas_call | solution.py:227
  38.7 1.0 %lower_far.1 = (f32[192,384]{1,0:T(8,128)S(1)}, f32[192,384]{1,0:T(8,128)S(1)}, bf16[4,192,384]{2,1,0:T(8,128)(2,1)S(1)}) custom-call(s32[1]{0:T(128)} %bitcast.parity_ref, bf16[2,192,384]{2,1,0:T(8,128)(2,1)S(1)} %collective-permute-done.1.ahead_ref, bf16[2,192,384]{2,1,0:T(8,128)(2,1)S(1)} %collective-permute-done.3.behind_ref, ...), custom_call_target="tpu_custom_call" | custom-call | flops 6794772 | bytes 40000 | tf_op jit(solution)/shard_map/lower_far/pallas_call | solution.py:227
  39.6 4.5 %collective-permute-start.4 = (bf16[4,192,384]{2,1,0:T(8,128)(2,1)S(1)}, bf16[4,192,384]{2,1,0:T(8,128)(2,1)S(1)}, u32[]{:S(2)}, u32[]{:S(2)}) collective-permute-start(bf16[4,192,384]{2,1,0:T(8,128)(2,1)S(1)} %get-tuple-element.16), channel_id=1, source_target_pairs={{0,1},{1,2},{2,3},{4,5},{5,6},{6,7},{8,9},{9,10},{10,11},{12,13},{... | collective-permute-start | bytes 1769480 | tf_op jit(solution)/shard_map/ppermute | solution.py:257
  44.1 1.7 %upper_near.1 = (f32[2,192,384]{2,1,0:T(8,128)S(1)}, f32[2,192,384]{2,1,0:T(8,128)S(1)}, f32[2,192,384]{2,1,0:T(8,128)S(1)}) custom-call(s32[1]{0:T(128)} %bitcast.parity_ref, bf16[1,192,384]{2,1,0:T(8,128)(2,1)S(1)} %get-tuple-element.19.own_ref, bf16[2,192,384]{2,1,0:T(8,128)(2,1)S(1)} %collective-permute-done.6.above_ref, ...), custom_call_target="tpu_custom_call" | custom-call | flops 13589544 | bytes 40000 | tf_op jit(solution)/shard_map/upper_near/pallas_call | solution.py:227
  45.9 0.1 pass.1
  46.0 2.1 %collective-permute-start.11 = (bf16[2,192,384]{2,1,0:T(8,128)(2,1)S(1)}, bf16[2,192,384]{2,1,0:T(8,128)(2,1)S(1)}, u32[]{:S(2)}, u32[]{:S(2)}) collective-permute-start(bf16[2,192,384]{2,1,0:T(8,128)(2,1)S(1)} %get-tuple-element.26), channel_id=1, source_target_pairs={{0,248},{4,252},{8,0},{12,4},{16,8},{20,12},{24,16},{28,20},{32,24... | collective-permute-start | bytes 884744 | tf_op jit(solution)/shard_map/ppermute | solution.py:248
  48.1 2.8 %collective-permute-done.4.below_ref = bf16[4,192,384]{2,1,0:T(8,128)(2,1)S(1)} collective-permute-done((bf16[4,192,384]{2,1,0:T(8,128)(2,1)S(1)}, bf16[4,192,384]{2,1,0:T(8,128)(2,1)S(1)}, u32[]{:S(2)}, u32[]{:S(2)}) %collective-permute-start.4) | collective-permute-done | bytes 589856 | tf_op jit(solution)/shard_map/ppermute | solution.py:257
  50.9 0.1 merge.1
  51.0 2.2 %collective-permute-start.5 = (bf16[2,192,384]{2,1,0:T(8,128)(2,1)S(1)}, bf16[2,192,384]{2,1,0:T(8,128)(2,1)S(1)}, u32[]{:S(2)}, u32[]{:S(2)}) collective-permute-start(bf16[2,192,384]{2,1,0:T(8,128)(2,1)S(1)} %merge.1), channel_id=1, source_target_pairs={{0,4},{1,5},{2,6},{3,7},{4,0},{5,1},{6,2},{7,3},{8,12},{9,13},{10,... | collective-permute-start | bytes 884744 | tf_op jit(solution)/shard_map/ppermute | solution.py:257
  53.1 0.9 %collective-permute-done.11.behind_ref = bf16[2,192,384]{2,1,0:T(8,128)(2,1)S(1)} collective-permute-done((bf16[2,192,384]{2,1,0:T(8,128)(2,1)S(1)}, bf16[2,192,384]{2,1,0:T(8,128)(2,1)S(1)}, u32[]{:S(2)}, u32[]{:S(2)}) %collective-permute-start.11) | collective-permute-done | bytes 294944 | tf_op jit(solution)/shard_map/ppermute | solution.py:248
  54.0 3.9 %collective-permute-done.12.ahead_ref = bf16[2,192,384]{2,1,0:T(8,128)(2,1)S(1)} collective-permute-done((bf16[2,192,384]{2,1,0:T(8,128)(2,1)S(1)}, bf16[2,192,384]{2,1,0:T(8,128)(2,1)S(1)}, u32[]{:S(2)}, u32[]{:S(2)}) %collective-permute-start.12) | collective-permute-done | bytes 294944 | tf_op jit(solution)/shard_map/ppermute | solution.py:248
  57.9 0.8 %total.1 = bf16[2,192,384]{2,1,0:T(8,128)(2,1)} custom-call(f32[2,192,384]{2,1,0:T(8,128)S(1)} %get-tuple-element.21.here_ref, bf16[2,192,384]{2,1,0:T(8,128)(2,1)S(1)} %collective-permute-done.11.behind_ref, bf16[2,192,384]{2,1,0:T(8,128)(2,1)S(1)} %collective-permute-done.12.ahead_ref), custom_call_target="tpu_custom_call" | custom-call | flops 10000000000 | bytes 40000 | tf_op jit(solution)/shard_map/total/pallas_call | solution.py:227
  58.7 2.3 %collective-permute-done.5.across_ref = bf16[2,192,384]{2,1,0:T(8,128)(2,1)S(1)} collective-permute-done((bf16[2,192,384]{2,1,0:T(8,128)(2,1)S(1)}, bf16[2,192,384]{2,1,0:T(8,128)(2,1)S(1)}, u32[]{:S(2)}, u32[]{:S(2)}) %collective-permute-start.5) | collective-permute-done | bytes 294944 | tf_op jit(solution)/shard_map/ppermute | solution.py:257
  61.0 1.5 %finish.1 = bf16[2,192,384]{2,1,0:T(8,128)(2,1)} custom-call(f32[192,384]{1,0:T(8,128)S(1)} %get-tuple-element.15.own_ref.after_ref, bf16[4,192,384]{2,1,0:T(8,128)(2,1)S(1)} %collective-permute-done.4.below_ref, bf16[2,192,384]{2,1,0:T(8,128)(2,1)S(1)} %collective-permute-done.5.across_ref, bf16[2,192,384]{2,1,0:T(8,128)(2,1)S(1)} %get-tuple-element.18.factor_ref), custom_call_target="tpu_custom_call" | custom-call | flops 2264924 | bytes 40000 | tf_op jit(solution)/shard_map/finish/pallas_call | solution.py:227
  (11 shorter events, 0.0 us)
Async XLA Ops:
  0.6 18.6 %collective-permute-start = (bf16[2,192,384]{2,1,0:T(8,128)(2,1)}, bf16[2,192,384]{2,1,0:T(8,128)(2,1)S(1)}, u32[]{:S(2)}, u32[]{:S(2)}) collective-permute-start(bf16[2,192,384]{2,1,0:T(8,128)(2,1)} %bitcast.5), channel_id=1, source_target_pairs={{0,248},{4,252},{8,0},{12,4},{16,8},{20,12},{24,16},{28,20},{32,24... | collective-permute-start | bytes 884744 | tf_op jit(solution)/shard_map/ppermute | solution.py:248
  9.3 15.1 %collective-permute-start.2 = (bf16[2,192,384]{2,1,0:T(8,128)(2,1)}, bf16[2,192,384]{2,1,0:T(8,128)(2,1)S(1)}, u32[]{:S(2)}, u32[]{:S(2)}) collective-permute-start(bf16[2,192,384]{2,1,0:T(8,128)(2,1)} %bitcast.6), channel_id=1, source_target_pairs={{0,8},{4,12},{8,16},{12,20},{16,24},{20,28},{24,32},{28,36},{32,40... | collective-permute-start | bytes 884744 | tf_op jit(solution)/shard_map/ppermute | solution.py:248
  9.3 1.0 %copy-start.1 = (bf16[1,2,192,384]{3,2,1,0:T(8,128)(2,1)S(1)}, bf16[1,2,192,384]{3,2,1,0:T(8,128)(2,1)}, u32[]{:S(2)}) copy-start(bf16[1,2,192,384]{3,2,1,0:T(8,128)(2,1)} %param.6) | copy-start | bytes 884740
  10.3 0.9 %copy-start.2 = (bf16[192,384]{1,0:T(8,128)(2,1)S(1)}, bf16[192,384]{1,0:T(8,128)(2,1)}, u32[]{:S(2)}) copy-start(bf16[192,384]{1,0:T(8,128)(2,1)} %c_ref.1) | copy-start | bytes 442372
  12.3 18.5 %collective-permute-start.6 = (bf16[2,192,384]{2,1,0:T(8,128)(2,1)S(1)}, bf16[2,192,384]{2,1,0:T(8,128)(2,1)S(1)}, u32[]{:S(2)}, u32[]{:S(2)}) collective-permute-start(bf16[2,192,384]{2,1,0:T(8,128)(2,1)S(1)} %get-tuple-element.20), channel_id=1, source_target_pairs={{1,0},{2,1},{3,2},{5,4},{6,5},{7,6},{9,8},{10,9},{11,10},{13,12},{... | collective-permute-start | bytes 884744 | tf_op jit(solution)/shard_map/ppermute | solution.py:257
  15.1 15.7 %collective-permute-start.8 = (bf16[2,192,384]{2,1,0:T(8,128)(2,1)S(1)}, bf16[2,192,384]{2,1,0:T(8,128)(2,1)S(1)}, u32[]{:S(2)}, u32[]{:S(2)}) collective-permute-start(bf16[2,192,384]{2,1,0:T(8,128)(2,1)S(1)} %get-tuple-element.20), channel_id=1, source_target_pairs={{1,4},{2,5},{3,6},{5,0},{6,1},{7,2},{9,12},{10,13},{11,14},{13,8},... | collective-permute-start | bytes 884744 | tf_op jit(solution)/shard_map/ppermute | solution.py:257
  19.3 19.4 %collective-permute-start.1 = (bf16[2,192,384]{2,1,0:T(8,128)(2,1)S(1)}, bf16[2,192,384]{2,1,0:T(8,128)(2,1)S(1)}, u32[]{:S(2)}, u32[]{:S(2)}) collective-permute-start(bf16[2,192,384]{2,1,0:T(8,128)(2,1)S(1)} %collective-permute-done.behind_ref.ahead_ref), channel_id=1, source_target_pairs={{0,248},{4,252},{8,0},{12,4},{16,8},{20,12},{24,16},{28,20},{32,24... | collective-permute-start | bytes 884744 | tf_op jit(solution)/shard_map/ppermute | solution.py:248
  24.4 14.2 %collective-permute-start.3 = (bf16[2,192,384]{2,1,0:T(8,128)(2,1)S(1)}, bf16[2,192,384]{2,1,0:T(8,128)(2,1)S(1)}, u32[]{:S(2)}, u32[]{:S(2)}) collective-permute-start(bf16[2,192,384]{2,1,0:T(8,128)(2,1)S(1)} %collective-permute-done.2.ahead_ref.behind_ref), channel_id=1, source_target_pairs={{0,8},{4,12},{8,16},{12,20},{16,24},{20,28},{24,32},{28,36},{32,40... | collective-permute-start | bytes 884744 | tf_op jit(solution)/shard_map/ppermute | solution.py:248
  24.4 6.4 %collective-permute-start.7 = (bf16[1,192,384]{2,1,0:T(8,128)(2,1)S(1)}, bf16[1,192,384]{2,1,0:T(8,128)(2,1)S(1)}, u32[]{:S(2)}, u32[]{:S(2)}) collective-permute-start(bf16[1,192,384]{2,1,0:T(8,128)(2,1)S(1)} %get-tuple-element.19.own_ref), channel_id=1, source_target_pairs={{0,4},{1,5},{2,6},{3,7},{4,0},{5,1},{6,2},{7,3},{8,12},{9,13},{10,... | collective-permute-start | bytes 442376 | tf_op jit(solution)/shard_map/ppermute | solution.py:257
  30.8 6.1 %copy-start = (bf16[1,2,192,384]{3,2,1,0:T(8,128)(2,1)S(1)}, bf16[1,2,192,384]{3,2,1,0:T(8,128)(2,1)}, u32[]{:S(2)}) copy-start(bf16[1,2,192,384]{3,2,1,0:T(8,128)(2,1)} %param.7) | copy-start | bytes 884740
  31.8 14.1 %collective-permute-start.9 = (bf16[2,192,384]{2,1,0:T(8,128)(2,1)S(1)}, bf16[2,192,384]{2,1,0:T(8,128)(2,1)S(1)}, u32[]{:S(2)}, u32[]{:S(2)}) collective-permute-start(bf16[2,192,384]{2,1,0:T(8,128)(2,1)S(1)} %get-tuple-element.24), channel_id=1, source_target_pairs={{0,8},{4,12},{8,16},{12,20},{16,24},{20,28},{24,32},{28,36},{32,40... | collective-permute-start | bytes 884744 | tf_op jit(solution)/shard_map/ppermute | solution.py:248
  31.9 14.0 %collective-permute-start.10 = (bf16[2,192,384]{2,1,0:T(8,128)(2,1)S(1)}, bf16[2,192,384]{2,1,0:T(8,128)(2,1)S(1)}, u32[]{:S(2)}, u32[]{:S(2)}) collective-permute-start(bf16[2,192,384]{2,1,0:T(8,128)(2,1)S(1)} %get-tuple-element.25), channel_id=1, source_target_pairs={{0,248},{4,252},{8,0},{12,4},{16,8},{20,12},{24,16},{28,20},{32,24... | collective-permute-start | bytes 884744 | tf_op jit(solution)/shard_map/ppermute | solution.py:248
  39.6 11.3 %collective-permute-start.4 = (bf16[4,192,384]{2,1,0:T(8,128)(2,1)S(1)}, bf16[4,192,384]{2,1,0:T(8,128)(2,1)S(1)}, u32[]{:S(2)}, u32[]{:S(2)}) collective-permute-start(bf16[4,192,384]{2,1,0:T(8,128)(2,1)S(1)} %get-tuple-element.16), channel_id=1, source_target_pairs={{0,1},{1,2},{2,3},{4,5},{5,6},{6,7},{8,9},{9,10},{10,11},{12,13},{... | collective-permute-start | bytes 1769480 | tf_op jit(solution)/shard_map/ppermute | solution.py:257
  46.0 8.0 %collective-permute-start.11 = (bf16[2,192,384]{2,1,0:T(8,128)(2,1)S(1)}, bf16[2,192,384]{2,1,0:T(8,128)(2,1)S(1)}, u32[]{:S(2)}, u32[]{:S(2)}) collective-permute-start(bf16[2,192,384]{2,1,0:T(8,128)(2,1)S(1)} %get-tuple-element.26), channel_id=1, source_target_pairs={{0,248},{4,252},{8,0},{12,4},{16,8},{20,12},{24,16},{28,20},{32,24... | collective-permute-start | bytes 884744 | tf_op jit(solution)/shard_map/ppermute | solution.py:248
  48.1 9.8 %collective-permute-start.12 = (bf16[2,192,384]{2,1,0:T(8,128)(2,1)S(1)}, bf16[2,192,384]{2,1,0:T(8,128)(2,1)S(1)}, u32[]{:S(2)}, u32[]{:S(2)}) collective-permute-start(bf16[2,192,384]{2,1,0:T(8,128)(2,1)S(1)} %get-tuple-element.27), channel_id=1, source_target_pairs={{0,8},{4,12},{8,16},{12,20},{16,24},{20,28},{24,32},{28,36},{32,40... | collective-permute-start | bytes 884744 | tf_op jit(solution)/shard_map/ppermute | solution.py:248
  51.0 10.0 %collective-permute-start.5 = (bf16[2,192,384]{2,1,0:T(8,128)(2,1)S(1)}, bf16[2,192,384]{2,1,0:T(8,128)(2,1)S(1)}, u32[]{:S(2)}, u32[]{:S(2)}) collective-permute-start(bf16[2,192,384]{2,1,0:T(8,128)(2,1)S(1)} %merge.1), channel_id=1, source_target_pairs={{0,4},{1,5},{2,6},{3,7},{4,0},{5,1},{6,2},{7,3},{8,12},{9,13},{10,... | collective-permute-start | bytes 884744 | tf_op jit(solution)/shard_map/ppermute | solution.py:257

commit v5 on v4

--- a/solution.py
+++ b/solution.py
@@ -45,7 +45,7 @@
 
 
 def weights_kernel(
-    facts_ref, p_ref, ahead_ref, behind_ref, w_ref, held_ref, turn_ref, facts, arrived, known
+    facts_ref, p_ref, ahead_ref, behind_ref, w_ref, held_ref, turn_ref, facts, order, arrived, known
 ):
     slots, modes, orbitals, width = p_ref.shape
     fetch = pltpu.make_async_copy(facts_ref, facts, known)
@@ -58,18 +58,40 @@
     turn = jnp.where(row == col + orbitals, -1.0, jnp.where(row + orbitals == col, 1.0, 0.0))
     turn_ref[...] = narrow(turn)
     fetch.wait()
-    for j, copy in enumerate(copies):
-        copy.wait()
+    shifts = [facts[slots + m] for m in range(modes)]
+    place = jnp.int32(0)
+    ends = []
+    for shift in range(1, SMAX + 1):
+        for m in range(modes):
+            found = shifts[m] == shift
+
+            @pl.when(found)
+            def _(place=place, m=m):
+                order[place] = m
+
+            place = place + found.astype(jnp.int32)
+        ends.append(place)
+    ordered = [order[m] for m in range(modes)]
+
+    def handle(j, first):
         slot = facts[j]
-        blocks = [held_ref[j, mode].astype(jnp.float32) for mode in range(modes)]
+        blocks = [held_ref[j, mode].astype(jnp.float32) for mode in ordered]
         totals = []
-        for shift in range(1, SMAX + 1):
-            terms = [jnp.where(facts[slots + m] == shift, b, 0.0) for m, b in enumerate(blocks)]
-            totals.append(narrow(sum(terms[1:], terms[0])))
+        for run in (blocks[:first], blocks[first:]):
+            total = sum(run[1:], run[0]) if run else jnp.zeros((orbitals, width), jnp.float32)
+            totals.append(narrow(total))
         turned = narrow(dot(jnp.concatenate(totals, 0), turn_ref[...]))
         for index, total in enumerate(totals):
             w_ref[slot, index, :orbitals, :] = total
             w_ref[slot, index, orbitals:, :] = turned[index * orbitals : (index + 1) * orbitals]
+
+    for first in range(modes + 1):
+
+        @pl.when(ends[0] == first)
+        def _(first=first):
+            for j, copy in enumerate(copies):
+                copy.wait()
+                handle(j, first)
 
 
 def make_weights(facts, cotangent, after):
@@ -85,6 +107,7 @@
             pltpu.VMEM(cotangent.shape, jnp.bfloat16),
             pltpu.VMEM((width, width), jnp.bfloat16),
             pltpu.SMEM((slots + modes,), jnp.int32),
+            pltpu.SMEM((modes,), jnp.int32),
             pltpu.SemaphoreType.DMA((slots,)),
             pltpu.SemaphoreType.DMA,
         ],
@@ -100,9 +123,10 @@
     return narrow(dot(half_r, factor_ref[0]) + dot(half_i, factor_ref[1]))
 
 
-def flip_kernel(x_ref, c_ref, out_ref, top_ref, factor_ref):
-    count, orbitals, width = x_ref.shape
-    turned = c_ref[...].astype(jnp.float32).T
+def flip_kernel(joined_ref, out_ref, top_ref, factor_ref, other_ref):
+    count, orbitals, width = out_ref.shape
+    other_ref[...] = joined_ref[count : 2 * count]
+    turned = joined_ref[2 * count].astype(jnp.float32).T
     c_r, c_i = narrow(turned[:orbitals]), narrow(turned[orbitals:])
     row = lax.broadcasted_iota(jnp.int32, (orbitals, width), 0)
     col = lax.broadcasted_iota(jnp.int32, (orbitals, width), 1)
@@ -111,7 +135,7 @@
     factor_ref[0] = narrow(dot(c_r, left) - dot(c_i, right))
     factor_ref[1] = narrow(-dot(c_i, left) - dot(c_r, right))
     for index in range(count):
-        result = sandwich(x_ref[index], factor_ref)
+        result = sandwich(joined_ref[index], factor_ref)
         out_ref[index] = result
         if index == count - 1:
             top_ref[0] = result
@@ -260,16 +284,16 @@
     one = (1, orbitals, width)
     big = 2 * count * orbitals * width * width
 
-    g_own = greater[0]
-    g_near = [column(g_own, 1), column(g_own, -1)]
-    flipped, top, factors = call(
-        flip_kernel, "flip", [(pair, bf16), (one, bf16), (pair, bf16)], [lesser[0], coupling], 2 * big
-    )
+    g_behind = [column(greater[0], distance) for distance in (1, 2)]
+    joined = jnp.concatenate([lesser[0], greater[0], coupling[None]], 0)
+    flipped, top, factors, g_own = call(
+        flip_kernel, "flip", [(pair, bf16), (one, bf16), (pair, bf16), (pair, bf16)], [joined], 2 * big
+    )
+    g_ahead = [column(g_own, -distance) for distance in (1, 2)]
     above = crossed(flipped, -1, False)
     diagonal = crossed(flipped, -1, True)
     across = crossed(top, 0, True)
-    weights = make_weights(jnp.concatenate([offsets, mode_shift]), cotangent, g_near)
-    g_far = [column(g_near[1], -1), column(g_near[0], 1)][::-1]
+    weights = make_weights(jnp.concatenate([offsets, mode_shift]), cotangent, [g_behind[0], top])
 
     upper = [parity, top, above, across, diagonal, weights]
     ahead, behind = call(upper_far_kernel, "upper_far", [(pair, bf16)] * 2, upper, 6 * big, True)
@@ -277,12 +301,12 @@
 
     (acc,) = call(
         lower_near_kernel, "lower_near", [((2, count * orbitals, SMAX * width), f32)],
-        [parity, g_near[0], g_own, g_near[1], weights], 12 * big, True,
+        [parity, g_behind[0], g_own, g_ahead[0], weights], 12 * big, True,
     )
     own, other, to_above = call(
         lower_far_kernel, "lower_far",
         [((orbitals, width), f32), ((orbitals, width), f32), ((2 * count, orbitals, width), bf16)],
-        [parity, g_far[1], g_far[0], weights, acc], 6 * big, True,
+        [parity, g_ahead[1], g_behind[1], weights, acc], 6 * big, True,
     )
     near_ahead, near_behind, here = call(
         upper_near_kernel, "upper_near", [(pair, f32)] * 3, upper, 12 * big, True, [own]

time: 62.7 us -> 66.2 us (1.056)
  the two profiles are of different devices: /device:TPU:1 before, /device:TPU:56 now
where the time goes in v5:
time: 66.2 us; the launch traced here: 66 us
  waiting for transfers between devices  25.9 us (39%)
  starting transfers between devices  23.6 us (36%)
  Pallas kernels  13.7 us (21%)
  other arithmetic  1.98 us (3%)
  between operations  0.77 us (1%)
    ppermute x5, waiting for transfers between devices, crossed(): return lax.ppermute(block, both, route)  14.4 us
    ppermute x8, starting transfers between devices, column(): return lax.ppermute(block, 'ka', route)  14 us
    ppermute x8, waiting for transfers between devices, column(): return lax.ppermute(block, 'ka', route)  11.5 us
    ppermute x5, starting transfers between devices, crossed(): return lax.ppermute(block, both, route)  9.66 us
    pallas_call x9, Pallas kernels, call(): pl.pallas_call(kernel, out_shape=[jax.ShapeDtypeStruct(s, d) for s, d in...  8.92 us
    pallas_call x1, Pallas kernels, make_weights(): pl.pallas_call(weights_kernel, out_shape=jax.ShapeDtypeStruct((slots, SMA...  4.76 us
  transfers between devices with their start and end apart: 13, of which 5 were waited for; matrix products, arithmetic and copies ran while one was open for 3% of the time, Pallas kernels for 18%

profile of v5, /device:TPU:56, one launch (start us, length us, event | category | flops | bytes accessed | tf_op | source)
XLA Modules:
  0.0 66.0 jit_solution(11589067988035600198)
XLA Ops:
  0.6 2.0 %collective-permute-start.2 = (bf16[2,192,384]{2,1,0:T(8,128)(2,1)}, bf16[2,192,384]{2,1,0:T(8,128)(2,1)S(1)}, u32[]{:S(2)}, u32[]{:S(2)}) collective-permute-start(bf16[2,192,384]{2,1,0:T(8,128)(2,1)} %bitcast.8), channel_id=1, source_target_pairs={{0,8},{4,12},{8,16},{12,20},{16,24},{20,28},{24,32},{28,36},{32,40... | collective-permute-start | bytes 884744 | tf_op jit(solution)/shard_map/ppermute | solution.py:272
  2.6 1.2 %pad_maximum_fusion.joined_ref = bf16[5,192,384]{2,1,0:T(8,128)(2,1)S(1)} fusion(bf16[1,192,384]{2,1,0:T(8,128)(2,1)} %bitcast.11, bf16[2,192,384]{2,1,0:T(8,128)(2,1)} %bitcast.9, bf16[2,192,384]{2,1,0:T(8,128)(2,1)} %bitcast.7), kind=kLoop, calls=%fused_computation | loop fusion | flops 737280 | bytes 1474560 | tf_op jit(solution)/shard_map/concatenate | solution.py:288
  3.9 1.1 %flip.1 = (bf16[2,192,384]{2,1,0:T(8,128)(2,1)S(1)}, bf16[1,192,384]{2,1,0:T(8,128)(2,1)S(1)}, bf16[2,192,384]{2,1,0:T(8,128)(2,1)S(1)}, bf16[2,192,384]{2,1,0:T(8,128)(2,1)S(1)}) custom-call(bf16[5,192,384]{2,1,0:T(8,128)(2,1)S(1)} %pad_maximum_fusion.joined_ref), custom_call_target="tpu_custom_call" | custom-call | flops 2264924 | bytes 40000 | tf_op jit(solution)/shard_map/flip/pallas_call | solution.py:251
  5.0 1.3 %collective-permute-start.7 = (bf16[1,192,384]{2,1,0:T(8,128)(2,1)S(1)}, bf16[1,192,384]{2,1,0:T(8,128)(2,1)S(1)}, u32[]{:S(2)}, u32[]{:S(2)}) collective-permute-start(bf16[1,192,384]{2,1,0:T(8,128)(2,1)S(1)} %get-tuple-element.17.behind_ref.own_ref), channel_id=1, source_target_pairs={{0,4},{1,5},{2,6},{3,7},{4,0},{5,1},{6,2},{7,3},{8,12},{9,13},{10,... | collective-permute-start | bytes 442376 | tf_op jit(solution)/shard_map/ppermute | solution.py:281
  6.3 1.9 %collective-permute-start.6 = (bf16[2,192,384]{2,1,0:T(8,128)(2,1)S(1)}, bf16[2,192,384]{2,1,0:T(8,128)(2,1)S(1)}, u32[]{:S(2)}, u32[]{:S(2)}) collective-permute-start(bf16[2,192,384]{2,1,0:T(8,128)(2,1)S(1)} %get-tuple-element.22), channel_id=1, source_target_pairs={{1,0},{2,1},{3,2},{5,4},{6,5},{7,6},{9,8},{10,9},{11,10},{13,12},{... | collective-permute-start | bytes 884744 | tf_op jit(solution)/shard_map/ppermute | solution.py:281
  8.2 4.2 %collective-permute-start.8 = (bf16[2,192,384]{2,1,0:T(8,128)(2,1)S(1)}, bf16[2,192,384]{2,1,0:T(8,128)(2,1)S(1)}, u32[]{:S(2)}, u32[]{:S(2)}) collective-permute-start(bf16[2,192,384]{2,1,0:T(8,128)(2,1)S(1)} %get-tuple-element.22), channel_id=1, source_target_pairs={{1,4},{2,5},{3,6},{5,0},{6,1},{7,2},{9,12},{10,13},{11,14},{13,8},... | collective-permute-start | bytes 884744 | tf_op jit(solution)/shard_map/ppermute | solution.py:281
  12.4 0.2 collective-permute-start.3
  12.6 7.6 %collective-permute-start = (bf16[2,192,384]{2,1,0:T(8,128)(2,1)S(1)}, bf16[2,192,384]{2,1,0:T(8,128)(2,1)S(1)}, u32[]{:S(2)}, u32[]{:S(2)}) collective-permute-start(bf16[2,192,384]{2,1,0:T(8,128)(2,1)S(1)} %get-tuple-element.16.own_ref), channel_id=1, source_target_pairs={{0,240},{4,244},{8,248},{12,252},{16,0},{20,4},{24,8},{28,12},{32,... | collective-permute-start | bytes 884744 | tf_op jit(solution)/shard_map/ppermute | solution.py:272
  20.2 0.0 collective-permute-done.2.ahead_ref.behind_ref
  20.2 0.0 collective-permute-start.1
  20.2 0.7 %pad_add_fusion.facts_ref = s32[13]{0:T(128)S(1)} fusion(s32[4]{0:T(128)} %param.11, s32[9]{0:T(128)} %param.10), kind=kLoop, calls=%fused_computation.1 | loop fusion | flops 13 | bytes 104 | tf_op jit(solution)/shard_map/concatenate | solution.py:296
  21.0 4.8 %weights.1.w_ref = bf16[9,2,384,384]{3,2,1,0:T(8,128)(2,1)S(1)} custom-call(s32[13]{0:T(128)S(1)} %pad_add_fusion.facts_ref, bf16[9,4,192,384]{3,2,1,0:T(8,128)(2,1)} %p_ref.1, bf16[2,192,384]{2,1,0:T(8,128)(2,1)S(1)} %collective-permute-done.2.ahead_ref.behind_ref, bf16[1,192,384]{2,1,0:T(8,128)(2,1)S(1)} %get-tuple-element.17.behind_ref.own_ref), custom_call_target="tpu_custom_call" | custom-call | flops 20000000 | bytes 100000 | tf_op jit(solution)/shard_map/weights/pallas_call | solution.py:101
  25.7 0.0 collective-permute-done.6.above_ref
  25.7 0.9 %upper_far.1 = (bf16[2,192,384]{2,1,0:T(8,128)(2,1)S(1)}, bf16[2,192,384]{2,1,0:T(8,128)(2,1)S(1)}) custom-call(s32[1]{0:T(128)} %bitcast.parity_ref, bf16[1,192,384]{2,1,0:T(8,128)(2,1)S(1)} %get-tuple-element.17.behind_ref.own_ref, bf16[2,192,384]{2,1,0:T(8,128)(2,1)S(1)} %collective-permute-done.6.above_ref, ...), custom_call_target="tpu_custom_call" | custom-call | flops 6794772 | bytes 40000 | tf_op jit(solution)/shard_map/upper_far/pallas_call | solution.py:251
  26.7 0.2 collective-permute-start.9
  26.9 1.9 %collective-permute-start.10 = (bf16[2,192,384]{2,1,0:T(8,128)(2,1)S(1)}, bf16[2,192,384]{2,1,0:T(8,128)(2,1)S(1)}, u32[]{:S(2)}, u32[]{:S(2)}) collective-permute-start(bf16[2,192,384]{2,1,0:T(8,128)(2,1)S(1)} %get-tuple-element.27), channel_id=1, source_target_pairs={{0,248},{4,252},{8,0},{12,4},{16,8},{20,12},{24,16},{28,20},{32,24... | collective-permute-start | bytes 884744 | tf_op jit(solution)/shard_map/ppermute | solution.py:272
  28.8 1.7 %lower_near.1.acc_ref = f32[2,384,768]{2,1,0:T(8,128)S(1)} custom-call(s32[1]{0:T(128)} %bitcast.parity_ref, bf16[2,192,384]{2,1,0:T(8,128)(2,1)S(1)} %collective-permute-done.2.ahead_ref.behind_ref, bf16[2,192,384]{2,1,0:T(8,128)(2,1)S(1)} %get-tuple-element.16.own_ref, bf16[2,192,384]{2,1,0:T(8,128)(2,1)S(1)} %collective-permute-done.3.ahead_ref, ...), custom_call_target="tpu_custom_call" | custom-call | flops 13589544 | bytes 40000 | tf_op jit(solution)/shard_map/lower_near/pallas_call | solution.py:251
  30.5 0.9 %collective-permute-done.ahead_ref = bf16[2,192,384]{2,1,0:T(8,128)(2,1)S(1)} collective-permute-done((bf16[2,192,384]{2,1,0:T(8,128)(2,1)S(1)}, bf16[2,192,384]{2,1,0:T(8,128)(2,1)S(1)}, u32[]{:S(2)}, u32[]{:S(2)}) %collective-permute-start) | collective-permute-done | bytes 294944 | tf_op jit(solution)/shard_map/ppermute | solution.py:272
  31.4 9.4 %collective-permute-done.1.behind_ref = bf16[2,192,384]{2,1,0:T(8,128)(2,1)S(1)} collective-permute-done((bf16[2,192,384]{2,1,0:T(8,128)(2,1)}, bf16[2,192,384]{2,1,0:T(8,128)(2,1)S(1)}, u32[]{:S(2)}, u32[]{:S(2)}) %collective-permute-start.1) | collective-permute-done | bytes 294944 | tf_op jit(solution)/shard_map/ppermute | solution.py:272
  40.8 1.0 %lower_far.1 = (f32[192,384]{1,0:T(8,128)S(1)}, f32[192,384]{1,0:T(8,128)S(1)}, bf16[4,192,384]{2,1,0:T(8,128)(2,1)S(1)}) custom-call(s32[1]{0:T(128)} %bitcast.parity_ref, bf16[2,192,384]{2,1,0:T(8,128)(2,1)S(1)} %collective-permute-done.ahead_ref, bf16[2,192,384]{2,1,0:T(8,128)(2,1)S(1)} %collective-permute-done.1.behind_ref, ...), custom_call_target="tpu_custom_call" | custom-call | flops 6794772 | bytes 40000 | tf_op jit(solution)/shard_map/lower_far/pallas_call | solution.py:251
  41.7 2.1 %collective-permute-start.4 = (bf16[4,192,384]{2,1,0:T(8,128)(2,1)S(1)}, bf16[4,192,384]{2,1,0:T(8,128)(2,1)S(1)}, u32[]{:S(2)}, u32[]{:S(2)}) collective-permute-start(bf16[4,192,384]{2,1,0:T(8,128)(2,1)S(1)} %get-tuple-element.19), channel_id=1, source_target_pairs={{0,1},{1,2},{2,3},{4,5},{5,6},{6,7},{8,9},{9,10},{10,11},{12,13},{... | collective-permute-start | bytes 1769480 | tf_op jit(solution)/shard_map/ppermute | solution.py:281
  43.9 1.7 %upper_near.1 = (f32[2,192,384]{2,1,0:T(8,128)S(1)}, f32[2,192,384]{2,1,0:T(8,128)S(1)}, f32[2,192,384]{2,1,0:T(8,128)S(1)}) custom-call(s32[1]{0:T(128)} %bitcast.parity_ref, bf16[1,192,384]{2,1,0:T(8,128)(2,1)S(1)} %get-tuple-element.17.behind_ref.own_ref, bf16[2,192,384]{2,1,0:T(8,128)(2,1)S(1)} %collective-permute-done.6.above_ref, ...), custom_call_target="tpu_custom_call" | custom-call | flops 13589544 | bytes 40000 | tf_op jit(solution)/shard_map/upper_near/pallas_call | solution.py:251
  45.6 0.1 pass.1
  45.8 1.0 %collective-permute-start.11 = (bf16[2,192,384]{2,1,0:T(8,128)(2,1)S(1)}, bf16[2,192,384]{2,1,0:T(8,128)(2,1)S(1)}, u32[]{:S(2)}, u32[]{:S(2)}) collective-permute-start(bf16[2,192,384]{2,1,0:T(8,128)(2,1)S(1)} %get-tuple-element.28), channel_id=1, source_target_pairs={{0,248},{4,252},{8,0},{12,4},{16,8},{20,12},{24,16},{28,20},{32,24... | collective-permute-start | bytes 884744 | tf_op jit(solution)/shard_map/ppermute | solution.py:272
  46.8 1.1 %collective-permute-start.12 = (bf16[2,192,384]{2,1,0:T(8,128)(2,1)S(1)}, bf16[2,192,384]{2,1,0:T(8,128)(2,1)S(1)}, u32[]{:S(2)}, u32[]{:S(2)}) collective-permute-start(bf16[2,192,384]{2,1,0:T(8,128)(2,1)S(1)} %get-tuple-element.29), channel_id=1, source_target_pairs={{0,8},{4,12},{8,16},{12,20},{16,24},{20,28},{24,32},{28,36},{32,40... | collective-permute-start | bytes 884744 | tf_op jit(solution)/shard_map/ppermute | solution.py:272
  47.9 8.2 %collective-permute-done.4.below_ref = bf16[4,192,384]{2,1,0:T(8,128)(2,1)S(1)} collective-permute-done((bf16[4,192,384]{2,1,0:T(8,128)(2,1)S(1)}, bf16[4,192,384]{2,1,0:T(8,128)(2,1)S(1)}, u32[]{:S(2)}, u32[]{:S(2)}) %collective-permute-start.4) | collective-permute-done | bytes 589856 | tf_op jit(solution)/shard_map/ppermute | solution.py:281
  56.1 0.1 merge.1
  56.2 0.1 collective-permute-start.5
  56.3 1.2 %collective-permute-done.12.ahead_ref = bf16[2,192,384]{2,1,0:T(8,128)(2,1)S(1)} collective-permute-done((bf16[2,192,384]{2,1,0:T(8,128)(2,1)S(1)}, bf16[2,192,384]{2,1,0:T(8,128)(2,1)S(1)}, u32[]{:S(2)}, u32[]{:S(2)}) %collective-permute-start.12) | collective-permute-done | bytes 294944 | tf_op jit(solution)/shard_map/ppermute | solution.py:272
  57.5 0.8 %total.1 = bf16[2,192,384]{2,1,0:T(8,128)(2,1)} custom-call(f32[2,192,384]{2,1,0:T(8,128)S(1)} %get-tuple-element.23.here_ref, bf16[2,192,384]{2,1,0:T(8,128)(2,1)S(1)} %collective-permute-done.11.behind_ref, bf16[2,192,384]{2,1,0:T(8,128)(2,1)S(1)} %collective-permute-done.12.ahead_ref), custom_call_target="tpu_custom_call" | custom-call | flops 10000000000 | bytes 40000 | tf_op jit(solution)/shard_map/total/pallas_call | solution.py:251
  58.3 6.2 %collective-permute-done.5.across_ref = bf16[2,192,384]{2,1,0:T(8,128)(2,1)S(1)} collective-permute-done((bf16[2,192,384]{2,1,0:T(8,128)(2,1)S(1)}, bf16[2,192,384]{2,1,0:T(8,128)(2,1)S(1)}, u32[]{:S(2)}, u32[]{:S(2)}) %collective-permute-start.5) | collective-permute-done | bytes 294944 | tf_op jit(solution)/shard_map/ppermute | solution.py:281
  64.5 1.5 %finish.1 = bf16[2,192,384]{2,1,0:T(8,128)(2,1)} custom-call(f32[192,384]{1,0:T(8,128)S(1)} %get-tuple-element.18.own_ref.after_ref, bf16[4,192,384]{2,1,0:T(8,128)(2,1)S(1)} %collective-permute-done.4.below_ref, bf16[2,192,384]{2,1,0:T(8,128)(2,1)S(1)} %collective-permute-done.5.across_ref, bf16[2,192,384]{2,1,0:T(8,128)(2,1)S(1)} %get-tuple-element.21.factor_ref), custom_call_target="tpu_custom_call" | custom-call | flops 2264924 | bytes 40000 | tf_op jit(solution)/shard_map/finish/pallas_call | solution.py:251
  (6 shorter events, 0.0 us)
Async XLA Ops:
  0.6 19.6 %collective-permute-start.2 = (bf16[2,192,384]{2,1,0:T(8,128)(2,1)}, bf16[2,192,384]{2,1,0:T(8,128)(2,1)S(1)}, u32[]{:S(2)}, u32[]{:S(2)}) collective-permute-start(bf16[2,192,384]{2,1,0:T(8,128)(2,1)} %bitcast.8), channel_id=1, source_target_pairs={{0,8},{4,12},{8,16},{12,20},{16,24},{20,28},{24,32},{28,36},{32,40... | collective-permute-start | bytes 884744 | tf_op jit(solution)/shard_map/ppermute | solution.py:272
  5.0 7.6 %collective-permute-start.7 = (bf16[1,192,384]{2,1,0:T(8,128)(2,1)S(1)}, bf16[1,192,384]{2,1,0:T(8,128)(2,1)S(1)}, u32[]{:S(2)}, u32[]{:S(2)}) collective-permute-start(bf16[1,192,384]{2,1,0:T(8,128)(2,1)S(1)} %get-tuple-element.17.behind_ref.own_ref), channel_id=1, source_target_pairs={{0,4},{1,5},{2,6},{3,7},{4,0},{5,1},{6,2},{7,3},{8,12},{9,13},{10,... | collective-permute-start | bytes 442376 | tf_op jit(solution)/shard_map/ppermute | solution.py:281
  6.3 19.4 %collective-permute-start.6 = (bf16[2,192,384]{2,1,0:T(8,128)(2,1)S(1)}, bf16[2,192,384]{2,1,0:T(8,128)(2,1)S(1)}, u32[]{:S(2)}, u32[]{:S(2)}) collective-permute-start(bf16[2,192,384]{2,1,0:T(8,128)(2,1)S(1)} %get-tuple-element.22), channel_id=1, source_target_pairs={{1,0},{2,1},{3,2},{5,4},{6,5},{7,6},{9,8},{10,9},{11,10},{13,12},{... | collective-permute-start | bytes 884744 | tf_op jit(solution)/shard_map/ppermute | solution.py:281
  8.2 17.5 %collective-permute-start.8 = (bf16[2,192,384]{2,1,0:T(8,128)(2,1)S(1)}, bf16[2,192,384]{2,1,0:T(8,128)(2,1)S(1)}, u32[]{:S(2)}, u32[]{:S(2)}) collective-permute-start(bf16[2,192,384]{2,1,0:T(8,128)(2,1)S(1)} %get-tuple-element.22), channel_id=1, source_target_pairs={{1,4},{2,5},{3,6},{5,0},{6,1},{7,2},{9,12},{10,13},{11,14},{13,8},... | collective-permute-start | bytes 884744 | tf_op jit(solution)/shard_map/ppermute | solution.py:281
  12.4 16.4 %collective-permute-start.3 = (bf16[2,192,384]{2,1,0:T(8,128)(2,1)S(1)}, bf16[2,192,384]{2,1,0:T(8,128)(2,1)S(1)}, u32[]{:S(2)}, u32[]{:S(2)}) collective-permute-start(bf16[2,192,384]{2,1,0:T(8,128)(2,1)S(1)} %get-tuple-element.16.own_ref), channel_id=1, source_target_pairs={{0,248},{4,252},{8,0},{12,4},{16,8},{20,12},{24,16},{28,20},{32,24... | collective-permute-start | bytes 884744 | tf_op jit(solution)/shard_map/ppermute | solution.py:272
  12.6 18.8 %collective-permute-start = (bf16[2,192,384]{2,1,0:T(8,128)(2,1)S(1)}, bf16[2,192,384]{2,1,0:T(8,128)(2,1)S(1)}, u32[]{:S(2)}, u32[]{:S(2)}) collective-permute-start(bf16[2,192,384]{2,1,0:T(8,128)(2,1)S(1)} %get-tuple-element.16.own_ref), channel_id=1, source_target_pairs={{0,240},{4,244},{8,248},{12,252},{16,0},{20,4},{24,8},{28,12},{32,... | collective-permute-start | bytes 884744 | tf_op jit(solution)/shard_map/ppermute | solution.py:272
  20.2 20.6 %collective-permute-start.1 = (bf16[2,192,384]{2,1,0:T(8,128)(2,1)}, bf16[2,192,384]{2,1,0:T(8,128)(2,1)S(1)}, u32[]{:S(2)}, u32[]{:S(2)}) collective-permute-start(bf16[2,192,384]{2,1,0:T(8,128)(2,1)} %bitcast.10), channel_id=1, source_target_pairs={{0,16},{4,20},{8,24},{12,28},{16,32},{20,36},{24,40},{28,44},{32,4... | collective-permute-start | bytes 884744 | tf_op jit(solution)/shard_map/ppermute | solution.py:272
  26.7 18.9 %collective-permute-start.9 = (bf16[2,192,384]{2,1,0:T(8,128)(2,1)S(1)}, bf16[2,192,384]{2,1,0:T(8,128)(2,1)S(1)}, u32[]{:S(2)}, u32[]{:S(2)}) collective-permute-start(bf16[2,192,384]{2,1,0:T(8,128)(2,1)S(1)} %get-tuple-element.26), channel_id=1, source_target_pairs={{0,8},{4,12},{8,16},{12,20},{16,24},{20,28},{24,32},{28,36},{32,40... | collective-permute-start | bytes 884744 | tf_op jit(solution)/shard_map/ppermute | solution.py:272
  26.9 18.8 %collective-permute-start.10 = (bf16[2,192,384]{2,1,0:T(8,128)(2,1)S(1)}, bf16[2,192,384]{2,1,0:T(8,128)(2,1)S(1)}, u32[]{:S(2)}, u32[]{:S(2)}) collective-permute-start(bf16[2,192,384]{2,1,0:T(8,128)(2,1)S(1)} %get-tuple-element.27), channel_id=1, source_target_pairs={{0,248},{4,252},{8,0},{12,4},{16,8},{20,12},{24,16},{28,20},{32,24... | collective-permute-start | bytes 884744 | tf_op jit(solution)/shard_map/ppermute | solution.py:272
  41.7 14.4 %collective-permute-start.4 = (bf16[4,192,384]{2,1,0:T(8,128)(2,1)S(1)}, bf16[4,192,384]{2,1,0:T(8,128)(2,1)S(1)}, u32[]{:S(2)}, u32[]{:S(2)}) collective-permute-start(bf16[4,192,384]{2,1,0:T(8,128)(2,1)S(1)} %get-tuple-element.19), channel_id=1, source_target_pairs={{0,1},{1,2},{2,3},{4,5},{5,6},{6,7},{8,9},{9,10},{10,11},{12,13},{... | collective-permute-start | bytes 1769480 | tf_op jit(solution)/shard_map/ppermute | solution.py:281
  45.8 10.5 %collective-permute-start.11 = (bf16[2,192,384]{2,1,0:T(8,128)(2,1)S(1)}, bf16[2,192,384]{2,1,0:T(8,128)(2,1)S(1)}, u32[]{:S(2)}, u32[]{:S(2)}) collective-permute-start(bf16[2,192,384]{2,1,0:T(8,128)(2,1)S(1)} %get-tuple-element.28), channel_id=1, source_target_pairs={{0,248},{4,252},{8,0},{12,4},{16,8},{20,12},{24,16},{28,20},{32,24... | collective-permute-start | bytes 884744 | tf_op jit(solution)/shard_map/ppermute | solution.py:272
  46.8 10.7 %collective-permute-start.12 = (bf16[2,192,384]{2,1,0:T(8,128)(2,1)S(1)}, bf16[2,192,384]{2,1,0:T(8,128)(2,1)S(1)}, u32[]{:S(2)}, u32[]{:S(2)}) collective-permute-start(bf16[2,192,384]{2,1,0:T(8,128)(2,1)S(1)} %get-tuple-element.29), channel_id=1, source_target_pairs={{0,8},{4,12},{8,16},{12,20},{16,24},{20,28},{24,32},{28,36},{32,40... | collective-permute-start | bytes 884744 | tf_op jit(solution)/shard_map/ppermute | solution.py:272
  56.2 8.3 %collective-permute-start.5 = (bf16[2,192,384]{2,1,0:T(8,128)(2,1)S(1)}, bf16[2,192,384]{2,1,0:T(8,128)(2,1)S(1)}, u32[]{:S(2)}, u32[]{:S(2)}) collective-permute-start(bf16[2,192,384]{2,1,0:T(8,128)(2,1)S(1)} %merge.1), channel_id=1, source_target_pairs={{0,4},{1,5},{2,6},{3,7},{4,0},{5,1},{6,2},{7,3},{8,12},{9,13},{10,... | collective-permute-start | bytes 884744 | tf_op jit(solution)/shard_map/ppermute | solution.py:281

commit v6 on v5

--- a/solution.py
+++ b/solution.py
@@ -173,7 +173,7 @@
         acc_ref[which] = dot_t(blocks, beside([slot_weights(w_ref, slot) for slot in slots]))
 
 
-def lower_far_kernel(parity_ref, ahead_ref, behind_ref, w_ref, acc_ref, own_ref, other_ref, above_ref):
+def lower_far_kernel(parity_ref, behind_ref, ahead_ref, w_ref, acc_ref, own_ref, other_ref, above_ref):
     even = parity_ref[0] == 0
     behind, ahead = flat(behind_ref), flat(ahead_ref)
     chosen = jnp.where(even, ahead, behind)
@@ -206,7 +206,7 @@
         ref[index] = part if kind is None else part.astype(kind)
 
 
-def upper_far_kernel(parity_ref, own_ref, above_ref, across_ref, diagonal_ref, w_ref, ahead_ref, behind_ref):
+def upper_far_kernel(parity_ref, own_ref, above_ref, across_ref, diagonal_ref, w_ref, behind_ref, ahead_ref):
     even = parity_ref[0] == 0
     width = w_ref.shape[-1]
     same = beside(stack_pairs(own_ref, above_ref))
@@ -233,12 +233,12 @@
         store(ref, sums[:, index * width : (index + 1) * width])
 
 
-def pass_kernel(near_ahead, near_behind, ahead_ref, behind_ref, behind_out, ahead_out):
+def pass_kernel(near_ahead, near_behind, behind_ref, ahead_ref, ahead_out, behind_out):
     ahead_out[...] = narrow(near_ahead[...] + ahead_ref[...].astype(jnp.float32))
     behind_out[...] = narrow(near_behind[...] + behind_ref[...].astype(jnp.float32))
 
 
-def total_kernel(here_ref, behind_ref, ahead_ref, out_ref):
+def total_kernel(here_ref, ahead_ref, behind_ref, out_ref):
     arrived = ahead_ref[...].astype(jnp.float32) + behind_ref[...].astype(jnp.float32)
     out_ref[...] = narrow(here_ref[...] + arrived)
 
@@ -284,19 +284,21 @@
     one = (1, orbitals, width)
     big = 2 * count * orbitals * width * width
 
-    g_behind = [column(greater[0], distance) for distance in (1, 2)]
+    g_behind = [column(greater[0], 1)]
+    g_behind.append(column(g_behind[0], 1))
     joined = jnp.concatenate([lesser[0], greater[0], coupling[None]], 0)
     flipped, top, factors, g_own = call(
         flip_kernel, "flip", [(pair, bf16), (one, bf16), (pair, bf16), (pair, bf16)], [joined], 2 * big
     )
-    g_ahead = [column(g_own, -distance) for distance in (1, 2)]
+    g_ahead = [column(g_own, -1)]
+    g_ahead.append(column(g_ahead[0], -1))
     above = crossed(flipped, -1, False)
     diagonal = crossed(flipped, -1, True)
     across = crossed(top, 0, True)
     weights = make_weights(jnp.concatenate([offsets, mode_shift]), cotangent, [g_behind[0], top])
 
     upper = [parity, top, above, across, diagonal, weights]
-    ahead, behind = call(upper_far_kernel, "upper_far", [(pair, bf16)] * 2, upper, 6 * big, True)
+    behind, ahead = call(upper_far_kernel, "upper_far", [(pair, bf16)] * 2, upper, 6 * big, True)
     ahead, behind = column(ahead, 1), column(behind, -1)
 
     (acc,) = call(
@@ -306,7 +308,7 @@
     own, other, to_above = call(
         lower_far_kernel, "lower_far",
         [((orbitals, width), f32), ((orbitals, width), f32), ((2 * count, orbitals, width), bf16)],
-        [parity, g_ahead[1], g_behind[1], weights, acc], 6 * big, True,
+        [parity, g_behind[1], g_ahead[1], weights, acc], 6 * big, True,
     )
     near_ahead, near_behind, here = call(
         upper_near_kernel, "upper_near", [(pair, f32)] * 3, upper, 12 * big, True, [own]
@@ -315,13 +317,13 @@
     (to_across,) = call(merge_kernel, "merge", [(pair, bf16)], [other, from_below], 10**6)
     from_across = crossed(to_across, 0, True)
 
-    behind, ahead = call(pass_kernel, "pass", [(pair, bf16)] * 2, [near_ahead, near_behind, ahead, behind], 10**6)
+    ahead, behind = call(pass_kernel, "pass", [(pair, bf16)] * 2, [near_ahead, near_behind, behind, ahead], 10**6)
     behind, ahead = column(behind, -1), column(ahead, 1)
     (grad_lesser,) = call(
         finish_kernel, "finish", [(pair, bf16)],
         [own, from_below, from_across, factors], 2 * big,
     )
-    (grad_greater,) = call(total_kernel, "total", [(pair, bf16)], [here, behind, ahead], TAIL)
+    (grad_greater,) = call(total_kernel, "total", [(pair, bf16)], [here, ahead, behind], TAIL)
     return (grad_lesser[None], grad_greater[None])
 
 

time: 66.2 us -> 59.1 us (0.89)
  the two profiles are of different devices: /device:TPU:56 before, /device:TPU:16 now
where the time goes in v6:
time: 59.1 us; the launch traced here: 58.9 us
  starting transfers between devices  27.5 us (47%)
  waiting for transfers between devices  15.2 us (26%)
  Pallas kernels  13.5 us (23%)
  other arithmetic  1.98 us (3%)
  between operations  0.75 us (1%)
    ppermute x8, starting transfers between devices, column(): return lax.ppermute(block, 'ka', route)  21.5 us
    ppermute x8, waiting for transfers between devices, column(): return lax.ppermute(block, 'ka', route)  11.8 us
    pallas_call x9, Pallas kernels, call(): pl.pallas_call(kernel, out_shape=[jax.ShapeDtypeStruct(s, d) for s, d in...  8.94 us
    ppermute x5, starting transfers between devices, crossed(): return lax.ppermute(block, both, route)  6 us
    pallas_call x1, Pallas kernels, make_weights(): pl.pallas_call(weights_kernel, out_shape=jax.ShapeDtypeStruct((slots, SMA...  4.51 us
    ppermute x5, waiting for transfers between devices, crossed(): return lax.ppermute(block, both, route)  3.36 us
    concatenate x1, other arithmetic, per_device(): joined = jnp.concatenate([lesser[0], greater[0], coupling[None]], 0)  1.24 us
  transfers between devices with their start and end apart: 13, of which 6 were waited for; matrix products, arithmetic and copies ran while one was open for 3% of the time, Pallas kernels for 20%

profile of v6, /device:TPU:16, one launch (start us, length us, event | category | flops | bytes accessed | tf_op | source)
XLA Modules:
  0.0 58.9 jit_solution(12869005584431460900)
XLA Ops:
  0.6 2.0 %collective-permute-start = (bf16[2,192,384]{2,1,0:T(8,128)(2,1)}, bf16[2,192,384]{2,1,0:T(8,128)(2,1)S(1)}, u32[]{:S(2)}, u32[]{:S(2)}) collective-permute-start(bf16[2,192,384]{2,1,0:T(8,128)(2,1)} %bitcast.8), channel_id=1, source_target_pairs={{0,8},{4,12},{8,16},{12,20},{16,24},{20,28},{24,32},{28,36},{32,40... | collective-permute-start | bytes 884744 | tf_op jit(solution)/shard_map/ppermute | solution.py:272
  2.6 1.2 %pad_maximum_fusion.joined_ref = bf16[5,192,384]{2,1,0:T(8,128)(2,1)S(1)} fusion(bf16[1,192,384]{2,1,0:T(8,128)(2,1)} %bitcast.10, bf16[2,192,384]{2,1,0:T(8,128)(2,1)} %bitcast.9, bf16[2,192,384]{2,1,0:T(8,128)(2,1)} %bitcast.7), kind=kLoop, calls=%fused_computation | loop fusion | flops 737280 | bytes 1474560 | tf_op jit(solution)/shard_map/concatenate | solution.py:289
  3.9 1.1 %flip.1 = (bf16[2,192,384]{2,1,0:T(8,128)(2,1)S(1)}, bf16[1,192,384]{2,1,0:T(8,128)(2,1)S(1)}, bf16[2,192,384]{2,1,0:T(8,128)(2,1)S(1)}, bf16[2,192,384]{2,1,0:T(8,128)(2,1)S(1)}) custom-call(bf16[5,192,384]{2,1,0:T(8,128)(2,1)S(1)} %pad_maximum_fusion.joined_ref), custom_call_target="tpu_custom_call" | custom-call | flops 2264924 | bytes 40000 | tf_op jit(solution)/shard_map/flip/pallas_call | solution.py:251
  5.0 6.2 %collective-permute-start.2 = (bf16[2,192,384]{2,1,0:T(8,128)(2,1)S(1)}, bf16[2,192,384]{2,1,0:T(8,128)(2,1)S(1)}, u32[]{:S(2)}, u32[]{:S(2)}) collective-permute-start(bf16[2,192,384]{2,1,0:T(8,128)(2,1)S(1)} %get-tuple-element.16.own_ref), channel_id=1, source_target_pairs={{0,248},{4,252},{8,0},{12,4},{16,8},{20,12},{24,16},{28,20},{32,24... | collective-permute-start | bytes 884744 | tf_op jit(solution)/shard_map/ppermute | solution.py:272
  11.2 1.3 %collective-permute-start.6 = (bf16[2,192,384]{2,1,0:T(8,128)(2,1)S(1)}, bf16[2,192,384]{2,1,0:T(8,128)(2,1)S(1)}, u32[]{:S(2)}, u32[]{:S(2)}) collective-permute-start(bf16[2,192,384]{2,1,0:T(8,128)(2,1)S(1)} %get-tuple-element.22), channel_id=1, source_target_pairs={{1,0},{2,1},{3,2},{5,4},{6,5},{7,6},{9,8},{10,9},{11,10},{13,12},{... | collective-permute-start | bytes 884744 | tf_op jit(solution)/shard_map/ppermute | solution.py:281
  12.5 1.3 %collective-permute-start.8 = (bf16[2,192,384]{2,1,0:T(8,128)(2,1)S(1)}, bf16[2,192,384]{2,1,0:T(8,128)(2,1)S(1)}, u32[]{:S(2)}, u32[]{:S(2)}) collective-permute-start(bf16[2,192,384]{2,1,0:T(8,128)(2,1)S(1)} %get-tuple-element.22), channel_id=1, source_target_pairs={{1,4},{2,5},{3,6},{5,0},{6,1},{7,2},{9,12},{10,13},{11,14},{13,8},... | collective-permute-start | bytes 884744 | tf_op jit(solution)/shard_map/ppermute | solution.py:281
  13.8 2.2 %collective-permute-done.ahead_ref.behind_ref = bf16[2,192,384]{2,1,0:T(8,128)(2,1)S(1)} collective-permute-done((bf16[2,192,384]{2,1,0:T(8,128)(2,1)}, bf16[2,192,384]{2,1,0:T(8,128)(2,1)S(1)}, u32[]{:S(2)}, u32[]{:S(2)}) %collective-permute-start) | collective-permute-done | bytes 294944 | tf_op jit(solution)/shard_map/ppermute | solution.py:272
  16.0 0.0 collective-permute-start.1
  16.0 1.5 %collective-permute-done.2.ahead_ref = bf16[2,192,384]{2,1,0:T(8,128)(2,1)S(1)} collective-permute-done((bf16[2,192,384]{2,1,0:T(8,128)(2,1)S(1)}, bf16[2,192,384]{2,1,0:T(8,128)(2,1)S(1)}, u32[]{:S(2)}, u32[]{:S(2)}) %collective-permute-start.2) | collective-permute-done | bytes 294944 | tf_op jit(solution)/shard_map/ppermute | solution.py:272
  17.5 5.8 %collective-permute-start.3 = (bf16[2,192,384]{2,1,0:T(8,128)(2,1)S(1)}, bf16[2,192,384]{2,1,0:T(8,128)(2,1)S(1)}, u32[]{:S(2)}, u32[]{:S(2)}) collective-permute-start(bf16[2,192,384]{2,1,0:T(8,128)(2,1)S(1)} %collective-permute-done.2.ahead_ref), channel_id=1, source_target_pairs={{0,248},{4,252},{8,0},{12,4},{16,8},{20,12},{24,16},{28,20},{32,24... | collective-permute-start | bytes 884744 | tf_op jit(solution)/shard_map/ppermute | solution.py:272
  23.3 0.3 collective-permute-start.7
  23.6 0.7 %pad_add_fusion.facts_ref = s32[13]{0:T(128)S(1)} fusion(s32[4]{0:T(128)} %param.11, s32[9]{0:T(128)} %param.10), kind=kLoop, calls=%fused_computation.1 | loop fusion | flops 13 | bytes 104 | tf_op jit(solution)/shard_map/concatenate | solution.py:298
  24.3 4.5 %weights.1.w_ref = bf16[9,2,384,384]{3,2,1,0:T(8,128)(2,1)S(1)} custom-call(s32[13]{0:T(128)S(1)} %pad_add_fusion.facts_ref, bf16[9,4,192,384]{3,2,1,0:T(8,128)(2,1)} %p_ref.1, bf16[2,192,384]{2,1,0:T(8,128)(2,1)S(1)} %collective-permute-done.ahead_ref.behind_ref, bf16[1,192,384]{2,1,0:T(8,128)(2,1)S(1)} %get-tuple-element.17.behind_ref.own_ref), custom_call_target="tpu_custom_call" | custom-call | flops 20000000 | bytes 100000 | tf_op jit(solution)/shard_map/weights/pallas_call | solution.py:101
  28.9 1.1 %collective-permute-done.7.across_ref = bf16[1,192,384]{2,1,0:T(8,128)(2,1)S(1)} collective-permute-done((bf16[1,192,384]{2,1,0:T(8,128)(2,1)S(1)}, bf16[1,192,384]{2,1,0:T(8,128)(2,1)S(1)}, u32[]{:S(2)}, u32[]{:S(2)}) %collective-permute-start.7) | collective-permute-done | bytes 147488 | tf_op jit(solution)/shard_map/ppermute | solution.py:281
  29.9 0.9 %upper_far.1 = (bf16[2,192,384]{2,1,0:T(8,128)(2,1)S(1)}, bf16[2,192,384]{2,1,0:T(8,128)(2,1)S(1)}) custom-call(s32[1]{0:T(128)} %bitcast.parity_ref, bf16[1,192,384]{2,1,0:T(8,128)(2,1)S(1)} %get-tuple-element.17.behind_ref.own_ref, bf16[2,192,384]{2,1,0:T(8,128)(2,1)S(1)} %collective-permute-done.6.above_ref, ...), custom_call_target="tpu_custom_call" | custom-call | flops 6794772 | bytes 40000 | tf_op jit(solution)/shard_map/upper_far/pallas_call | solution.py:251
  30.9 0.1 collective-permute-start.9
  31.0 2.0 %collective-permute-start.10 = (bf16[2,192,384]{2,1,0:T(8,128)(2,1)S(1)}, bf16[2,192,384]{2,1,0:T(8,128)(2,1)S(1)}, u32[]{:S(2)}, u32[]{:S(2)}) collective-permute-start(bf16[2,192,384]{2,1,0:T(8,128)(2,1)S(1)} %get-tuple-element.27), channel_id=1, source_target_pairs={{0,8},{4,12},{8,16},{12,20},{16,24},{20,28},{24,32},{28,36},{32,40... | collective-permute-start | bytes 884744 | tf_op jit(solution)/shard_map/ppermute | solution.py:272
  33.0 1.7 %lower_near.1.acc_ref = f32[2,384,768]{2,1,0:T(8,128)S(1)} custom-call(s32[1]{0:T(128)} %bitcast.parity_ref, bf16[2,192,384]{2,1,0:T(8,128)(2,1)S(1)} %collective-permute-done.ahead_ref.behind_ref, bf16[2,192,384]{2,1,0:T(8,128)(2,1)S(1)} %get-tuple-element.16.own_ref, bf16[2,192,384]{2,1,0:T(8,128)(2,1)S(1)} %collective-permute-done.2.ahead_ref, ...), custom_call_target="tpu_custom_call" | custom-call | flops 13589544 | bytes 40000 | tf_op jit(solution)/shard_map/lower_near/pallas_call | solution.py:251
  34.7 0.0 collective-permute-done.1.behind_ref
  34.7 1.0 %lower_far.1 = (f32[192,384]{1,0:T(8,128)S(1)}, f32[192,384]{1,0:T(8,128)S(1)}, bf16[4,192,384]{2,1,0:T(8,128)(2,1)S(1)}) custom-call(s32[1]{0:T(128)} %bitcast.parity_ref, bf16[2,192,384]{2,1,0:T(8,128)(2,1)S(1)} %collective-permute-done.1.behind_ref, bf16[2,192,384]{2,1,0:T(8,128)(2,1)S(1)} %collective-permute-done.3.ahead_ref, ...), custom_call_target="tpu_custom_call" | custom-call | flops 6794772 | bytes 40000 | tf_op jit(solution)/shard_map/lower_far/pallas_call | solution.py:251
  35.7 1.5 %collective-permute-start.4 = (bf16[4,192,384]{2,1,0:T(8,128)(2,1)S(1)}, bf16[4,192,384]{2,1,0:T(8,128)(2,1)S(1)}, u32[]{:S(2)}, u32[]{:S(2)}) collective-permute-start(bf16[4,192,384]{2,1,0:T(8,128)(2,1)S(1)} %get-tuple-element.19), channel_id=1, source_target_pairs={{0,1},{1,2},{2,3},{4,5},{5,6},{6,7},{8,9},{9,10},{10,11},{12,13},{... | collective-permute-start | bytes 1769480 | tf_op jit(solution)/shard_map/ppermute | solution.py:281
  37.3 1.7 %upper_near.1 = (f32[2,192,384]{2,1,0:T(8,128)S(1)}, f32[2,192,384]{2,1,0:T(8,128)S(1)}, f32[2,192,384]{2,1,0:T(8,128)S(1)}) custom-call(s32[1]{0:T(128)} %bitcast.parity_ref, bf16[1,192,384]{2,1,0:T(8,128)(2,1)S(1)} %get-tuple-element.17.behind_ref.own_ref, bf16[2,192,384]{2,1,0:T(8,128)(2,1)S(1)} %collective-permute-done.6.above_ref, ...), custom_call_target="tpu_custom_call" | custom-call | flops 13589544 | bytes 40000 | tf_op jit(solution)/shard_map/upper_near/pallas_call | solution.py:251
  39.0 4.0 %collective-permute-done.10.ahead_ref = bf16[2,192,384]{2,1,0:T(8,128)(2,1)S(1)} collective-permute-done((bf16[2,192,384]{2,1,0:T(8,128)(2,1)S(1)}, bf16[2,192,384]{2,1,0:T(8,128)(2,1)S(1)}, u32[]{:S(2)}, u32[]{:S(2)}) %collective-permute-start.10) | collective-permute-done | bytes 294944 | tf_op jit(solution)/shard_map/ppermute | solution.py:272
  43.0 0.1 pass.1
  43.1 0.1 collective-permute-start.11
  43.2 5.3 %collective-permute-start.12 = (bf16[2,192,384]{2,1,0:T(8,128)(2,1)S(1)}, bf16[2,192,384]{2,1,0:T(8,128)(2,1)S(1)}, u32[]{:S(2)}, u32[]{:S(2)}) collective-permute-start(bf16[2,192,384]{2,1,0:T(8,128)(2,1)S(1)} %get-tuple-element.29), channel_id=1, source_target_pairs={{0,248},{4,252},{8,0},{12,4},{16,8},{20,12},{24,16},{28,20},{32,24... | collective-permute-start | bytes 884744 | tf_op jit(solution)/shard_map/ppermute | solution.py:272
  48.6 0.1 merge.1
  48.6 1.5 %collective-permute-start.5 = (bf16[2,192,384]{2,1,0:T(8,128)(2,1)S(1)}, bf16[2,192,384]{2,1,0:T(8,128)(2,1)S(1)}, u32[]{:S(2)}, u32[]{:S(2)}) collective-permute-start(bf16[2,192,384]{2,1,0:T(8,128)(2,1)S(1)} %merge.1), channel_id=1, source_target_pairs={{0,4},{1,5},{2,6},{3,7},{4,0},{5,1},{6,2},{7,3},{8,12},{9,13},{10,... | collective-permute-start | bytes 884744 | tf_op jit(solution)/shard_map/ppermute | solution.py:281
  50.2 4.1 %collective-permute-done.11.ahead_ref = bf16[2,192,384]{2,1,0:T(8,128)(2,1)S(1)} collective-permute-done((bf16[2,192,384]{2,1,0:T(8,128)(2,1)S(1)}, bf16[2,192,384]{2,1,0:T(8,128)(2,1)S(1)}, u32[]{:S(2)}, u32[]{:S(2)}) %collective-permute-start.11) | collective-permute-done | bytes 294944 | tf_op jit(solution)/shard_map/ppermute | solution.py:272
  54.3 0.8 %total.1 = bf16[2,192,384]{2,1,0:T(8,128)(2,1)} custom-call(f32[2,192,384]{2,1,0:T(8,128)S(1)} %get-tuple-element.23.here_ref, bf16[2,192,384]{2,1,0:T(8,128)(2,1)S(1)} %collective-permute-done.11.ahead_ref, bf16[2,192,384]{2,1,0:T(8,128)(2,1)S(1)} %collective-permute-done.12.behind_ref), custom_call_target="tpu_custom_call" | custom-call | flops 10000000000 | bytes 40000 | tf_op jit(solution)/shard_map/total/pallas_call | solution.py:251
  55.1 2.3 %collective-permute-done.5.across_ref = bf16[2,192,384]{2,1,0:T(8,128)(2,1)S(1)} collective-permute-done((bf16[2,192,384]{2,1,0:T(8,128)(2,1)S(1)}, bf16[2,192,384]{2,1,0:T(8,128)(2,1)S(1)}, u32[]{:S(2)}, u32[]{:S(2)}) %collective-permute-start.5) | collective-permute-done | bytes 294944 | tf_op jit(solution)/shard_map/ppermute | solution.py:281
  57.4 1.5 %finish.1 = bf16[2,192,384]{2,1,0:T(8,128)(2,1)} custom-call(f32[192,384]{1,0:T(8,128)S(1)} %get-tuple-element.18.own_ref.after_ref, bf16[4,192,384]{2,1,0:T(8,128)(2,1)S(1)} %collective-permute-done.4.below_ref, bf16[2,192,384]{2,1,0:T(8,128)(2,1)S(1)} %collective-permute-done.5.across_ref, bf16[2,192,384]{2,1,0:T(8,128)(2,1)S(1)} %get-tuple-element.21.factor_ref), custom_call_target="tpu_custom_call" | custom-call | flops 2264924 | bytes 40000 | tf_op jit(solution)/shard_map/finish/pallas_call | solution.py:251
  (6 shorter events, 0.0 us)
Async XLA Ops:
  0.6 15.3 %collective-permute-start = (bf16[2,192,384]{2,1,0:T(8,128)(2,1)}, bf16[2,192,384]{2,1,0:T(8,128)(2,1)S(1)}, u32[]{:S(2)}, u32[]{:S(2)}) collective-permute-start(bf16[2,192,384]{2,1,0:T(8,128)(2,1)} %bitcast.8), channel_id=1, source_target_pairs={{0,8},{4,12},{8,16},{12,20},{16,24},{20,28},{24,32},{28,36},{32,40... | collective-permute-start | bytes 884744 | tf_op jit(solution)/shard_map/ppermute | solution.py:272
  5.0 12.5 %collective-permute-start.2 = (bf16[2,192,384]{2,1,0:T(8,128)(2,1)S(1)}, bf16[2,192,384]{2,1,0:T(8,128)(2,1)S(1)}, u32[]{:S(2)}, u32[]{:S(2)}) collective-permute-start(bf16[2,192,384]{2,1,0:T(8,128)(2,1)S(1)} %get-tuple-element.16.own_ref), channel_id=1, source_target_pairs={{0,248},{4,252},{8,0},{12,4},{16,8},{20,12},{24,16},{28,20},{32,24... | collective-permute-start | bytes 884744 | tf_op jit(solution)/shard_map/ppermute | solution.py:272
  11.2 18.7 %collective-permute-start.6 = (bf16[2,192,384]{2,1,0:T(8,128)(2,1)S(1)}, bf16[2,192,384]{2,1,0:T(8,128)(2,1)S(1)}, u32[]{:S(2)}, u32[]{:S(2)}) collective-permute-start(bf16[2,192,384]{2,1,0:T(8,128)(2,1)S(1)} %get-tuple-element.22), channel_id=1, source_target_pairs={{1,0},{2,1},{3,2},{5,4},{6,5},{7,6},{9,8},{10,9},{11,10},{13,12},{... | collective-permute-start | bytes 884744 | tf_op jit(solution)/shard_map/ppermute | solution.py:281
  12.5 17.4 %collective-permute-start.8 = (bf16[2,192,384]{2,1,0:T(8,128)(2,1)S(1)}, bf16[2,192,384]{2,1,0:T(8,128)(2,1)S(1)}, u32[]{:S(2)}, u32[]{:S(2)}) collective-permute-start(bf16[2,192,384]{2,1,0:T(8,128)(2,1)S(1)} %get-tuple-element.22), channel_id=1, source_target_pairs={{1,4},{2,5},{3,6},{5,0},{6,1},{7,2},{9,12},{10,13},{11,14},{13,8},... | collective-permute-start | bytes 884744 | tf_op jit(solution)/shard_map/ppermute | solution.py:281
  16.0 18.7 %collective-permute-start.1 = (bf16[2,192,384]{2,1,0:T(8,128)(2,1)S(1)}, bf16[2,192,384]{2,1,0:T(8,128)(2,1)S(1)}, u32[]{:S(2)}, u32[]{:S(2)}) collective-permute-start(bf16[2,192,384]{2,1,0:T(8,128)(2,1)S(1)} %collective-permute-done.ahead_ref.behind_ref), channel_id=1, source_target_pairs={{0,8},{4,12},{8,16},{12,20},{16,24},{20,28},{24,32},{28,36},{32,40... | collective-permute-start | bytes 884744 | tf_op jit(solution)/shard_map/ppermute | solution.py:272
  17.5 17.2 %collective-permute-start.3 = (bf16[2,192,384]{2,1,0:T(8,128)(2,1)S(1)}, bf16[2,192,384]{2,1,0:T(8,128)(2,1)S(1)}, u32[]{:S(2)}, u32[]{:S(2)}) collective-permute-start(bf16[2,192,384]{2,1,0:T(8,128)(2,1)S(1)} %collective-permute-done.2.ahead_ref), channel_id=1, source_target_pairs={{0,248},{4,252},{8,0},{12,4},{16,8},{20,12},{24,16},{28,20},{32,24... | collective-permute-start | bytes 884744 | tf_op jit(solution)/shard_map/ppermute | solution.py:272
  23.3 6.6 %collective-permute-start.7 = (bf16[1,192,384]{2,1,0:T(8,128)(2,1)S(1)}, bf16[1,192,384]{2,1,0:T(8,128)(2,1)S(1)}, u32[]{:S(2)}, u32[]{:S(2)}) collective-permute-start(bf16[1,192,384]{2,1,0:T(8,128)(2,1)S(1)} %get-tuple-element.17.behind_ref.own_ref), channel_id=1, source_target_pairs={{0,4},{1,5},{2,6},{3,7},{4,0},{5,1},{6,2},{7,3},{8,12},{9,13},{10,... | collective-permute-start | bytes 442376 | tf_op jit(solution)/shard_map/ppermute | solution.py:281
  30.9 8.1 %collective-permute-start.9 = (bf16[2,192,384]{2,1,0:T(8,128)(2,1)S(1)}, bf16[2,192,384]{2,1,0:T(8,128)(2,1)S(1)}, u32[]{:S(2)}, u32[]{:S(2)}) collective-permute-start(bf16[2,192,384]{2,1,0:T(8,128)(2,1)S(1)} %get-tuple-element.26), channel_id=1, source_target_pairs={{0,248},{4,252},{8,0},{12,4},{16,8},{20,12},{24,16},{28,20},{32,24... | collective-permute-start | bytes 884744 | tf_op jit(solution)/shard_map/ppermute | solution.py:272
  31.0 12.0 %collective-permute-start.10 = (bf16[2,192,384]{2,1,0:T(8,128)(2,1)S(1)}, bf16[2,192,384]{2,1,0:T(8,128)(2,1)S(1)}, u32[]{:S(2)}, u32[]{:S(2)}) collective-permute-start(bf16[2,192,384]{2,1,0:T(8,128)(2,1)S(1)} %get-tuple-element.27), channel_id=1, source_target_pairs={{0,8},{4,12},{8,16},{12,20},{16,24},{20,28},{24,32},{28,36},{32,40... | collective-permute-start | bytes 884744 | tf_op jit(solution)/shard_map/ppermute | solution.py:272
  35.7 12.9 %collective-permute-start.4 = (bf16[4,192,384]{2,1,0:T(8,128)(2,1)S(1)}, bf16[4,192,384]{2,1,0:T(8,128)(2,1)S(1)}, u32[]{:S(2)}, u32[]{:S(2)}) collective-permute-start(bf16[4,192,384]{2,1,0:T(8,128)(2,1)S(1)} %get-tuple-element.19), channel_id=1, source_target_pairs={{0,1},{1,2},{2,3},{4,5},{5,6},{6,7},{8,9},{9,10},{10,11},{12,13},{... | collective-permute-start | bytes 1769480 | tf_op jit(solution)/shard_map/ppermute | solution.py:281
  43.1 11.2 %collective-permute-start.11 = (bf16[2,192,384]{2,1,0:T(8,128)(2,1)S(1)}, bf16[2,192,384]{2,1,0:T(8,128)(2,1)S(1)}, u32[]{:S(2)}, u32[]{:S(2)}) collective-permute-start(bf16[2,192,384]{2,1,0:T(8,128)(2,1)S(1)} %get-tuple-element.28), channel_id=1, source_target_pairs={{0,8},{4,12},{8,16},{12,20},{16,24},{20,28},{24,32},{28,36},{32,40... | collective-permute-start | bytes 884744 | tf_op jit(solution)/shard_map/ppermute | solution.py:272
  43.2 11.1 %collective-permute-start.12 = (bf16[2,192,384]{2,1,0:T(8,128)(2,1)S(1)}, bf16[2,192,384]{2,1,0:T(8,128)(2,1)S(1)}, u32[]{:S(2)}, u32[]{:S(2)}) collective-permute-start(bf16[2,192,384]{2,1,0:T(8,128)(2,1)S(1)} %get-tuple-element.29), channel_id=1, source_target_pairs={{0,248},{4,252},{8,0},{12,4},{16,8},{20,12},{24,16},{28,20},{32,24... | collective-permute-start | bytes 884744 | tf_op jit(solution)/shard_map/ppermute | solution.py:272
  48.6 8.8 %collective-permute-start.5 = (bf16[2,192,384]{2,1,0:T(8,128)(2,1)S(1)}, bf16[2,192,384]{2,1,0:T(8,128)(2,1)S(1)}, u32[]{:S(2)}, u32[]{:S(2)}) collective-permute-start(bf16[2,192,384]{2,1,0:T(8,128)(2,1)S(1)} %merge.1), channel_id=1, source_target_pairs={{0,4},{1,5},{2,6},{3,7},{4,0},{5,1},{6,2},{7,3},{8,12},{9,13},{10,... | collective-permute-start | bytes 884744 | tf_op jit(solution)/shard_map/ppermute | solution.py:281

commit v7 on v6

--- a/solution.py
+++ b/solution.py
@@ -9,8 +9,10 @@
 
 SMAX = 2
 MID = 4
+FAR = (0, 1, 7, 8)
+NEAR = (1, 2, 3, 4, 5, 6, 7)
 VMEM = 24 * 1024 * 1024
-WEIGHTS_VMEM = 44 * 1024 * 1024
+WEIGHTS_VMEM = {4: 48, 7: 44}
 TAIL = 10**12
 
 
@@ -45,19 +47,24 @@
 
 
 def weights_kernel(
-    facts_ref, p_ref, ahead_ref, behind_ref, w_ref, held_ref, turn_ref, facts, order, arrived, known
+    wanted, facts_ref, p_ref, first_ref, second_ref, w_ref, held_ref, turn_ref, facts, order, place_of, arrived, known
 ):
     slots, modes, orbitals, width = p_ref.shape
     fetch = pltpu.make_async_copy(facts_ref, facts, known)
     fetch.start()
-    copies = [pltpu.make_async_copy(p_ref.at[j], held_ref.at[j], arrived.at[j]) for j in range(slots)]
+    fetch.wait()
+    for j in range(slots):
+        place_of[facts[j]] = jnp.int32(j)
+    copies = [
+        pltpu.make_async_copy(p_ref.at[place_of[slot]], held_ref.at[i], arrived.at[i])
+        for i, slot in enumerate(wanted)
+    ]
     for copy in copies:
         copy.start()
     row = lax.broadcasted_iota(jnp.int32, (width, width), 0)
     col = lax.broadcasted_iota(jnp.int32, (width, width), 1)
     turn = jnp.where(row == col + orbitals, -1.0, jnp.where(row + orbitals == col, 1.0, 0.0))
     turn_ref[...] = narrow(turn)
-    fetch.wait()
     shifts = [facts[slots + m] for m in range(modes)]
     place = jnp.int32(0)
     ends = []
@@ -74,7 +81,6 @@
     ordered = [order[m] for m in range(modes)]
 
     def handle(j, first):
-        slot = facts[j]
         blocks = [held_ref[j, mode].astype(jnp.float32) for mode in ordered]
         totals = []
         for run in (blocks[:first], blocks[first:]):
@@ -82,8 +88,8 @@
             totals.append(narrow(total))
         turned = narrow(dot(jnp.concatenate(totals, 0), turn_ref[...]))
         for index, total in enumerate(totals):
-            w_ref[slot, index, :orbitals, :] = total
-            w_ref[slot, index, orbitals:, :] = turned[index * orbitals : (index + 1) * orbitals]
+            w_ref[j, index, :orbitals, :] = total
+            w_ref[j, index, orbitals:, :] = turned[index * orbitals : (index + 1) * orbitals]
 
     for first in range(modes + 1):
 
@@ -94,24 +100,26 @@
                 handle(j, first)
 
 
-def make_weights(facts, cotangent, after):
+def make_weights(facts, cotangent, wanted, after):
     slots, modes, orbitals, width = cotangent.shape
+    count = len(wanted)
     anywhere = pl.BlockSpec(memory_space=pl.ANY)
     main = pl.BlockSpec(memory_space=pltpu.HBM)
     return pl.pallas_call(
-        weights_kernel,
-        out_shape=jax.ShapeDtypeStruct((slots, SMAX, width, width), jnp.bfloat16),
+        functools.partial(weights_kernel, wanted),
+        out_shape=jax.ShapeDtypeStruct((count, SMAX, width, width), jnp.bfloat16),
         in_specs=[main, main, anywhere, anywhere],
         out_specs=resident(),
         scratch_shapes=[
-            pltpu.VMEM(cotangent.shape, jnp.bfloat16),
+            pltpu.VMEM((count,) + cotangent.shape[1:], jnp.bfloat16),
             pltpu.VMEM((width, width), jnp.bfloat16),
             pltpu.SMEM((slots + modes,), jnp.int32),
             pltpu.SMEM((modes,), jnp.int32),
-            pltpu.SemaphoreType.DMA((slots,)),
+            pltpu.SMEM((slots,), jnp.int32),
+            pltpu.SemaphoreType.DMA((count,)),
             pltpu.SemaphoreType.DMA,
         ],
-        compiler_params=pltpu.CompilerParams(vmem_limit_bytes=WEIGHTS_VMEM),
+        compiler_params=pltpu.CompilerParams(vmem_limit_bytes=WEIGHTS_VMEM[count] * 1024 * 1024),
         cost_estimate=cost(2 * 10**9, 10**7),
         name="weights",
     )(facts, cotangent, *after)
@@ -167,7 +175,7 @@
     even = parity_ref[0] == 0
     blocks = beside([flat(behind_ref), flat(own_ref), flat(ahead_ref)])
     for which in range(2):
-        slots = [MID - 2 * column for column in (-1, 0, 1)]
+        slots = [MID - NEAR[0] - 2 * column for column in (-1, 0, 1)]
         if which == 1:
             slots = [jnp.where(even, slot + 1, slot - 1) for slot in slots]
         acc_ref[which] = dot_t(blocks, beside([slot_weights(w_ref, slot) for slot in slots]))
@@ -177,9 +185,9 @@
     even = parity_ref[0] == 0
     behind, ahead = flat(behind_ref), flat(ahead_ref)
     chosen = jnp.where(even, ahead, behind)
-    slot = jnp.where(even, 1, 2 * MID - 1)
+    slot = jnp.where(even, 1, 2)
     rows, width = own_ref.shape
-    both = beside([slot_weights(w_ref, 0), slot_weights(w_ref, 2 * MID)])
+    both = beside([slot_weights(w_ref, 0), slot_weights(w_ref, 3)])
     same = acc_ref[0] + dot_t(beside([ahead, behind]), both)
     other = acc_ref[1] + dot_t(chosen, slot_weights(w_ref, slot))
     own_ref[...] = same[:rows, :width]
@@ -211,8 +219,8 @@
     width = w_ref.shape[-1]
     same = beside(stack_pairs(own_ref, above_ref))
     other = beside(stack_pairs(across_ref, diagonal_ref))
-    extra = dot(other, slot_weights(w_ref, jnp.where(even, 1, 2 * MID - 1)))
-    sums = dot(same, beside([slot_weights(w_ref, 0), slot_weights(w_ref, 2 * MID)]))
+    extra = dot(other, slot_weights(w_ref, jnp.where(even, 1, 2)))
+    sums = dot(same, beside([slot_weights(w_ref, 0), slot_weights(w_ref, 3)]))
     store(ahead_ref, sums[:, :width] + jnp.where(even, extra, 0.0), jnp.bfloat16)
     store(behind_ref, sums[:, width:] + jnp.where(even, 0.0, extra), jnp.bfloat16)
 
@@ -223,7 +231,7 @@
     even = parity_ref[0] == 0
     width = w_ref.shape[-1]
     blocks = beside(stack_pairs(own_ref, above_ref) + stack_pairs(across_ref, diagonal_ref))
-    same = [MID - 2 * column for column in (1, -1, 0)]
+    same = [MID - NEAR[0] - 2 * column for column in (1, -1, 0)]
     other = [jnp.where(even, slot + 1, slot - 1) for slot in same]
     weights = jnp.concatenate(
         [beside([slot_weights(w_ref, slot) for slot in slots]) for slots in (same, other)], 0
@@ -295,23 +303,26 @@
     above = crossed(flipped, -1, False)
     diagonal = crossed(flipped, -1, True)
     across = crossed(top, 0, True)
-    weights = make_weights(jnp.concatenate([offsets, mode_shift]), cotangent, [g_behind[0], top])
-
-    upper = [parity, top, above, across, diagonal, weights]
-    behind, ahead = call(upper_far_kernel, "upper_far", [(pair, bf16)] * 2, upper, 6 * big, True)
+    facts = jnp.concatenate([offsets, mode_shift])
+    weights_far = make_weights(facts, cotangent, FAR, [g_behind[0], top])
+
+    upper = [parity, top, above, across, diagonal]
+    behind, ahead = call(upper_far_kernel, "upper_far", [(pair, bf16)] * 2, upper + [weights_far], 6 * big, True)
+    sent = [behind, ahead]
     ahead, behind = column(ahead, 1), column(behind, -1)
 
+    weights_near = make_weights(facts, cotangent, NEAR, sent)
     (acc,) = call(
         lower_near_kernel, "lower_near", [((2, count * orbitals, SMAX * width), f32)],
-        [parity, g_behind[0], g_own, g_ahead[0], weights], 12 * big, True,
+        [parity, g_behind[0], g_own, g_ahead[0], weights_near], 12 * big, True,
     )
     own, other, to_above = call(
         lower_far_kernel, "lower_far",
         [((orbitals, width), f32), ((orbitals, width), f32), ((2 * count, orbitals, width), bf16)],
-        [parity, g_behind[1], g_ahead[1], weights, acc], 6 * big, True,
+        [parity, g_behind[1], g_ahead[1], weights_far, acc], 6 * big, True,
     )
     near_ahead, near_behind, here = call(
-        upper_near_kernel, "upper_near", [(pair, f32)] * 3, upper, 12 * big, True, [own]
+        upper_near_kernel, "upper_near", [(pair, f32)] * 3, upper + [weights_near], 12 * big, True, [own]
     )
     from_below = crossed(to_above, 1, False)
     (to_across,) = call(merge_kernel, "merge", [(pair, bf16)], [other, from_below], 10**6)

time: 59.1 us -> 63.6 us (1.076)
  the two profiles are of different devices: /device:TPU:16 before, /device:TPU:1 now
where the time goes in v7:
time: 63.6 us; the launch traced here: 63.4 us
  starting transfers between devices  36.4 us (57%)
  Pallas kernels  16.7 us (26%)
  waiting for transfers between devices  7.37 us (12%)
  other arithmetic  2.13 us (3%)
  between operations  0.79 us (1%)
    ppermute x8, starting transfers between devices, column(): return lax.ppermute(block, 'ka', route)  20 us
    ppermute x5, starting transfers between devices, crossed(): return lax.ppermute(block, both, route)  16.4 us
    pallas_call x9, Pallas kernels, call(): pl.pallas_call(kernel, out_shape=[jax.ShapeDtypeStruct(s, d) for s, d in...  8.93 us
    pallas_call x2, Pallas kernels, make_weights(): pl.pallas_call(functools.partial(weights_kernel, wanted), out_shape=jax.S...  7.75 us
    ppermute x8, waiting for transfers between devices, column(): return lax.ppermute(block, 'ka', route)  4 us
    ppermute x5, waiting for transfers between devices, crossed(): return lax.ppermute(block, both, route)  3.37 us
  transfers between devices with their start and end apart: 13, of which 4 were waited for; matrix products, arithmetic and copies ran while one was open for 3% of the time, Pallas kernels for 24%

profile of v7, /device:TPU:1, one launch (start us, length us, event | category | flops | bytes accessed | tf_op | source)
XLA Modules:
  0.0 63.4 jit_solution(658121759312410758)
XLA Ops:
  0.6 2.5 %collective-permute-start = (bf16[2,192,384]{2,1,0:T(8,128)(2,1)}, bf16[2,192,384]{2,1,0:T(8,128)(2,1)S(1)}, u32[]{:S(2)}, u32[]{:S(2)}) collective-permute-start(bf16[2,192,384]{2,1,0:T(8,128)(2,1)} %bitcast.10), channel_id=1, source_target_pairs={{0,8},{4,12},{8,16},{12,20},{16,24},{20,28},{24,32},{28,36},{32,40... | collective-permute-start | bytes 884744 | tf_op jit(solution)/shard_map/ppermute | solution.py:280
  3.2 1.2 %pad_maximum_fusion.joined_ref = bf16[5,192,384]{2,1,0:T(8,128)(2,1)S(1)} fusion(bf16[1,192,384]{2,1,0:T(8,128)(2,1)} %bitcast.12, bf16[2,192,384]{2,1,0:T(8,128)(2,1)} %bitcast.11, bf16[2,192,384]{2,1,0:T(8,128)(2,1)} %bitcast.9), kind=kLoop, calls=%fused_computation | loop fusion | flops 737280 | bytes 1474560 | tf_op jit(solution)/shard_map/concatenate | solution.py:297
  4.4 1.1 %flip.1 = (bf16[2,192,384]{2,1,0:T(8,128)(2,1)S(1)}, bf16[1,192,384]{2,1,0:T(8,128)(2,1)S(1)}, bf16[2,192,384]{2,1,0:T(8,128)(2,1)S(1)}, bf16[2,192,384]{2,1,0:T(8,128)(2,1)S(1)}) custom-call(bf16[5,192,384]{2,1,0:T(8,128)(2,1)S(1)} %pad_maximum_fusion.joined_ref), custom_call_target="tpu_custom_call" | custom-call | flops 2264924 | bytes 40000 | tf_op jit(solution)/shard_map/flip/pallas_call | solution.py:259
  5.5 6.2 %collective-permute-start.2 = (bf16[2,192,384]{2,1,0:T(8,128)(2,1)S(1)}, bf16[2,192,384]{2,1,0:T(8,128)(2,1)S(1)}, u32[]{:S(2)}, u32[]{:S(2)}) collective-permute-start(bf16[2,192,384]{2,1,0:T(8,128)(2,1)S(1)} %get-tuple-element.16.own_ref), channel_id=1, source_target_pairs={{0,248},{4,252},{8,0},{12,4},{16,8},{20,12},{24,16},{28,20},{32,24... | collective-permute-start | bytes 884744 | tf_op jit(solution)/shard_map/ppermute | solution.py:280
  11.7 5.7 %collective-permute-start.6 = (bf16[2,192,384]{2,1,0:T(8,128)(2,1)S(1)}, bf16[2,192,384]{2,1,0:T(8,128)(2,1)S(1)}, u32[]{:S(2)}, u32[]{:S(2)}) collective-permute-start(bf16[2,192,384]{2,1,0:T(8,128)(2,1)S(1)} %get-tuple-element.18), channel_id=1, source_target_pairs={{1,4},{2,5},{3,6},{5,0},{6,1},{7,2},{9,12},{10,13},{11,14},{13,8},... | collective-permute-start | bytes 884744 | tf_op jit(solution)/shard_map/ppermute | solution.py:289
  17.4 1.9 %collective-permute-start.4 = (bf16[2,192,384]{2,1,0:T(8,128)(2,1)S(1)}, bf16[2,192,384]{2,1,0:T(8,128)(2,1)S(1)}, u32[]{:S(2)}, u32[]{:S(2)}) collective-permute-start(bf16[2,192,384]{2,1,0:T(8,128)(2,1)S(1)} %get-tuple-element.18), channel_id=1, source_target_pairs={{1,0},{2,1},{3,2},{5,4},{6,5},{7,6},{9,8},{10,9},{11,10},{13,12},{... | collective-permute-start | bytes 884744 | tf_op jit(solution)/shard_map/ppermute | solution.py:289
  19.3 0.0 collective-permute-done.first_ref.behind_ref
  19.3 0.1 collective-permute-start.1
  19.4 4.8 %collective-permute-start.3 = (bf16[2,192,384]{2,1,0:T(8,128)(2,1)S(1)}, bf16[2,192,384]{2,1,0:T(8,128)(2,1)S(1)}, u32[]{:S(2)}, u32[]{:S(2)}) collective-permute-start(bf16[2,192,384]{2,1,0:T(8,128)(2,1)S(1)} %collective-permute-done.2.ahead_ref), channel_id=1, source_target_pairs={{0,248},{4,252},{8,0},{12,4},{16,8},{20,12},{24,16},{28,20},{32,24... | collective-permute-start | bytes 884744 | tf_op jit(solution)/shard_map/ppermute | solution.py:280
  24.2 1.6 %collective-permute-start.5 = (bf16[1,192,384]{2,1,0:T(8,128)(2,1)S(1)}, bf16[1,192,384]{2,1,0:T(8,128)(2,1)S(1)}, u32[]{:S(2)}, u32[]{:S(2)}) collective-permute-start(bf16[1,192,384]{2,1,0:T(8,128)(2,1)S(1)} %get-tuple-element.17.second_ref.own_ref), channel_id=1, source_target_pairs={{0,4},{1,5},{2,6},{3,7},{4,0},{5,1},{6,2},{7,3},{8,12},{9,13},{10,... | collective-permute-start | bytes 442376 | tf_op jit(solution)/shard_map/ppermute | solution.py:289
  25.9 0.9 %pad_add_fusion.facts_ref = s32[13]{0:T(128)S(1)} fusion(s32[4]{0:T(128)} %param.11, s32[9]{0:T(128)} %param.10), kind=kLoop, calls=%fused_computation.1 | loop fusion | flops 13 | bytes 104 | tf_op jit(solution)/shard_map/concatenate | solution.py:306
  26.8 3.4 %weights.2.w_ref = bf16[4,2,384,384]{3,2,1,0:T(8,128)(2,1)S(1)} custom-call(s32[13]{0:T(128)S(1)} %pad_add_fusion.facts_ref, bf16[9,4,192,384]{3,2,1,0:T(8,128)(2,1)} %p_ref.3, bf16[2,192,384]{2,1,0:T(8,128)(2,1)S(1)} %collective-permute-done.first_ref.behind_ref, bf16[1,192,384]{2,1,0:T(8,128)(2,1)S(1)} %get-tuple-element.17.second_ref.own_ref), custom_call_target="tpu_custom_call" | custom-call | flops 20000000 | bytes 100000 | tf_op jit(solution)/shard_map/weights/pallas_call | solution.py:108
  30.1 0.4 collective-permute-done.5.across_ref
  30.6 0.9 %upper_far.1 = (bf16[2,192,384]{2,1,0:T(8,128)(2,1)S(1)}, bf16[2,192,384]{2,1,0:T(8,128)(2,1)S(1)}) custom-call(s32[1]{0:T(128)} %bitcast.parity_ref, bf16[1,192,384]{2,1,0:T(8,128)(2,1)S(1)} %get-tuple-element.17.second_ref.own_ref, bf16[2,192,384]{2,1,0:T(8,128)(2,1)S(1)} %collective-permute-done.4.above_ref, ...), custom_call_target="tpu_custom_call" | custom-call | flops 6794772 | bytes 40000 | tf_op jit(solution)/shard_map/upper_far/pallas_call | solution.py:259
  31.5 0.4 collective-permute-start.9
  31.9 1.1 %collective-permute-start.10 = (bf16[2,192,384]{2,1,0:T(8,128)(2,1)S(1)}, bf16[2,192,384]{2,1,0:T(8,128)(2,1)S(1)}, u32[]{:S(2)}, u32[]{:S(2)}) collective-permute-start(bf16[2,192,384]{2,1,0:T(8,128)(2,1)S(1)} %get-tuple-element.20.second_ref), channel_id=1, source_target_pairs={{0,8},{4,12},{8,16},{12,20},{16,24},{20,28},{24,32},{28,36},{32,40... | collective-permute-start | bytes 884744 | tf_op jit(solution)/shard_map/ppermute | solution.py:280
  33.1 4.4 %weights.3.w_ref = bf16[7,2,384,384]{3,2,1,0:T(8,128)(2,1)S(1)} custom-call(s32[13]{0:T(128)S(1)} %pad_add_fusion.facts_ref, bf16[9,4,192,384]{3,2,1,0:T(8,128)(2,1)S(1)} %bitcast.7, bf16[2,192,384]{2,1,0:T(8,128)(2,1)S(1)} %get-tuple-element.19.first_ref, bf16[2,192,384]{2,1,0:T(8,128)(2,1)S(1)} %get-tuple-element.20.second_ref), custom_call_target="tpu_custom_call" | custom-call | flops 20000000 | bytes 100000 | tf_op jit(solution)/shard_map/weights/pallas_call | solution.py:108
  37.4 1.7 %lower_near.1.acc_ref = f32[2,384,768]{2,1,0:T(8,128)S(1)} custom-call(s32[1]{0:T(128)} %bitcast.parity_ref, bf16[2,192,384]{2,1,0:T(8,128)(2,1)S(1)} %collective-permute-done.first_ref.behind_ref, bf16[2,192,384]{2,1,0:T(8,128)(2,1)S(1)} %get-tuple-element.16.own_ref, bf16[2,192,384]{2,1,0:T(8,128)(2,1)S(1)} %collective-permute-done.2.ahead_ref, ...), custom_call_target="tpu_custom_call" | custom-call | flops 13589544 | bytes 40000 | tf_op jit(solution)/shard_map/lower_near/pallas_call | solution.py:259
  39.2 0.0 collective-permute-done.1.behind_ref
  39.2 1.0 %lower_far.1 = (f32[192,384]{1,0:T(8,128)S(1)}, f32[192,384]{1,0:T(8,128)S(1)}, bf16[4,192,384]{2,1,0:T(8,128)(2,1)S(1)}) custom-call(s32[1]{0:T(128)} %bitcast.parity_ref, bf16[2,192,384]{2,1,0:T(8,128)(2,1)S(1)} %collective-permute-done.1.behind_ref, bf16[2,192,384]{2,1,0:T(8,128)(2,1)S(1)} %collective-permute-done.3.ahead_ref, ...), custom_call_target="tpu_custom_call" | custom-call | flops 6794772 | bytes 40000 | tf_op jit(solution)/shard_map/lower_far/pallas_call | solution.py:259
  40.2 5.1 %collective-permute-start.7 = (bf16[4,192,384]{2,1,0:T(8,128)(2,1)S(1)}, bf16[4,192,384]{2,1,0:T(8,128)(2,1)S(1)}, u32[]{:S(2)}, u32[]{:S(2)}) collective-permute-start(bf16[4,192,384]{2,1,0:T(8,128)(2,1)S(1)} %get-tuple-element.22), channel_id=1, source_target_pairs={{0,1},{1,2},{2,3},{4,5},{5,6},{6,7},{8,9},{9,10},{10,11},{12,13},{... | collective-permute-start | bytes 1769480 | tf_op jit(solution)/shard_map/ppermute | solution.py:289
  45.3 1.7 %upper_near.1 = (f32[2,192,384]{2,1,0:T(8,128)S(1)}, f32[2,192,384]{2,1,0:T(8,128)S(1)}, f32[2,192,384]{2,1,0:T(8,128)S(1)}) custom-call(s32[1]{0:T(128)} %bitcast.parity_ref, bf16[1,192,384]{2,1,0:T(8,128)(2,1)S(1)} %get-tuple-element.17.second_ref.own_ref, bf16[2,192,384]{2,1,0:T(8,128)(2,1)S(1)} %collective-permute-done.4.above_ref, ...), custom_call_target="tpu_custom_call" | custom-call | flops 13589544 | bytes 40000 | tf_op jit(solution)/shard_map/upper_near/pallas_call | solution.py:259
  47.0 0.1 pass.1
  47.1 0.1 collective-permute-start.11
  47.2 4.8 %collective-permute-start.12 = (bf16[2,192,384]{2,1,0:T(8,128)(2,1)S(1)}, bf16[2,192,384]{2,1,0:T(8,128)(2,1)S(1)}, u32[]{:S(2)}, u32[]{:S(2)}) collective-permute-start(bf16[2,192,384]{2,1,0:T(8,128)(2,1)S(1)} %get-tuple-element.29), channel_id=1, source_target_pairs={{0,248},{4,252},{8,0},{12,4},{16,8},{20,12},{24,16},{28,20},{32,24... | collective-permute-start | bytes 884744 | tf_op jit(solution)/shard_map/ppermute | solution.py:280
  52.0 0.1 collective-permute-done.7.below_ref
  52.1 0.1 merge.1
  52.1 2.1 %collective-permute-start.8 = (bf16[2,192,384]{2,1,0:T(8,128)(2,1)S(1)}, bf16[2,192,384]{2,1,0:T(8,128)(2,1)S(1)}, u32[]{:S(2)}, u32[]{:S(2)}) collective-permute-start(bf16[2,192,384]{2,1,0:T(8,128)(2,1)S(1)} %merge.1), channel_id=1, source_target_pairs={{0,4},{1,5},{2,6},{3,7},{4,0},{5,1},{6,2},{7,3},{8,12},{9,13},{10,... | collective-permute-start | bytes 884744 | tf_op jit(solution)/shard_map/ppermute | solution.py:289
  54.3 4.0 %collective-permute-done.11.ahead_ref = bf16[2,192,384]{2,1,0:T(8,128)(2,1)S(1)} collective-permute-done((bf16[2,192,384]{2,1,0:T(8,128)(2,1)S(1)}, bf16[2,192,384]{2,1,0:T(8,128)(2,1)S(1)}, u32[]{:S(2)}, u32[]{:S(2)}) %collective-permute-start.11) | collective-permute-done | bytes 294944 | tf_op jit(solution)/shard_map/ppermute | solution.py:280
  58.2 0.8 %total.1 = bf16[2,192,384]{2,1,0:T(8,128)(2,1)} custom-call(f32[2,192,384]{2,1,0:T(8,128)S(1)} %get-tuple-element.25.here_ref, bf16[2,192,384]{2,1,0:T(8,128)(2,1)S(1)} %collective-permute-done.11.ahead_ref, bf16[2,192,384]{2,1,0:T(8,128)(2,1)S(1)} %collective-permute-done.12.behind_ref), custom_call_target="tpu_custom_call" | custom-call | flops 10000000000 | bytes 40000 | tf_op jit(solution)/shard_map/total/pallas_call | solution.py:259
  59.1 2.8 %collective-permute-done.8.across_ref = bf16[2,192,384]{2,1,0:T(8,128)(2,1)S(1)} collective-permute-done((bf16[2,192,384]{2,1,0:T(8,128)(2,1)S(1)}, bf16[2,192,384]{2,1,0:T(8,128)(2,1)S(1)}, u32[]{:S(2)}, u32[]{:S(2)}) %collective-permute-start.8) | collective-permute-done | bytes 294944 | tf_op jit(solution)/shard_map/ppermute | solution.py:289
  61.9 1.5 %finish.1 = bf16[2,192,384]{2,1,0:T(8,128)(2,1)} custom-call(f32[192,384]{1,0:T(8,128)S(1)} %get-tuple-element.21.own_ref.after_ref, bf16[4,192,384]{2,1,0:T(8,128)(2,1)S(1)} %collective-permute-done.7.below_ref, bf16[2,192,384]{2,1,0:T(8,128)(2,1)S(1)} %collective-permute-done.8.across_ref, bf16[2,192,384]{2,1,0:T(8,128)(2,1)S(1)} %get-tuple-element.24.factor_ref), custom_call_target="tpu_custom_call" | custom-call | flops 2264924 | bytes 40000 | tf_op jit(solution)/shard_map/finish/pallas_call | solution.py:259
  (12 shorter events, 0.0 us)
Async XLA Ops:
  0.6 18.7 %collective-permute-start = (bf16[2,192,384]{2,1,0:T(8,128)(2,1)}, bf16[2,192,384]{2,1,0:T(8,128)(2,1)S(1)}, u32[]{:S(2)}, u32[]{:S(2)}) collective-permute-start(bf16[2,192,384]{2,1,0:T(8,128)(2,1)} %bitcast.10), channel_id=1, source_target_pairs={{0,8},{4,12},{8,16},{12,20},{16,24},{20,28},{24,32},{28,36},{32,40... | collective-permute-start | bytes 884744 | tf_op jit(solution)/shard_map/ppermute | solution.py:280
  5.5 13.9 %collective-permute-start.2 = (bf16[2,192,384]{2,1,0:T(8,128)(2,1)S(1)}, bf16[2,192,384]{2,1,0:T(8,128)(2,1)S(1)}, u32[]{:S(2)}, u32[]{:S(2)}) collective-permute-start(bf16[2,192,384]{2,1,0:T(8,128)(2,1)S(1)} %get-tuple-element.16.own_ref), channel_id=1, source_target_pairs={{0,248},{4,252},{8,0},{12,4},{16,8},{20,12},{24,16},{28,20},{32,24... | collective-permute-start | bytes 884744 | tf_op jit(solution)/shard_map/ppermute | solution.py:280
  11.7 18.8 %collective-permute-start.6 = (bf16[2,192,384]{2,1,0:T(8,128)(2,1)S(1)}, bf16[2,192,384]{2,1,0:T(8,128)(2,1)S(1)}, u32[]{:S(2)}, u32[]{:S(2)}) collective-permute-start(bf16[2,192,384]{2,1,0:T(8,128)(2,1)S(1)} %get-tuple-element.18), channel_id=1, source_target_pairs={{1,4},{2,5},{3,6},{5,0},{6,1},{7,2},{9,12},{10,13},{11,14},{13,8},... | collective-permute-start | bytes 884744 | tf_op jit(solution)/shard_map/ppermute | solution.py:289
  17.4 13.2 %collective-permute-start.4 = (bf16[2,192,384]{2,1,0:T(8,128)(2,1)S(1)}, bf16[2,192,384]{2,1,0:T(8,128)(2,1)S(1)}, u32[]{:S(2)}, u32[]{:S(2)}) collective-permute-start(bf16[2,192,384]{2,1,0:T(8,128)(2,1)S(1)} %get-tuple-element.18), channel_id=1, source_target_pairs={{1,0},{2,1},{3,2},{5,4},{6,5},{7,6},{9,8},{10,9},{11,10},{13,12},{... | collective-permute-start | bytes 884744 | tf_op jit(solution)/shard_map/ppermute | solution.py:289
  19.3 19.8 %collective-permute-start.1 = (bf16[2,192,384]{2,1,0:T(8,128)(2,1)S(1)}, bf16[2,192,384]{2,1,0:T(8,128)(2,1)S(1)}, u32[]{:S(2)}, u32[]{:S(2)}) collective-permute-start(bf16[2,192,384]{2,1,0:T(8,128)(2,1)S(1)} %collective-permute-done.first_ref.behind_ref), channel_id=1, source_target_pairs={{0,8},{4,12},{8,16},{12,20},{16,24},{20,28},{24,32},{28,36},{32,40... | collective-permute-start | bytes 884744 | tf_op jit(solution)/shard_map/ppermute | solution.py:280
  19.4 19.7 %collective-permute-start.3 = (bf16[2,192,384]{2,1,0:T(8,128)(2,1)S(1)}, bf16[2,192,384]{2,1,0:T(8,128)(2,1)S(1)}, u32[]{:S(2)}, u32[]{:S(2)}) collective-permute-start(bf16[2,192,384]{2,1,0:T(8,128)(2,1)S(1)} %collective-permute-done.2.ahead_ref), channel_id=1, source_target_pairs={{0,248},{4,252},{8,0},{12,4},{16,8},{20,12},{24,16},{28,20},{32,24... | collective-permute-start | bytes 884744 | tf_op jit(solution)/shard_map/ppermute | solution.py:280
  24.2 6.4 %collective-permute-start.5 = (bf16[1,192,384]{2,1,0:T(8,128)(2,1)S(1)}, bf16[1,192,384]{2,1,0:T(8,128)(2,1)S(1)}, u32[]{:S(2)}, u32[]{:S(2)}) collective-permute-start(bf16[1,192,384]{2,1,0:T(8,128)(2,1)S(1)} %get-tuple-element.17.second_ref.own_ref), channel_id=1, source_target_pairs={{0,4},{1,5},{2,6},{3,7},{4,0},{5,1},{6,2},{7,3},{8,12},{9,13},{10,... | collective-permute-start | bytes 442376 | tf_op jit(solution)/shard_map/ppermute | solution.py:289
  25.9 7.2 %slice-start = ((s8[5308416]{0:T(1024)(128)(4,1)}), s8[4194304]{0:T(1024)(128)(4,1)S(1)}, s32[]{:S(2)}) async-start(s8[5308416]{0:T(1024)(128)(4,1)} %bitcast.6), calls=%async_computation | async-start | bytes 8388608
  26.8 6.3 %slice-start.1 = ((s8[5308416]{0:T(1024)(128)(4,1)}), s8[1114112]{0:T(1024)(128)(4,1)S(1)}, s32[]{:S(2)}) async-start(s8[5308416]{0:T(1024)(128)(4,1)} %bitcast.6), calls=%async_computation.1 | async-start | bytes 2228224
  31.5 15.5 %collective-permute-start.9 = (bf16[2,192,384]{2,1,0:T(8,128)(2,1)S(1)}, bf16[2,192,384]{2,1,0:T(8,128)(2,1)S(1)}, u32[]{:S(2)}, u32[]{:S(2)}) collective-permute-start(bf16[2,192,384]{2,1,0:T(8,128)(2,1)S(1)} %get-tuple-element.19.first_ref), channel_id=1, source_target_pairs={{0,248},{4,252},{8,0},{12,4},{16,8},{20,12},{24,16},{28,20},{32,24... | collective-permute-start | bytes 884744 | tf_op jit(solution)/shard_map/ppermute | solution.py:280
  31.9 15.1 %collective-permute-start.10 = (bf16[2,192,384]{2,1,0:T(8,128)(2,1)S(1)}, bf16[2,192,384]{2,1,0:T(8,128)(2,1)S(1)}, u32[]{:S(2)}, u32[]{:S(2)}) collective-permute-start(bf16[2,192,384]{2,1,0:T(8,128)(2,1)S(1)} %get-tuple-element.20.second_ref), channel_id=1, source_target_pairs={{0,8},{4,12},{8,16},{12,20},{16,24},{20,28},{24,32},{28,36},{32,40... | collective-permute-start | bytes 884744 | tf_op jit(solution)/shard_map/ppermute | solution.py:280
  40.2 11.9 %collective-permute-start.7 = (bf16[4,192,384]{2,1,0:T(8,128)(2,1)S(1)}, bf16[4,192,384]{2,1,0:T(8,128)(2,1)S(1)}, u32[]{:S(2)}, u32[]{:S(2)}) collective-permute-start(bf16[4,192,384]{2,1,0:T(8,128)(2,1)S(1)} %get-tuple-element.22), channel_id=1, source_target_pairs={{0,1},{1,2},{2,3},{4,5},{5,6},{6,7},{8,9},{9,10},{10,11},{12,13},{... | collective-permute-start | bytes 1769480 | tf_op jit(solution)/shard_map/ppermute | solution.py:289
  47.1 11.1 %collective-permute-start.11 = (bf16[2,192,384]{2,1,0:T(8,128)(2,1)S(1)}, bf16[2,192,384]{2,1,0:T(8,128)(2,1)S(1)}, u32[]{:S(2)}, u32[]{:S(2)}) collective-permute-start(bf16[2,192,384]{2,1,0:T(8,128)(2,1)S(1)} %get-tuple-element.28), channel_id=1, source_target_pairs={{0,8},{4,12},{8,16},{12,20},{16,24},{20,28},{24,32},{28,36},{32,40... | collective-permute-start | bytes 884744 | tf_op jit(solution)/shard_map/ppermute | solution.py:280
  47.2 11.0 %collective-permute-start.12 = (bf16[2,192,384]{2,1,0:T(8,128)(2,1)S(1)}, bf16[2,192,384]{2,1,0:T(8,128)(2,1)S(1)}, u32[]{:S(2)}, u32[]{:S(2)}) collective-permute-start(bf16[2,192,384]{2,1,0:T(8,128)(2,1)S(1)} %get-tuple-element.29), channel_id=1, source_target_pairs={{0,248},{4,252},{8,0},{12,4},{16,8},{20,12},{24,16},{28,20},{32,24... | collective-permute-start | bytes 884744 | tf_op jit(solution)/shard_map/ppermute | solution.py:280
  52.1 9.8 %collective-permute-start.8 = (bf16[2,192,384]{2,1,0:T(8,128)(2,1)S(1)}, bf16[2,192,384]{2,1,0:T(8,128)(2,1)S(1)}, u32[]{:S(2)}, u32[]{:S(2)}) collective-permute-start(bf16[2,192,384]{2,1,0:T(8,128)(2,1)S(1)} %merge.1), channel_id=1, source_target_pairs={{0,4},{1,5},{2,6},{3,7},{4,0},{5,1},{6,2},{7,3},{8,12},{9,13},{10,... | collective-permute-start | bytes 884744 | tf_op jit(solution)/shard_map/ppermute | solution.py:289
